TPU v7x, 32 devices: a whole 2x2x4 slice. The times are simulated.
32 devices in a mesh: wide: 8 (over y, x, core), narrow: 4 (over z).
Axes of the slice: x: 2, y: 2, z: 4, core: 2. Of those that a mesh axis runs over, the one named last changes fastest.
Arguments:
- tokens: bfloat16 [32, 128, 2048], P(('wide', 'narrow')), may hold values from -6 to 6
- conv_state: float32 [32, 3, 2816], P(('wide', 'narrow')), may hold values from -6 to 6
- recur_state: float32 [32, 2816], P(('wide', 'narrow')), may hold values from -6 to 6
- fresh_rows: int32 [32], P(('wide', 'narrow')), may hold values 0 or 1
- gain_mixer: bfloat16 [2048], P(('wide', 'narrow')), may hold values from 0.5 to 1.5
- proj_input: bfloat16 [2048, 2816], P(('wide', 'narrow')), may hold values from -0.125 to 0.125
- proj_gate: bfloat16 [2048, 2816], P(('wide', 'narrow')), may hold values from -0.125 to 0.125
- conv_kernel: bfloat16 [4, 2816], P(None, ('wide', 'narrow')), may hold values from -3 to 3
- decay_param: bfloat16 [2816], P(('wide', 'narrow')), may hold values from 1 to 9
- gate_recur: bfloat16 [2816, 176], P(('wide', 'narrow')), may hold values from -0.4375 to 0.4375
- gate_input: bfloat16 [2816, 176], P(('wide', 'narrow')), may hold values from -0.4375 to 0.4375
- proj_output: bfloat16 [2816, 2048], P(('wide', 'narrow')), may hold values from -0.4375 to 0.4375
- gain_mlp: bfloat16 [2048], P(('wide', 'narrow')), may hold values from 0.5 to 1.5
- mlp_gate: bfloat16 [2048, 6144], P(('wide', 'narrow')), may hold values from -0.125 to 0.125
- mlp_up: bfloat16 [2048, 6144], P(('wide', 'narrow')), may hold values from -0.125 to 0.125
- mlp_down: bfloat16 [6144, 2048], P(('wide', 'narrow')), may hold values from -0.15625 to 0.15625
- cotangent: bfloat16 [32, 128, 2048], P(('wide', 'narrow')), may hold values from -6 to 6
Outputs:
- output: bfloat16 [32, 128, 2048], P(('wide', 'narrow'))
- grad_tokens: bfloat16 [32, 128, 2048], P(('wide', 'narrow'))
- grad_conv_state: float32 [32, 3, 2816], P(('wide', 'narrow'))
- grad_recur_state: float32 [32, 2816], P(('wide', 'narrow'))
- grad_gain_mixer: float32 [2048], P(('wide', 'narrow'))
- grad_proj_input: float32 [2048, 2816], P(('wide', 'narrow'))
- grad_proj_gate: float32 [2048, 2816], P(('wide', 'narrow'))
- grad_conv_kernel: float32 [4, 2816], P(None, ('wide', 'narrow'))
- grad_decay_param: float32 [2816], P(('wide', 'narrow'))
- grad_gate_recur: float32 [2816, 176], P(('wide', 'narrow'))
- grad_gate_input: float32 [2816, 176], P(('wide', 'narrow'))
- grad_proj_output: float32 [2816, 2048], P(('wide', 'narrow'))
- grad_gain_mlp: float32 [2048], P(('wide', 'narrow'))
- grad_mlp_gate: float32 [2048, 6144], P(('wide', 'narrow'))
- grad_mlp_up: float32 [2048, 6144], P(('wide', 'narrow'))
- grad_mlp_down: float32 [6144, 2048], P(('wide', 'narrow'))
Inputs may be any that keep to these rules, and one draw needn't show every extreme that they name: `fresh_rows`: 1 marks a row whose given states are replaced by zeros.
All inputs are finite; a program needn't handle non-finite values. No bound on the sum of `fresh_rows` on one device may be relied on, other than what follows from the above.
Results may differ from a plain program's by a relative error of at most 0.012.
Values may be sent and summed in bfloat16 or wider, within the bound.
A program may use at most 448 MiB of HBM per device.

v0:
```python
from functools import reduce

import jax
import jax.numpy as jnp
from jax import lax
from jax.sharding import PartitionSpec as P

BLOCKS = 16
BLK = 176
SCAN_BLOCK = 16


epsilon = 1e-06
contract_rows = (((0,), (0,)), ((), ()))
contract_cols = (((1,), (1,)), ((), ()))


def plain_product(left_side, right_side):
    return jnp.dot(left_side, right_side, preferred_element_type=jnp.float32)


def rows_product(left_side, right_side):
    return lax.dot_general(left_side, right_side, contract_rows, preferred_element_type=jnp.float32)


def cols_product(left_side, right_side):
    return lax.dot_general(left_side, right_side, contract_cols, preferred_element_type=jnp.float32)


def norm_scale(values, gain_vec):
    return (
        values * lax.rsqrt(jnp.mean(values * values, axis=-1, keepdims=True) + epsilon) * gain_vec
    )


def conv_apply(values, history, kernel):
    joined = jnp.concatenate([history, values], axis=0)
    length = values.shape[0]
    kernel_taps = kernel.shape[0]
    result = jnp.zeros_like(values)
    for offset in range(kernel_taps):
        first_row = kernel_taps - 1 - offset
        result = result + kernel[offset] * joined[first_row : first_row + length]
    return result


def block_mix(values, matrix):
    length = values.shape[0]
    mixed_out = jnp.einsum(
        "tki,kij->tkj",
        values.reshape(length, BLOCKS, BLK),
        matrix.reshape(BLOCKS, BLK, BLK),
        preferred_element_type=jnp.float32,
    )
    return mixed_out.reshape(length, BLOCKS * BLK)


def block_back(grad_logits, matrix):
    length = grad_logits.shape[0]
    spread_back = jnp.einsum(
        "tkj,kij->tki",
        grad_logits.reshape(length, BLOCKS, BLK),
        matrix.reshape(BLOCKS, BLK, BLK),
        preferred_element_type=jnp.float32,
    )
    return spread_back.reshape(length, BLOCKS * BLK)


def block_grad(values, grad_logits):
    length = values.shape[0]
    summed = jnp.einsum(
        "tki,tkj->kij",
        values.reshape(length, BLOCKS, BLK),
        grad_logits.reshape(length, BLOCKS, BLK),
        preferred_element_type=jnp.float32,
    )
    return summed.reshape(BLOCKS * BLK, BLK)


def gate_apply(recur_logits, input_logits, conv_float, decay_float):
    log_decay = -8.0 * jax.nn.sigmoid(recur_logits) * jax.nn.softplus(-decay_float)
    scan_in = jnp.sqrt(-jnp.expm1(2.0 * log_decay)) * jax.nn.sigmoid(input_logits) * conv_float
    return (log_decay, scan_in)


def branch_apply(hidden, gate_logits):
    return hidden * jax.nn.gelu(gate_logits)


def mlp_apply(gate_part, up_part):
    return jax.nn.gelu(gate_part) * up_part


def block_scan(log_decay, scan_in, initial):
    length, channels = scan_in.shape
    block_count = length // SCAN_BLOCK
    positions = jnp.arange(SCAN_BLOCK)
    causal = (positions[:, None] >= positions[None, :])[:, :, None]

    def advance(carried, pieces):
        decay_piece, input_piece = pieces
        cumulative = jnp.cumsum(decay_piece, axis=0)
        spread = jnp.where(causal, cumulative[:, None, :] - cumulative[None, :, :], 0.0)
        factors = jnp.where(causal, jnp.exp(spread), 0.0)
        states = jnp.sum(factors * input_piece[None, :, :], axis=1) + jnp.exp(cumulative) * carried
        return (states[-1], states)

    last_state, states = lax.scan(
        advance,
        initial,
        (
            log_decay.reshape(block_count, SCAN_BLOCK, channels),
            scan_in.reshape(block_count, SCAN_BLOCK, channels),
        ),
    )
    return states.reshape(length, channels)


def scan_back(log_decay, hidden, initial, grad_hidden):
    following = jnp.concatenate([log_decay[1:], jnp.zeros_like(log_decay[:1])], axis=0)
    carried = block_scan(following[::-1], grad_hidden[::-1], jnp.zeros_like(initial))[::-1]
    previous = jnp.concatenate([initial[None], hidden[:-1]], axis=0)
    grad_log_decay = carried * jnp.exp(log_decay) * previous
    grad_initial = jnp.exp(log_decay[0]) * carried[0]
    return (grad_log_decay, carried, grad_initial)


def mixer_forward(tokens_row, history, initial, keep_row, mixer):
    (
        gain_vec,
        proj_input,
        proj_gate,
        conv_kernel,
        decay_param,
        gate_recur,
        gate_input,
        proj_output,
    ) = mixer
    values = tokens_row.astype(jnp.float32)
    normed_one = norm_scale(values, gain_vec.astype(jnp.float32)).astype(jnp.bfloat16)
    branch_in = plain_product(normed_one, proj_input)
    gate_logits = plain_product(normed_one, proj_gate)
    history_kept = history * keep_row
    kernel_float = conv_kernel.astype(jnp.float32)
    conv_out = conv_apply(branch_in, history_kept, kernel_float).astype(jnp.bfloat16)
    recur_logits = block_mix(conv_out, gate_recur)
    input_logits = block_mix(conv_out, gate_input)
    decay_float = decay_param.astype(jnp.float32)
    conv_float = conv_out.astype(jnp.float32)
    log_decay, scan_in = gate_apply(recur_logits, input_logits, conv_float, decay_float)
    initial_kept = initial * keep_row
    hidden = block_scan(log_decay, scan_in, initial_kept)
    mixed_out = branch_apply(hidden, gate_logits).astype(jnp.bfloat16)
    after_mixer = values + plain_product(mixed_out, proj_output)
    kept = (
        values,
        normed_one,
        branch_in,
        gate_logits,
        history_kept,
        kernel_float,
        conv_out,
        conv_float,
        recur_logits,
        input_logits,
        decay_float,
        log_decay,
        initial_kept,
        hidden,
        mixed_out,
    )
    return (after_mixer, kept)


def mlp_forward(after_mixer, mlp):
    gain_vec, mlp_gate, mlp_up, mlp_down = mlp
    normed_two = norm_scale(after_mixer, gain_vec.astype(jnp.float32)).astype(jnp.bfloat16)
    gate_part = plain_product(normed_two, mlp_gate)
    up_part = plain_product(normed_two, mlp_up)
    activated = mlp_apply(gate_part, up_part).astype(jnp.bfloat16)
    result = after_mixer + plain_product(activated, mlp_down)
    return (result, (after_mixer, normed_two, gate_part, up_part, activated))


def mlp_backward(grad_result, mlp, kept):
    gain_vec, mlp_gate, mlp_up, mlp_down = mlp
    after_mixer, normed_two, gate_part, up_part, activated = kept
    grad_activated = cols_product(grad_result, mlp_down)
    grad_down = rows_product(activated, grad_result)
    unused, mlp_pull = jax.vjp(mlp_apply, gate_part, up_part)
    grad_gate_part, grad_up_part = mlp_pull(grad_activated)
    grad_gate_part = grad_gate_part.astype(jnp.bfloat16)
    grad_up_part = grad_up_part.astype(jnp.bfloat16)
    grad_normed = cols_product(grad_gate_part, mlp_gate) + cols_product(grad_up_part, mlp_up)
    grad_mlp_gate = rows_product(normed_two, grad_gate_part)
    grad_mlp_up = rows_product(normed_two, grad_up_part)
    unused, norm_pull = jax.vjp(norm_scale, after_mixer, gain_vec.astype(jnp.float32))
    grad_values, grad_gain = norm_pull(grad_normed)
    grad_after = grad_result.astype(jnp.float32) + grad_values
    return (grad_after, (grad_gain, grad_mlp_gate, grad_mlp_up, grad_down))


def mixer_backward(grad_after, mixer, kept, keep_row):
    (
        gain_vec,
        proj_input,
        proj_gate,
        conv_kernel,
        decay_param,
        gate_recur,
        gate_input,
        proj_output,
    ) = mixer
    (
        values,
        normed_one,
        branch_in,
        gate_logits,
        history_kept,
        kernel_float,
        conv_out,
        conv_float,
        recur_logits,
        input_logits,
        decay_float,
        log_decay,
        initial_kept,
        hidden,
        mixed_out,
    ) = kept
    grad_mixed = grad_after.astype(jnp.bfloat16)
    grad_proj_output = rows_product(mixed_out, grad_mixed)
    grad_branch = cols_product(grad_mixed, proj_output)
    unused, branch_pull = jax.vjp(branch_apply, hidden, gate_logits)
    grad_hidden, grad_gate_logits = branch_pull(grad_branch)
    grad_gate_logits = grad_gate_logits.astype(jnp.bfloat16)
    grad_log_decay, grad_scan_in, grad_initial = scan_back(
        log_decay, hidden, initial_kept, grad_hidden
    )
    unused, gate_pull = jax.vjp(gate_apply, recur_logits, input_logits, conv_float, decay_float)
    grad_recur_logits, grad_input_logits, grad_conv, grad_decay = gate_pull(
        (grad_log_decay, grad_scan_in)
    )
    grad_recur_logits = grad_recur_logits.astype(jnp.bfloat16)
    grad_input_logits = grad_input_logits.astype(jnp.bfloat16)
    grad_gate_recur = block_grad(conv_out, grad_recur_logits)
    grad_gate_input = block_grad(conv_out, grad_input_logits)
    grad_conv = (
        grad_conv
        + block_back(grad_recur_logits, gate_recur)
        + block_back(grad_input_logits, gate_input)
    )
    unused, conv_pull = jax.vjp(conv_apply, branch_in, history_kept, kernel_float)
    grad_branch_in, grad_history, grad_kernel = conv_pull(grad_conv)
    grad_branch_low = grad_branch_in.astype(jnp.bfloat16)
    grad_proj_input = rows_product(normed_one, grad_branch_low)
    grad_proj_gate = rows_product(normed_one, grad_gate_logits)
    grad_normed = cols_product(grad_branch_low, proj_input) + cols_product(
        grad_gate_logits, proj_gate
    )
    unused, norm_pull = jax.vjp(norm_scale, values, gain_vec.astype(jnp.float32))
    grad_values, grad_gain = norm_pull(grad_normed)
    grad_tokens = (grad_after + grad_values).astype(jnp.bfloat16)
    weight_terms = (
        grad_gain,
        grad_proj_input,
        grad_proj_gate,
        grad_kernel,
        grad_decay,
        grad_gate_recur,
        grad_gate_input,
        grad_proj_output,
    )
    return (grad_tokens, grad_history * keep_row, grad_initial * keep_row, weight_terms)


def add_terms(first_terms, second_terms):
    return tuple(
        (left_side + right_side for left_side, right_side in zip(first_terms, second_terms))
    )


def shards(
    tokens,
    conv_state,
    recur_state,
    fresh_rows,
    gain_mixer,
    proj_input,
    proj_gate,
    conv_kernel,
    decay_param,
    gate_recur,
    gate_input,
    proj_output,
    gain_mlp,
    mlp_gate,
    mlp_up,
    mlp_down,
    cotangent,
):
    mixer_full = (
        lax.all_gather(gain_mixer, ("wide", "narrow"), axis=0, tiled=True),
        lax.all_gather(proj_input, ("wide", "narrow"), axis=0, tiled=True),
        lax.all_gather(proj_gate, ("wide", "narrow"), axis=0, tiled=True),
        lax.all_gather(conv_kernel, ("wide", "narrow"), axis=1, tiled=True),
        lax.all_gather(decay_param, ("wide", "narrow"), axis=0, tiled=True),
        lax.all_gather(gate_recur, ("wide", "narrow"), axis=0, tiled=True),
        lax.all_gather(gate_input, ("wide", "narrow"), axis=0, tiled=True),
        lax.all_gather(proj_output, ("wide", "narrow"), axis=0, tiled=True),
    )
    mlp_full = (
        lax.all_gather(gain_mlp, ("wide", "narrow"), axis=0, tiled=True),
        lax.all_gather(mlp_gate, ("wide", "narrow"), axis=0, tiled=True),
        lax.all_gather(mlp_up, ("wide", "narrow"), axis=0, tiled=True),
        lax.all_gather(mlp_down, ("wide", "narrow"), axis=0, tiled=True),
    )
    keep_rows = (1 - fresh_rows).astype(jnp.float32)
    stored = []
    row_index = 0
    after_mixer, mixer_kept = mixer_forward(
        tokens[row_index],
        conv_state[row_index],
        recur_state[row_index],
        keep_rows[row_index],
        mixer_full,
    )
    result, mlp_kept = mlp_forward(after_mixer, mlp_full)
    outputs = [result.astype(jnp.bfloat16)]
    stored.append((mixer_kept, mlp_kept))
    mixer_back = (
        lax.all_gather(gain_mixer, ("wide", "narrow"), axis=0, tiled=True),
        lax.all_gather(proj_input, ("wide", "narrow"), axis=0, tiled=True),
        lax.all_gather(proj_gate, ("wide", "narrow"), axis=0, tiled=True),
        lax.all_gather(conv_kernel, ("wide", "narrow"), axis=1, tiled=True),
        lax.all_gather(decay_param, ("wide", "narrow"), axis=0, tiled=True),
        lax.all_gather(gate_recur, ("wide", "narrow"), axis=0, tiled=True),
        lax.all_gather(gate_input, ("wide", "narrow"), axis=0, tiled=True),
        lax.all_gather(proj_output, ("wide", "narrow"), axis=0, tiled=True),
    )
    mlp_back = (
        lax.all_gather(gain_mlp, ("wide", "narrow"), axis=0, tiled=True),
        lax.all_gather(mlp_gate, ("wide", "narrow"), axis=0, tiled=True),
        lax.all_gather(mlp_up, ("wide", "narrow"), axis=0, tiled=True),
        lax.all_gather(mlp_down, ("wide", "narrow"), axis=0, tiled=True),
    )
    stored = []
    row_index = 0
    after_mixer, mixer_kept = mixer_forward(
        tokens[row_index],
        conv_state[row_index],
        recur_state[row_index],
        keep_rows[row_index],
        mixer_back,
    )
    unused, mlp_kept = mlp_forward(after_mixer, mlp_back)
    stored.append((mixer_kept, mlp_kept))
    row_index = 0
    grad_after, row_terms = mlp_backward(cotangent[row_index], mlp_back, stored[row_index][1])
    after_grads = [grad_after]
    mlp_terms = [row_terms]
    mlp_total = reduce(add_terms, mlp_terms)
    mlp_sums = (
        lax.psum_scatter(mlp_total[0], ("wide", "narrow"), scatter_dimension=0, tiled=True),
        lax.psum_scatter(mlp_total[1], ("wide", "narrow"), scatter_dimension=0, tiled=True),
        lax.psum_scatter(mlp_total[2], ("wide", "narrow"), scatter_dimension=0, tiled=True),
        lax.psum_scatter(mlp_total[3], ("wide", "narrow"), scatter_dimension=0, tiled=True),
    )
    row_index = 0
    grad_tokens, grad_history, grad_initial, row_terms = mixer_backward(
        after_grads[row_index], mixer_back, stored[row_index][0], keep_rows[row_index]
    )
    token_grads = [grad_tokens]
    history_grads = [grad_history]
    initial_grads = [grad_initial]
    mixer_terms = [row_terms]
    mixer_total = reduce(add_terms, mixer_terms)
    mixer_sums = (
        lax.psum_scatter(mixer_total[0], ("wide", "narrow"), scatter_dimension=0, tiled=True),
        lax.psum_scatter(mixer_total[1], ("wide", "narrow"), scatter_dimension=0, tiled=True),
        lax.psum_scatter(mixer_total[2], ("wide", "narrow"), scatter_dimension=0, tiled=True),
        lax.psum_scatter(mixer_total[3], ("wide", "narrow"), scatter_dimension=1, tiled=True),
        lax.psum_scatter(mixer_total[4], ("wide", "narrow"), scatter_dimension=0, tiled=True),
        lax.psum_scatter(mixer_total[5], ("wide", "narrow"), scatter_dimension=0, tiled=True),
        lax.psum_scatter(mixer_total[6], ("wide", "narrow"), scatter_dimension=0, tiled=True),
        lax.psum_scatter(mixer_total[7], ("wide", "narrow"), scatter_dimension=0, tiled=True),
    )
    return (
        jnp.stack(outputs),
        jnp.stack(token_grads),
        jnp.stack(history_grads),
        jnp.stack(initial_grads),
        mixer_sums[0],
        mixer_sums[1],
        mixer_sums[2],
        mixer_sums[3],
        mixer_sums[4],
        mixer_sums[5],
        mixer_sums[6],
        mixer_sums[7],
        mlp_sums[0],
        mlp_sums[1],
        mlp_sums[2],
        mlp_sums[3],
    )


def solution(mesh):
    return jax.shard_map(
        shards,
        mesh=mesh,
        in_specs=(
            P(("wide", "narrow"), None, None),
            P(("wide", "narrow"), None, None),
            P(("wide", "narrow"), None),
            P(("wide", "narrow")),
            P(("wide", "narrow")),
            P(("wide", "narrow"), None),
            P(("wide", "narrow"), None),
            P(None, ("wide", "narrow")),
            P(("wide", "narrow")),
            P(("wide", "narrow"), None),
            P(("wide", "narrow"), None),
            P(("wide", "narrow"), None),
            P(("wide", "narrow")),
            P(("wide", "narrow"), None),
            P(("wide", "narrow"), None),
            P(("wide", "narrow"), None),
            P(("wide", "narrow"), None, None),
        ),
        out_specs=(
            P(("wide", "narrow"), None, None),
            P(("wide", "narrow"), None, None),
            P(("wide", "narrow"), None, None),
            P(("wide", "narrow"), None),
            P(("wide", "narrow")),
            P(("wide", "narrow"), None),
            P(("wide", "narrow"), None),
            P(None, ("wide", "narrow")),
            P(("wide", "narrow")),
            P(("wide", "narrow"), None),
            P(("wide", "narrow"), None),
            P(("wide", "narrow"), None),
            P(("wide", "narrow")),
            P(("wide", "narrow"), None),
            P(("wide", "narrow"), None),
            P(("wide", "narrow"), None),
        ),
        check_vma=False,
    )
```

profile of v0, /device:TPU:0, one launch (start us, length us, event | category | flops | bytes accessed | tf_op | source)
XLA Modules:
  0.0 4166.6 jit_solution(15338633227689331018)
XLA Ops:
  12.7 43.1 %all-reduce.17 = (bf16[2048]{0:T(1024)(128)(2,1)S(1)}, bf16[2816]{0:T(1024)(128)(2,1)S(1)}, bf16[2048]{0:T(1024)(128)(2,1)S(1)}) all-reduce(bf16[2048]{0:T(1024)(128)(2,1)S(1)} %dynamic-update-slice, bf16[2816]{0:T(1024)(128)(2,1)S(1)} %dynamic-update-slice.1, ...), channel_id=1, replica_groups=mesh['wide'=8,'narrow'=4] {'wide','narrow'}, use_global_device_ids=true, to_apply=%add.9 | all-reduce | flops 6912 | bytes 27648
  55.8 66.4 %all-gather = bf16[32,88,4]{1,2,0:T(4,128)(2,1)S(1)} all-gather(bf16[1,88,4]{1,2,0:T(4,128)(2,1)S(1)} %bitcast.176), channel_id=1, replica_groups=mesh['wide'=8,'narrow'=4] {'wide','narrow'}, dimensions={0}, use_global_device_ids=true | all-gather | bytes 23232 | tf_op jit(solution)/shard_map/all_gather | solution.py:306
  123.9 98.1 %all_gather.51 = bf16[2816,176]{1,0:T(8,128)(2,1)S(1)} all-gather(bf16[88,176]{1,0:T(8,128)(2,1)S(1)} %copy-done.43), channel_id=1, replica_groups=mesh['wide'=8,'narrow'=4] {'wide','narrow'}, dimensions={0}, use_global_device_ids=true | all-gather | bytes 1022208 | tf_op jit(solution)/shard_map/all_gather | solution.py:308
  222.1 100.2 %all_gather.53 = bf16[2816,176]{1,0:T(8,128)(2,1)} all-gather(bf16[88,176]{1,0:T(8,128)(2,1)S(1)} %copy-done.44), channel_id=1, replica_groups=mesh['wide'=8,'narrow'=4] {'wide','narrow'}, dimensions={0}, use_global_device_ids=true | all-gather | bytes 1022208 | tf_op jit(solution)/shard_map/all_gather | solution.py:309
  322.3 6.0 fusion.77
  337.1 3.4 fusion.23
  340.5 3.0 copy.128
  345.1 3.9 convert_multiply_fusion.5
  350.4 11.9 rev.9
  366.2 25.6 while.33
  391.8 8.1 multiply_convert_fusion.2
  399.8 6.3 multiply_reduce_fusion.9
  407.3 73.5 %all-gather.14.cloned.1.call-done = bf16[2048,6144]{1,0:T(8,128)(2,1)} async-done(((bf16[64,6144]{1,0:T(8,128)(2,1)}), bf16[2048,6144]{1,0:T(8,128)(2,1)}) %all-gather.14.cloned.1.call-update) | async-done | bytes 25165840 | tf_op jit(solution)/shard_map/all_gather | solution.py:314
  480.8 13.2 fusion.81
  494.1 142.4 %all-gather.16.cloned.1.call-done = bf16[2048,6144]{1,0:T(8,128)(2,1)} async-done(((bf16[64,6144]{1,0:T(8,128)(2,1)}), bf16[2048,6144]{1,0:T(8,128)(2,1)}) %all-gather.16.cloned.1.call-update) | async-done | bytes 25165840 | tf_op jit(solution)/shard_map/all_gather | solution.py:315
  636.4 13.2 fusion.82
  649.6 142.4 %all-gather.18.cloned.1.call-done = bf16[6144,2048]{1,0:T(8,128)(2,1)} async-done(((bf16[192,2048]{1,0:T(8,128)(2,1)}), bf16[6144,2048]{1,0:T(8,128)(2,1)}) %all-gather.18.cloned.1.call-update) | async-done | bytes 25165840 | tf_op jit(solution)/shard_map/all_gather | solution.py:316
  792.0 17.8 multiply_convert_fusion
  809.8 14.3 fusion.83
  824.1 15.3 multiply_reduce_fusion.7
  842.4 10.2 fusion.35
  852.6 12.0 rev.10
  865.8 25.3 while.34
  891.2 12.2 rev.11
  903.4 6.0 multiply_reduce_fusion.2
  910.9 3.2 fusion.89
  914.1 3.0 copy.139
  922.2 3.3 fusion.88
  928.4 6.5 multiply_reduce_fusion.6
  938.2 8.8 fusion.57
  947.1 5.5 fusion.45
  952.6 3.3 fusion.84
  957.1 3.2 fusion.85
  961.4 9.5 fusion.58
  972.0 9.5 fusion.72
  982.8 10.7 fusion.59
  993.5 20.9 fusion.86
  1014.5 20.8 fusion.87
  1036.7 20.5 fusion.53
  1063.1 10.9 fusion.20
  1079.1 138.1 %reduce-scatter.14.cloned.1.call-done = f32[88,176]{1,0:T(8,128)} async-done(((f32[2816,176]{1,0:T(8,128)}), f32[88,176]{1,0:T(8,128)}) %reduce-scatter.14.cloned.1.call-update) | async-done | bytes 61968 | tf_op jit(solution)/shard_map/reduce_scatter | solution.py:384
  1217.3 142.5 %reduce-scatter.16.cloned.1.call-done = f32[88,176]{1,0:T(8,128)} async-done(((f32[2816,176]{1,0:T(8,128)}), f32[88,176]{1,0:T(8,128)}) %reduce-scatter.16.cloned.1.call-update) | async-done | bytes 61968 | tf_op jit(solution)/shard_map/reduce_scatter | solution.py:385
  1359.8 496.0 %reduce-scatter.10.cloned.1.call-done = f32[64,2816]{1,0:T(8,128)} async-done(((f32[2048,2816]{1,0:T(8,128)}), f32[64,2816]{1,0:T(8,128)}) %reduce-scatter.10.cloned.1.call-update) | async-done | bytes 720912 | tf_op jit(solution)/shard_map/reduce_scatter | solution.py:380
  1855.8 496.0 %reduce-scatter.12.cloned.1.call-done = f32[64,2816]{1,0:T(8,128)} async-done(((f32[2048,2816]{1,0:T(8,128)}), f32[64,2816]{1,0:T(8,128)}) %reduce-scatter.12.cloned.1.call-update) | async-done | bytes 720912 | tf_op jit(solution)/shard_map/reduce_scatter | solution.py:381
  2351.8 495.9 %reduce-scatter.18.cloned.1.call-done = f32[88,2048]{1,0:T(8,128)} async-done(((f32[2816,2048]{1,0:T(8,128)}), f32[88,2048]{1,0:T(8,128)}) %reduce-scatter.18.cloned.1.call-update) | async-done | bytes 720912 | tf_op jit(solution)/shard_map/reduce_scatter | solution.py:386
  2847.7 437.3 %reduce-scatter.20.cloned.1.call-done = f32[64,6144]{1,0:T(8,128)} async-done(((f32[2048,6144]{1,0:T(8,128)}), f32[64,6144]{1,0:T(8,128)}) %reduce-scatter.20.cloned.1.call-update) | async-done | bytes 1572880 | tf_op jit(solution)/shard_map/reduce_scatter | solution.py:365
  3285.0 437.5 %reduce-scatter.22.cloned.1.call-done = f32[64,6144]{1,0:T(8,128)} async-done(((f32[2048,6144]{1,0:T(8,128)}), f32[64,6144]{1,0:T(8,128)}) %reduce-scatter.22.cloned.1.call-update) | async-done | bytes 1572880 | tf_op jit(solution)/shard_map/reduce_scatter | solution.py:366
  3722.4 437.3 %reduce-scatter.24.cloned.1.call-done = f32[192,2048]{1,0:T(8,128)} async-done(((f32[6144,2048]{1,0:T(8,128)}), f32[192,2048]{1,0:T(8,128)}) %reduce-scatter.24.cloned.1.call-update) | async-done | bytes 1572880 | tf_op jit(solution)/shard_map/reduce_scatter | solution.py:367
  (336 shorter events, 106.8 us)
Async XLA Ops:
  7.2 315.1 %all-gather.8.cloned.1.call-start = ((), (), s32[]{:S(2)}) async-start(), calls=%async_computation.8 | async-start | bytes 11894784 | tf_op jit(solution)/shard_map/all_gather | solution.py:304
  7.9 383.8 %all-gather.10.cloned.1.call-start = ((), (), s32[]{:S(2)}) async-start(), calls=%async_computation.9 | async-start | bytes 11894784 | tf_op jit(solution)/shard_map/all_gather | solution.py:305
  8.7 3.5 copy-start.55
  8.7 3.8 copy-start.56
  8.7 47.1 %copy-start.50 = (bf16[4,88]{1,0:T(4,128)(2,1)S(1)}, bf16[4,88]{1,0:T(4,128)(2,1)}, u32[]{:S(2)}) copy-start(bf16[4,88]{1,0:T(4,128)(2,1)} %param.28) | copy-start | bytes 2116
  8.7 391.1 %all-gather.12.cloned.1.call-start = ((), (), s32[]{:S(2)}) async-start(), calls=%async_computation.10 | async-start | bytes 11894784 | tf_op jit(solution)/shard_map/all_gather | solution.py:310
  9.4 113.0 %copy-start = (bf16[1,128,2048]{2,1,0:T(8,128)(2,1)S(1)}, bf16[1,128,2048]{2,1,0:T(8,128)(2,1)}, u32[]{:S(2)}) copy-start(bf16[1,128,2048]{2,1,0:T(8,128)(2,1)} %param.21) | copy-start | bytes 1572868
  9.5 471.4 %all-gather.14.cloned.1.call-start = ((), (), s32[]{:S(2)}) async-start(), calls=%async_computation.11 | async-start | bytes 25952256 | tf_op jit(solution)/shard_map/all_gather | solution.py:314
  10.0 113.2 %copy-start.48 = (f32[1,2816]{1,0:T(1,128)S(1)}, f32[1,2816]{1,0:T(1,128)}, u32[]{:S(2)}) copy-start(f32[1,2816]{1,0:T(1,128)} %param.23) | copy-start | bytes 33796
  10.0 113.9 %copy-start.43 = (bf16[88,176]{1,0:T(8,128)(2,1)S(1)}, bf16[88,176]{1,0:T(8,128)(2,1)}, u32[]{:S(2)}) copy-start(bf16[88,176]{1,0:T(8,128)(2,1)} %param.30) | copy-start | bytes 92932
  10.0 626.4 %all-gather.16.cloned.1.call-start = ((), (), s32[]{:S(2)}) async-start(), calls=%async_computation.12 | async-start | bytes 25952256 | tf_op jit(solution)/shard_map/all_gather | solution.py:315
  10.6 781.4 %all-gather.18.cloned.1.call-start = ((), (), s32[]{:S(2)}) async-start(), calls=%async_computation.13 | async-start | bytes 25952256 | tf_op jit(solution)/shard_map/all_gather | solution.py:316
  11.2 210.8 %copy-start.44 = (bf16[88,176]{1,0:T(8,128)(2,1)S(1)}, bf16[88,176]{1,0:T(8,128)(2,1)}, u32[]{:S(2)}) copy-start(bf16[88,176]{1,0:T(8,128)(2,1)} %param.31) | copy-start | bytes 92932
  11.2 1062.8 %all-reduce.20.cloned.1.call-start = ((), (), s32[]{:S(2)}) async-start(), calls=%async_computation.22 | async-start | bytes 147456
  55.8 266.5 %copy-start.46 = (bf16[2816]{0:T(1024)(128)(2,1)}, bf16[2816]{0:T(1024)(128)(2,1)S(1)}, u32[]{:S(2)}) copy-start(bf16[2816]{0:T(1024)(128)(2,1)S(1)} %get-tuple-element.273) | copy-start | bytes 16900
  122.5 205.8 %copy-start.32 = (f32[2816]{0:T(1024)}, f32[2816]{0:T(1024)S(1)}, u32[]{:S(2)}) copy-start(f32[2816]{0:T(1024)S(1)} %get-tuple-element.244) | copy-start | bytes 33796
  122.5 205.8 %copy-start.34 = (f32[2816]{0:T(1024)}, f32[2816]{0:T(1024)S(1)}, u32[]{:S(2)}) copy-start(f32[2816]{0:T(1024)S(1)} %get-tuple-element.245) | copy-start | bytes 33796
  122.5 205.8 %copy-start.36 = (f32[2816]{0:T(1024)}, f32[2816]{0:T(1024)S(1)}, u32[]{:S(2)}) copy-start(f32[2816]{0:T(1024)S(1)} %get-tuple-element.246) | copy-start | bytes 33796
  122.5 205.8 %copy-start.38 = (f32[2816]{0:T(1024)}, f32[2816]{0:T(1024)S(1)}, u32[]{:S(2)}) copy-start(f32[2816]{0:T(1024)S(1)} %get-tuple-element.247) | copy-start | bytes 33796
  123.2 268.5 %copy-start.40 = (f32[128]{0:T(128)}, f32[128]{0:T(128)S(1)}, u32[]{:S(2)}) copy-start(f32[128]{0:T(128)S(1)} %fusion.70) | copy-start | bytes 1540
  123.9 198.3 %copy-start.45 = (f32[1,3,2816]{2,0,1:T(1,128)S(1)}, f32[1,3,2816]{2,0,1:T(1,128)}, u32[]{:S(2)}) copy-start(f32[1,3,2816]{2,0,1:T(1,128)} %param.22) | copy-start | bytes 101380
  222.0 108.4 %copy-start.24 = (bf16[2816,176]{1,0:T(8,128)(2,1)}, bf16[2816,176]{1,0:T(8,128)(2,1)S(1)}, u32[]{:S(2)}) copy-start(bf16[2816,176]{1,0:T(8,128)(2,1)S(1)} %all_gather.51) | copy-start | bytes 2973700
  322.2 6.1 copy-start.30
  330.1 15.0 copy-start.10
  349.0 579.3 %copy-start.3 = (f32[128,2816]{1,0:T(8,128)}, f32[128,2816]{1,0:T(8,128)S(1)}, u32[]{:S(2)}) copy-start(f32[128,2816]{1,0:T(8,128)S(1)} %get-tuple-element.279) | copy-start | bytes 4325380
  406.2 434.0 %copy-start.1 = (f32[128,2048]{1,0:T(8,128)}, f32[128,2048]{1,0:T(8,128)S(1)}, u32[]{:S(2)}) copy-start(f32[128,2048]{1,0:T(8,128)S(1)} %get-tuple-element.301) | copy-start | bytes 3145732
  842.0 10.6 copy-start.14
  891.2 12.2 copy-start.11
  891.2 12.2 copy-start.42
  928.3 6.6 copy-start.33
  928.3 6.6 copy-start.35
  928.3 6.6 copy-start.37
  928.3 6.6 copy-start.39
  934.9 12.1 slice-start
  935.4 11.6 slice-start.1
  937.5 9.5 copy-start.22
  938.2 8.9 slice-start.2
  938.2 8.9 copy-start.27
  938.2 8.9 copy-start.41
  947.1 5.5 copy-start.20
  952.6 264.7 %reduce-scatter.14.cloned.1.call-start = ((), (), s32[]{:S(2)}) async-start(), calls=%async_computation.16 | async-start | bytes 2973696 | tf_op jit(solution)/shard_map/reduce_scatter | solution.py:384
  956.0 403.8 %reduce-scatter.16.cloned.1.call-start = ((), (), s32[]{:S(2)}) async-start(), calls=%async_computation.17 | async-start | bytes 2973696 | tf_op jit(solution)/shard_map/reduce_scatter | solution.py:385
  960.3 895.5 %reduce-scatter.10.cloned.1.call-start = ((), (), s32[]{:S(2)}) async-start(), calls=%async_computation.14 | async-start | bytes 23789568 | tf_op jit(solution)/shard_map/reduce_scatter | solution.py:380
  971.0 1380.9 %reduce-scatter.12.cloned.1.call-start = ((), (), s32[]{:S(2)}) async-start(), calls=%async_computation.15 | async-start | bytes 23789568 | tf_op jit(solution)/shard_map/reduce_scatter | solution.py:381
  981.6 1866.1 %reduce-scatter.18.cloned.1.call-start = ((), (), s32[]{:S(2)}) async-start(), calls=%async_computation.18 | async-start | bytes 23789568 | tf_op jit(solution)/shard_map/reduce_scatter | solution.py:386
  993.5 2291.5 %reduce-scatter.20.cloned.1.call-start = ((), (), s32[]{:S(2)}) async-start(), calls=%async_computation.19 | async-start | bytes 51904512 | tf_op jit(solution)/shard_map/reduce_scatter | solution.py:365
  1014.4 2708.0 %reduce-scatter.22.cloned.1.call-start = ((), (), s32[]{:S(2)}) async-start(), calls=%async_computation.20 | async-start | bytes 51904512 | tf_op jit(solution)/shard_map/reduce_scatter | solution.py:366
  1035.3 3124.4 %reduce-scatter.24.cloned.1.call-start = ((), (), s32[]{:S(2)}) async-start(), calls=%async_computation.21 | async-start | bytes 51904512 | tf_op jit(solution)/shard_map/reduce_scatter | solution.py:367
  (27 other events, 50.5 us)
Sparse Core Ops, SparseCore 0:
  10.8 94.8 all-gather.7
  108.6 105.7 all-gather.9
  217.2 106.5 all-gather.11
  326.5 154.2 all-gather.13
  483.5 152.8 all-gather.15
  639.1 152.8 all-gather.17
  952.7 117.7 all-reduce.19
  1073.3 143.9 reduce-scatter.13
  1220.1 139.6 reduce-scatter.15
  1362.5 493.2 reduce-scatter.9
  1858.7 493.0 reduce-scatter.11
  2354.6 493.0 reduce-scatter.17
  2854.7 430.2 reduce-scatter.19
  3291.8 430.5 reduce-scatter.21
  3729.3 430.4 reduce-scatter.23
where the time goes:
time: 4170 us
  waiting for transfers between devices  3440 us (82%)
  blocking collectives  308 us (7%)
  matrix products  240 us (6%)
  local copies, waits for them, and re-layouts  93.8 us (2%)
  other arithmetic  64.8 us (2%)
    reduce_scatter x1, waiting for transfers between devices, shards(): lax.psum_scatter(mixer_total[1], ('wide', 'narrow'), scatter_dimension=0,...  496 us
    reduce_scatter x1, waiting for transfers between devices, shards(): lax.psum_scatter(mixer_total[2], ('wide', 'narrow'), scatter_dimension=0,...  496 us
    reduce_scatter x1, waiting for transfers between devices, shards(): lax.psum_scatter(mixer_total[7], ('wide', 'narrow'), scatter_dimension=0,...  496 us
    reduce_scatter x1, waiting for transfers between devices, shards(): lax.psum_scatter(mlp_total[2], ('wide', 'narrow'), scatter_dimension=0, t...  437 us
    reduce_scatter x1, waiting for transfers between devices, shards(): lax.psum_scatter(mlp_total[3], ('wide', 'narrow'), scatter_dimension=0, t...  437 us
    reduce_scatter x1, waiting for transfers between devices, shards(): lax.psum_scatter(mlp_total[1], ('wide', 'narrow'), scatter_dimension=0, t...  437 us
    reduce_scatter x1, waiting for transfers between devices, shards(): lax.psum_scatter(mixer_total[6], ('wide', 'narrow'), scatter_dimension=0,...  143 us
    all_gather x1, waiting for transfers between devices, shards(): lax.all_gather(mlp_down, ('wide', 'narrow'), axis=0, tiled=True)  142 us
  transfers between devices with their start and end apart: 15, of which 11 were waited for; matrix products, arithmetic and copies ran while one was open for 6% of the time, Pallas kernels for 0%

commit v1 on v0

--- a/solution.py
+++ b/solution.py
@@ -1,8 +1,12 @@
+import functools
+import itertools
 from functools import reduce
 
 import jax
 import jax.numpy as jnp
 from jax import lax
+from jax.experimental import pallas as pl
+from jax.experimental.pallas import tpu as pltpu
 from jax.sharding import PartitionSpec as P
 
 BLOCKS = 16
@@ -405,9 +409,1132 @@
     )
 
 
+COLUMNS = 4
+LOWS = 2
+PARTS = COLUMNS * LOWS
+TOK = 128
+CHUNK = 88
+LANES = 96
+WIDTH = 4 * LANES
+SPAN = PARTS * TOK
+MESH = pl.DeviceIdType.MESH
+VMEM_BYTES = 60 * 1024 * 1024
+low_type = jnp.bfloat16
+full_type = jnp.float32
+
+
+class Place:
+    def __init__(self):
+        wide = lax.axis_index("wide")
+        self.z = lax.axis_index("narrow")
+        self.column, self.core = wide // 2, wide % 2
+        self.half, self.low = self.z // 2, self.z % 2
+        self.part = self.column * 2 + self.low
+        self.index = wide * 4 + self.z
+        self.own = (self.column // 2, self.column % 2, self.low)
+
+    def shifted(self, by_y, by_x, by_low, by_half):
+        column = (self.column // 2 + by_y) % 2 * 2 + (self.column % 2 + by_x) % 2
+        low, half = (self.low + by_low) % 2, (self.half + by_half) % 2
+        return (column, low, half)
+
+    def neighbour(self, axis):
+        y, x, low = (1 - at if axis == here else at for here, at in enumerate(self.own))
+        return (y * 4 + x * 2 + self.core, self.half * 2 + low)
+
+    def cube(self, fixed, other=None):
+        return tuple(
+            1 - at if axis == other else at if axis in fixed else slice(None)
+            for axis, at in enumerate(self.own)
+        )
+
+    def sibling(self):
+        return (self.column * 2 + 1 - self.core, self.z)
+
+
+def greet_all(place):
+    barrier = pltpu.get_barrier_semaphore()
+
+    @pl.loop(1, 32)
+    def _(step):
+        other = (place.index + step) % 32
+        pl.semaphore_signal(
+            barrier, inc=1, device_id=(other // 4, other % 4), device_id_type=MESH
+        )
+
+    pl.semaphore_wait(barrier, 31)
+
+
+def remote(source, target, send, receive, device):
+    return pltpu.make_async_remote_copy(
+        src_ref=source,
+        dst_ref=target,
+        send_sem=send,
+        recv_sem=receive,
+        device_id=device,
+        device_id_type=MESH,
+    )
+
+
+def await_bytes(view, semaphore):
+    pltpu.make_async_copy(view, view, semaphore).wait()
+
+
+class Spread:
+    def __init__(self, pick):
+        self.pick = pick
+
+    def start(self, place, source, target, sems):
+        self.copies = []
+        slot = target.at[place.column, place.core, place.z]
+        for shift in itertools.product(range(2), repeat=4):
+            column, low, half = place.shifted(*shift)
+            block = self.pick(source, column * 2 + low)
+            if any(shift):
+                copy = remote(
+                    block, slot, sems.at[0], sems.at[1], (column * 2 + place.core, half * 2 + low)
+                )
+                copy.start()
+                self.copies.append(copy)
+            else:
+                pltpu.make_async_copy(block, slot, sems.at[1]).start()
+
+    def relay(self, place, source, target, sems):
+        mine = target.at[:, place.core]
+        await_bytes(mine, sems.at[1])
+        self.passed = remote(mine, mine, sems.at[2], sems.at[3], place.sibling())
+        self.passed.start()
+
+    def finish(self, place, source, target, sems):
+        self.passed.wait()
+        for copy in self.copies:
+            copy.wait_send()
+
+
+class RowSpread:
+    def start(self, place, source, target, sems):
+        self.copies = []
+        slot = target.at[place.half, place.low]
+        for half in range(2):
+            copy = remote(
+                source,
+                slot,
+                sems.at[0],
+                sems.at[1],
+                (place.column * 2 + place.low, half * 2 + place.core),
+            )
+            own = (place.low == place.core) & (place.half == half)
+
+            @pl.when(own)
+            def _():
+                pltpu.make_async_copy(source, slot, sems.at[1]).start()
+
+            @pl.when(jnp.logical_not(own))
+            def _():
+                copy.start()
+
+            self.copies.append((own, copy))
+
+    def relay(self, place, source, target, sems):
+        mine = target.at[:, place.core]
+        await_bytes(mine, sems.at[1])
+        self.passed = remote(mine, mine, sems.at[2], sems.at[3], place.sibling())
+        self.passed.start()
+
+    def finish(self, place, source, target, sems):
+        self.passed.wait()
+        for own, copy in self.copies:
+
+            @pl.when(jnp.logical_not(own))
+            def _():
+                copy.wait_send()
+
+
+class Peers:
+    def __init__(self, pick):
+        self.pick = pick
+
+    def start(self, place, source, target, sems):
+        self.copies = []
+        slot = target.at[place.part]
+        for shift in itertools.product(range(2), repeat=3):
+            column, low, half = place.shifted(*shift, 0)
+            block = self.pick(source, column * 2 + low)
+            if any(shift):
+                copy = remote(
+                    block, slot, sems.at[0], sems.at[1], (column * 2 + place.core, half * 2 + low)
+                )
+                copy.start()
+                self.copies.append(copy)
+            else:
+                pltpu.make_async_copy(block, slot, sems.at[1]).start()
+
+    def relay(self, place, source, target, sems):
+        pass
+
+    def finish(self, place, source, target, sems):
+        await_bytes(target, sems.at[1])
+        for copy in self.copies:
+            copy.wait_send()
+
+
+class Swap:
+    def start(self, place, source, target, sems):
+        self.copy = remote(
+            source.at[:, 1 - place.core], target, sems.at[0], sems.at[1], place.sibling()
+        )
+        self.copy.start()
+
+    def relay(self, place, source, target, sems):
+        pass
+
+    def finish(self, place, source, target, sems):
+        self.copy.wait()
+
+
+class Owners:
+    def start(self, place, source, target, sems):
+        self.copies = []
+        slot = target.at[place.half, place.part]
+        for shift in itertools.product(range(2), repeat=4):
+            column, low, half = place.shifted(*shift)
+            z = half * 2 + low
+            block = source.at[column, z]
+            if any(shift):
+                copy = remote(
+                    block, slot, sems.at[0], sems.at[1], (column * 2 + place.core, z)
+                )
+                copy.start()
+                self.copies.append(copy)
+            else:
+                pltpu.make_async_copy(block, slot, sems.at[1]).start()
+
+    def relay(self, place, source, target, sems):
+        pass
+
+    def finish(self, place, source, target, sems):
+        await_bytes(target, sems.at[1])
+        for copy in self.copies:
+            copy.wait_send()
+
+
+class RowOwners:
+    def start(self, place, source, target, sems):
+        self.copies = []
+        slot = target.at[place.half]
+        for half in range(2):
+            block = source.at[half]
+            copy = remote(
+                block,
+                slot,
+                sems.at[0],
+                sems.at[1],
+                (place.column * 2 + place.low, half * 2 + place.core),
+            )
+            own = (place.low == place.core) & (place.half == half)
+
+            @pl.when(own)
+            def _():
+                pltpu.make_async_copy(block, slot, sems.at[1]).start()
+
+            @pl.when(jnp.logical_not(own))
+            def _():
+                copy.start()
+
+            self.copies.append((own, copy))
+
+    def relay(self, place, source, target, sems):
+        pass
+
+    def finish(self, place, source, target, sems):
+        await_bytes(target, sems.at[1])
+        for own, copy in self.copies:
+
+            @pl.when(jnp.logical_not(own))
+            def _():
+                copy.wait_send()
+
+
+class Semaphores:
+    def __init__(self, array):
+        self.array, self.used = array, 0
+
+    def take(self, count):
+        taken = self.array.at[pl.ds(self.used, count)]
+        self.used += count
+        return taken
+
+
+ORDERS = ((2, 0, 1), (2, 1, 0), (0, 2, 1), (1, 2, 0))
+ROUTES = len(ORDERS)
+
+
+def cuts(width):
+    part = width // ROUTES
+    return [pl.ds(route * part, part) for route in range(ROUTES)]
+
+
+class CubeGather:
+    def __init__(self, place, buffer, semaphores):
+        self.place, self.buffer, self.copies = place, buffer, []
+        self.sems = semaphores.take(6 * ROUTES)
+
+    def step(self, number):
+        rows = pl.ds(0, self.buffer.shape[3])
+        for order, cut in enumerate(cuts(self.buffer.shape[4])):
+            axes = ORDERS[order]
+            if number > 0:
+                self.copies[ROUTES * (number - 1) + order].wait_recv()
+            region = self.buffer.at[self.place.cube(axes[number:]) + (rows, cut)]
+            index = ROUTES * number + order
+            copy = remote(
+                region,
+                region,
+                self.sems.at[index],
+                self.sems.at[3 * ROUTES + index],
+                self.place.neighbour(axes[number]),
+            )
+            copy.start()
+            self.copies.append(copy)
+
+    def finish(self):
+        for copy in self.copies[2 * ROUTES :]:
+            copy.wait_recv()
+        for copy in self.copies:
+            copy.wait_send()
+
+
+class CubeSum:
+    def __init__(self, place, blocks, landings, semaphores):
+        self.place, self.blocks, self.landings, self.copies = place, blocks, landings, []
+        self.sems = semaphores.take(6 * ROUTES)
+
+    def send(self, number, order, cut):
+        axes = ORDERS[order][::-1]
+        index = ROUTES * number + order
+        rows = pl.ds(0, TOK)
+        landing = self.landings[number]
+        copy = remote(
+            self.blocks.at[self.place.cube(axes[:number], axes[number]) + (rows, cut)],
+            landing.at[(slice(None),) * (2 - number) + (rows, cut)],
+            self.sems.at[index],
+            self.sems.at[3 * ROUTES + index],
+            self.place.neighbour(axes[number]),
+        )
+        copy.start()
+        self.copies.append(copy)
+
+    def start(self):
+        for order, cut in enumerate(cuts(self.blocks.shape[4])):
+            self.send(0, order, cut)
+
+    def step(self, number, result=None):
+        for order, cut in enumerate(cuts(self.blocks.shape[4])):
+            axes = ORDERS[order][::-1]
+            self.copies[ROUTES * number + order].wait_recv()
+            landing = self.landings[number]
+            for picks in itertools.product(range(2), repeat=2 - number):
+                chosen = iter(picks)
+                index = tuple(
+                    self.place.own[axis] if axis in axes[: number + 1] else next(chosen)
+                    for axis in range(3)
+                )
+
+                @pl.loop(0, TOK // 32)
+                def _(block):
+                    rows = pl.ds(pl.multiple_of(block * 32, 32), 32)
+                    total = self.blocks[index + (rows, cut)].astype(full_type) + landing[
+                        picks + (rows, cut)
+                    ].astype(full_type)
+                    if number < 2:
+                        self.blocks[index + (rows, cut)] = total.astype(low_type)
+                    else:
+                        result[rows, cut] = total
+
+            if number < 2:
+                self.send(number + 1, order, cut)
+
+    def finish(self):
+        for copy in self.copies:
+            copy.wait_send()
+
+
+class Move:
+    def __init__(self, place, plan, source, target, semaphores):
+        self.plan, self.arguments = plan, (place, source, target, semaphores.take(4))
+
+    def start(self):
+        self.plan.start(*self.arguments)
+
+    def relay(self):
+        self.plan.relay(*self.arguments)
+
+    def finish(self):
+        self.plan.finish(*self.arguments)
+
+
+class Local:
+    def __init__(self, semaphores):
+        self.semaphores, self.copies = semaphores, []
+
+    def start(self, source, target):
+        copy = pltpu.make_async_copy(source, target, self.semaphores.take(1).at[0])
+        copy.start()
+        self.copies.append(copy)
+        return copy
+
+    def finish(self):
+        for copy in self.copies:
+            copy.wait()
+
+
+def whole(source, part):
+    return source
+
+
+def by_part(source, part):
+    return source.at[part]
+
+
+def by_columns(source, part):
+    width = source.shape[1] // PARTS
+    return source.at[:, pl.ds(pl.multiple_of(part * width, 128), width)]
+
+
+def exchange_kernel(plan, *refs):
+    count = len(plan)
+    sources, targets, sems = refs[:count], refs[count : 2 * count], refs[2 * count]
+    place = Place()
+    greet_all(place)
+    for step in ("start", "relay", "finish"):
+        for index, move in enumerate(plan):
+            getattr(move, step)(place, sources[index], targets[index], sems.at[index])
+
+
+def exchange(name, identity, moves):
+    plan = [move for move, array, shape in moves]
+    hbm = pl.BlockSpec(memory_space=pl.ANY)
+    return pl.pallas_call(
+        functools.partial(exchange_kernel, plan),
+        out_shape=[jax.ShapeDtypeStruct(shape, array.dtype) for move, array, shape in moves],
+        in_specs=[hbm] * len(moves),
+        out_specs=[hbm] * len(moves),
+        scratch_shapes=[pltpu.SemaphoreType.DMA((len(moves), 4))],
+        compiler_params=pltpu.CompilerParams(collective_id=identity, has_side_effects=True),
+        name=name,
+    )(*[array for move, array, shape in moves])
+
+
+def row_block(row):
+    return pl.ds(pl.multiple_of(row * TOK, TOK), TOK)
+
+
+def small_expm1(values):
+    near = values * (
+        1.0
+        + values
+        * (0.5 + values * (1 / 6 + values * (1 / 24 + values * (1 / 120 + values * (1 / 720)))))
+    )
+    return jnp.where(values > -0.25, near, jnp.exp(values) - 1.0)
+
+
+def gelu_parts(values):
+    scale = 0.7978845608028654
+    bent = jnp.tanh(scale * (values + 0.044715 * values * values * values))
+    slope = 0.5 * (1.0 + bent) + 0.5 * values * (1.0 - bent * bent) * scale * (
+        1.0 + 3 * 0.044715 * values * values
+    )
+    return (0.5 * values * (1.0 + bent), slope)
+
+
+def put(array, rows, values):
+    for piece in range(WIDTH // 128):
+        array[piece, rows, :] = values[:, piece * 128 : (piece + 1) * 128]
+
+
+def take(array, rows):
+    return jnp.concatenate([array[piece, rows, :] for piece in range(WIDTH // 128)], axis=1)
+
+
+def taps_of(aux):
+    return [aux[tap : tap + 1, :] for tap in range(4)]
+
+
+def placed_sum(gathered, place, row):
+    owners = [
+        gathered[place.part // 2, place.part % 2, z, row : row + 1, :].astype(full_type)
+        for z in range(4)
+    ]
+    return owners[0] + owners[1] + owners[2] + owners[3]
+
+
+def placed_gain(gathered, row):
+    pieces = []
+    for column, core, pair in itertools.product(range(COLUMNS), range(2), range(2)):
+        both = [
+            gathered[column, core, 2 * pair + odd, row : row + 1, 0:128].astype(full_type)
+            for odd in range(2)
+        ]
+        pieces.append(both[0] + both[1])
+    return jnp.concatenate(pieces, axis=1)
+
+
+def scaled_norm(values, gain):
+    scale = lax.rsqrt(jnp.mean(values * values, axis=1, keepdims=True) + epsilon)
+    return values * scale * gain
+
+
+def forward_kernel(
+    tokens,
+    small,
+    states,
+    columns,
+    gates,
+    out_rows,
+    mlp_gate,
+    mlp_up,
+    mlp_down,
+    cotangent,
+    normed_out,
+    states_out,
+    columns_out,
+    gates_out,
+    rows_out,
+    gate_out,
+    up_out,
+    down_out,
+    cot_out,
+    pre_out,
+    conv_out,
+    logits_out,
+    hidden_out,
+    mixed_out,
+    after_out,
+    two_out,
+    aux_out,
+    gains_out,
+    tokens_all,
+    small_all,
+    states_all,
+    columns_all,
+    gates_all,
+    rows_all,
+    normed,
+    pre,
+    conv,
+    logits,
+    hidden,
+    mixed,
+    decays,
+    inputs,
+    padded,
+    blocks,
+    landing_one,
+    landing_two,
+    landing_three,
+    after,
+    two_all,
+    aux,
+    gains,
+    sems,
+):
+    place = Place()
+    semaphores = Semaphores(sems)
+    local = Local(semaphores)
+
+    def move(plan, source, target):
+        return Move(place, plan, source, target, semaphores)
+
+    own_tokens = tokens_all.at[place.own]
+    load = pltpu.make_async_copy(tokens, own_tokens, semaphores.take(1).at[0])
+    load.start()
+    greet_all(place)
+    load.wait()
+    tokens_gather = CubeGather(place, tokens_all, semaphores)
+    tokens_gather.step(0)
+    small_move = move(Spread(whole), small, small_all)
+    small_move.start()
+    states_move = move(Peers(by_part), states, states_all)
+    states_move.start()
+    columns_move = move(Spread(by_part), columns, columns_all)
+    columns_move.start()
+    gates_move = move(RowSpread(), gates, gates_all)
+    gates_move.start()
+    rows_move = move(RowSpread(), out_rows, rows_all)
+    rows_move.start()
+    local.start(cotangent, cot_out.at[place.own])
+    tokens_gather.step(1)
+    small_move.relay()
+    tokens_gather.step(2)
+    late = [
+        move(Spread(by_columns), mlp_gate, gate_out),
+        move(Spread(by_columns), mlp_up, up_out),
+        move(RowSpread(), mlp_down, down_out),
+    ]
+    for item in late:
+        item.start()
+    small_move.finish()
+    for tap in range(5):
+        aux[tap : tap + 1, :] = placed_sum(small_all, place, tap)
+    decay = aux[4:5, :]
+    aux[4:5, :] = jnp.maximum(-decay, 0.0) + jnp.log1p(jnp.exp(-jnp.abs(decay)))
+    aux[5:6, :] = jax.nn.sigmoid(-decay)
+    aux[6:8, :] = jnp.zeros((2, WIDTH), full_type)
+    gains[0:1, :] = placed_gain(small_all, 5)
+    gains[1:2, :] = placed_gain(small_all, 6)
+    tokens_gather.finish()
+
+    @pl.loop(0, SPAN // 32)
+    def _(step):
+        part, piece = step // 4, step % 4
+        rows = pl.ds(pl.multiple_of(piece * 32, 32), 32)
+        values = tokens_all[part // 4, part // 2 % 2, part % 2, rows, :].astype(full_type)
+        normed[pl.ds(pl.multiple_of(step * 32, 32), 32), :] = scaled_norm(
+            values, gains[0:1, :]
+        ).astype(low_type)
+
+    local.start(normed, normed_out)
+    local.start(aux, aux_out)
+    local.start(gains, gains_out)
+    columns_move.relay()
+    gates_move.relay()
+    rows_move.relay()
+    columns_move.finish()
+    local.start(columns_all, columns_out)
+
+    @pl.loop(0, SPAN // 256)
+    def _(step):
+        rows = pl.ds(pl.multiple_of(step * 256, 256), 256)
+        pre[rows, :] = jnp.dot(
+            normed[rows, :],
+            columns_all[...].reshape(-1, 2 * WIDTH),
+            preferred_element_type=full_type,
+        )
+
+    local.start(pre, pre_out)
+    gates_move.finish()
+    states_move.finish()
+    local.start(gates_all, gates_out)
+    local.start(states_all, states_out)
+    taps = taps_of(aux)
+    soft = aux[4:5, :]
+
+    @pl.loop(0, PARTS)
+    def _(row):
+        rows = row_block(row)
+        padded[0:8, :] = states_all[row]
+        padded[8 : 8 + TOK, :] = pre[rows, 0:WIDTH]
+        total = taps[0] * padded[8 : 8 + TOK, :]
+        for tap in range(1, 4):
+            total = total + taps[tap] * padded[8 - tap : 8 - tap + TOK, :]
+        low = total.astype(low_type)
+        conv[rows, :] = low
+        both = jnp.dot(
+            low, gates_all[...].reshape(WIDTH, 2 * WIDTH), preferred_element_type=full_type
+        )
+        logits[rows, :] = both
+        log_decay = -8.0 * jax.nn.sigmoid(both[:, 0:WIDTH]) * soft
+        scale = jnp.sqrt(-small_expm1(2.0 * log_decay))
+        put(inputs, rows, scale * jax.nn.sigmoid(both[:, WIDTH:]) * low.astype(full_type))
+        put(decays, rows, jnp.exp(log_decay))
+
+    local.start(conv, conv_out)
+    local.start(logits, logits_out)
+
+    def advance(time, carried):
+        across = pl.ds(time, PARTS, stride=TOK)
+        carried = [
+            decays[piece, across, :] * before + inputs[piece, across, :]
+            for piece, before in enumerate(carried)
+        ]
+        for piece, now in enumerate(carried):
+            hidden[piece, across, :] = now
+        return carried
+
+    initial = states_all[:, 0, :]
+    initial = [initial[:, piece * 128 : (piece + 1) * 128] for piece in range(WIDTH // 128)]
+    lax.fori_loop(0, TOK, advance, initial, unroll=8)
+    local.start(hidden, hidden_out)
+    rows_move.finish()
+    local.start(rows_all, rows_out)
+
+    @pl.loop(0, PARTS)
+    def _(row):
+        rows = row_block(row)
+        gated, _ = gelu_parts(pre[rows, WIDTH:])
+        low = (take(hidden, rows) * gated).astype(low_type)
+        mixed[rows, :] = low
+        blocks[row // 4, row // 2 % 2, row % 2] = jnp.dot(
+            low, rows_all[...].reshape(WIDTH, -1), preferred_element_type=full_type
+        ).astype(low_type)
+
+    local.start(mixed, mixed_out)
+    mixer_sum = CubeSum(place, blocks, (landing_one, landing_two, landing_three), semaphores)
+    mixer_sum.start()
+    mixer_sum.step(0)
+    mixer_sum.step(1)
+    mixer_sum.step(2, after)
+
+    @pl.loop(0, TOK // 32)
+    def _(step):
+        rows = pl.ds(pl.multiple_of(step * 32, 32), 32)
+        total = after[rows, :] + tokens_all[place.own + (rows,)].astype(full_type)
+        after[rows, :] = total
+        two_all[place.own + (rows,)] = scaled_norm(total, gains[1:2, :]).astype(low_type)
+
+    local.start(after, after_out)
+    two_gather = CubeGather(place, two_all, semaphores)
+    two_gather.step(0)
+    cot_gather = CubeGather(place, cot_out, semaphores)
+    local.copies[0].wait()
+    cot_gather.step(0)
+    two_gather.step(1)
+    cot_gather.step(1)
+    two_gather.step(2)
+    cot_gather.step(2)
+    two_gather.finish()
+    local.start(two_all, two_out)
+    mixer_sum.finish()
+    for item in late:
+        item.relay()
+    cot_gather.finish()
+    for item in late:
+        item.finish()
+    states_move_done = local.copies[1:]
+    for copy in states_move_done:
+        copy.wait()
+
+
+def forward_mixer(arrays, rows, width, units):
+    hbm = pl.BlockSpec(memory_space=pl.ANY)
+    lanes = (WIDTH // 128, SPAN, 128)
+    cube = (2, 2, 2, TOK, width)
+    spread = (COLUMNS, 2, 4, rows)
+    outputs = [
+        ((SPAN, width), low_type),
+        ((PARTS, 8, WIDTH), full_type),
+        (spread + (2 * WIDTH,), low_type),
+        ((2, 2, LANES, 2 * WIDTH), low_type),
+        ((2, 2, LANES, width), low_type),
+        (spread + (4 * units,), low_type),
+        (spread + (4 * units,), low_type),
+        ((2, 2, units, width), low_type),
+        (cube, low_type),
+        ((SPAN, 2 * WIDTH), full_type),
+        ((SPAN, WIDTH), low_type),
+        ((SPAN, 2 * WIDTH), full_type),
+        (lanes, full_type),
+        ((SPAN, WIDTH), low_type),
+        ((TOK, width), full_type),
+        (cube, low_type),
+        ((8, WIDTH), full_type),
+        ((2, width), full_type),
+    ]
+    scratch = [
+        (cube, low_type),
+        ((COLUMNS, 2, 4, 16, WIDTH), low_type),
+        ((PARTS, 8, WIDTH), full_type),
+        (spread + (2 * WIDTH,), low_type),
+        ((2, 2, LANES, 2 * WIDTH), low_type),
+        ((2, 2, LANES, width), low_type),
+        ((SPAN, width), low_type),
+        ((SPAN, 2 * WIDTH), full_type),
+        ((SPAN, WIDTH), low_type),
+        ((SPAN, 2 * WIDTH), full_type),
+        (lanes, full_type),
+        ((SPAN, WIDTH), low_type),
+        (lanes, full_type),
+        (lanes, full_type),
+        ((TOK + 8, WIDTH), full_type),
+        (cube, low_type),
+        ((2, 2, TOK, width), low_type),
+        ((2, TOK, width), low_type),
+        ((TOK, width), low_type),
+        ((TOK, width), full_type),
+        (cube, low_type),
+        ((8, WIDTH), full_type),
+        ((2, width), full_type),
+    ]
+    return pl.pallas_call(
+        forward_kernel,
+        out_shape=[jax.ShapeDtypeStruct(shape, kind) for shape, kind in outputs],
+        in_specs=[hbm] * len(arrays),
+        out_specs=[hbm] * len(outputs),
+        scratch_shapes=[pltpu.VMEM(shape, kind) for shape, kind in scratch]
+        + [pltpu.SemaphoreType.DMA((192,))],
+        compiler_params=pltpu.CompilerParams(
+            collective_id=0, has_side_effects=True, vmem_limit_bytes=VMEM_BYTES
+        ),
+        name="forward_mixer",
+    )(*arrays)
+
+
+def mixer_backward_kernel(
+    pre,
+    states,
+    aux,
+    blocks,
+    conv_out,
+    logits,
+    hidden,
+    grad_branch,
+    grad_pre,
+    grad_blocks,
+    grad_states,
+    grad_aux,
+    decays,
+    carries,
+    padded,
+):
+    taps = taps_of(aux)
+    soft, slope = aux[4:5, :], aux[5:6, :]
+
+    @pl.loop(0, PARTS)
+    def _(row):
+        rows = row_block(row)
+        gated, bend = gelu_parts(pre[rows, WIDTH:])
+        branch = grad_branch[rows, :]
+        grad_pre[rows, WIDTH:] = (branch * take(hidden, rows) * bend).astype(low_type)
+        put(carries, rows, branch * gated)
+        put(decays, rows, jnp.exp(-8.0 * jax.nn.sigmoid(logits[rows, 0:WIDTH]) * soft))
+
+    def advance(step, state):
+        factors, carried = state
+        across = pl.ds(TOK - 1 - step, PARTS, stride=TOK)
+        carried = [
+            carries[piece, across, :] + factors[piece] * before
+            for piece, before in enumerate(carried)
+        ]
+        for piece, now in enumerate(carried):
+            carries[piece, across, :] = now
+        return ([decays[piece, across, :] for piece in range(WIDTH // 128)], carried)
+
+    zeros = [jnp.zeros((PARTS, 128), full_type)] * (WIDTH // 128)
+    lax.fori_loop(0, TOK, advance, (zeros, zeros), unroll=8)
+    grad_aux[...] = jnp.zeros_like(grad_aux)
+    grad_blocks[...] = jnp.zeros_like(grad_blocks)
+
+    @pl.loop(0, PARTS)
+    def _(row):
+        rows = row_block(row)
+        padded[0:8, :] = jnp.broadcast_to(states[row, 0:1, :], (8, WIDTH))
+        padded[8 : 8 + TOK, :] = take(hidden, rows)
+        recur = jax.nn.sigmoid(logits[rows, 0:WIDTH])
+        gate = jax.nn.sigmoid(logits[rows, WIDTH:])
+        log_decay = -8.0 * recur * soft
+        decay = take(decays, rows)
+        scale = jnp.sqrt(-small_expm1(2.0 * log_decay))
+        low = conv_out[rows, :]
+        conv = low.astype(full_type)
+        carried = take(carries, rows)
+        total = (
+            carried * decay * padded[7 : 7 + TOK, :]
+            - carried * gate * conv * (decay * decay) / scale
+        )
+        grad_aux[4:5, :] += jnp.sum(total * 8.0 * recur * slope, axis=0, keepdims=True)
+        to_recur = (total * (-8.0 * soft) * recur * (1.0 - recur)).astype(low_type)
+        to_input = (carried * scale * conv * gate * (1.0 - gate)).astype(low_type)
+        both = jnp.concatenate([to_recur, to_input], axis=1)
+        grad_blocks[...] += lax.dot_general(
+            low, both, contract_rows, preferred_element_type=full_type
+        )
+        back = carried * scale * gate + lax.dot_general(
+            both, blocks[...], contract_cols, preferred_element_type=full_type
+        )
+        first = decay[0:1, :] * carried[0:1, :]
+        padded[0:8, :] = jnp.zeros((8, WIDTH), full_type)
+        padded[8 : 8 + TOK, :] = back
+        padded[8 + TOK :, :] = jnp.zeros((8, WIDTH), full_type)
+        spread = taps[0] * padded[0 : 8 + TOK, :]
+        for tap in range(1, 4):
+            spread = spread + taps[tap] * padded[tap : tap + 8 + TOK, :]
+        grad_pre[rows, 0:WIDTH] = spread[8:, :].astype(low_type)
+        grad_states[row] = spread[0:8, :]
+        grad_states[row, 0:1, :] = first
+        padded[0:8, :] = states[row]
+        padded[8 : 8 + TOK, :] = pre[rows, 0:WIDTH]
+        for tap in range(4):
+            grad_aux[tap : tap + 1, :] += jnp.sum(
+                back * padded[8 - tap : 8 - tap + TOK, :], axis=0, keepdims=True
+            )
+
+
+def in_vmem(kernel, name, arrays, shapes, scratch):
+    vmem = pl.BlockSpec(memory_space=pltpu.VMEM)
+    return pl.pallas_call(
+        kernel,
+        out_shape=[jax.ShapeDtypeStruct(shape, kind) for shape, kind in shapes],
+        in_specs=[vmem] * len(arrays),
+        out_specs=[vmem] * len(shapes),
+        scratch_shapes=[pltpu.VMEM(shape, kind) for shape, kind in scratch],
+        compiler_params=pltpu.CompilerParams(vmem_limit_bytes=VMEM_BYTES),
+        name=name,
+    )(*arrays)
+
+
+def to_lanes(array):
+    chunks = array.reshape(array.shape[:-1] + (-1, CHUNK))
+    pads = [(0, 0)] * (chunks.ndim - 1) + [(0, LANES - CHUNK)]
+    return jnp.pad(chunks, pads).reshape(array.shape[:-1] + (-1,))
+
+
+def from_lanes(array):
+    chunks = array.reshape(array.shape[:-1] + (-1, LANES))
+    return chunks[..., :CHUNK].reshape(array.shape[:-1] + (-1,))
+
+
+def pad_rows(array, rows):
+    return jnp.pad(array, ((0, rows - array.shape[0]), (0, 0)))
+
+
+def from_dense(dense):
+    pair = 2 * LANES
+    return jnp.concatenate(
+        [
+            jnp.concatenate(
+                [
+                    dense[
+                        block * pair : (block + 1) * pair,
+                        kind * WIDTH + block * pair : kind * WIDTH + (block + 1) * pair,
+                    ]
+                    for kind in range(2)
+                ],
+                axis=1,
+            )
+            for block in range(2)
+        ],
+        axis=0,
+    )
+
+
+def halves(
+    tokens,
+    conv_state,
+    recur_state,
+    fresh_rows,
+    gain_mixer,
+    proj_input,
+    proj_gate,
+    conv_kernel,
+    decay_param,
+    gate_recur,
+    gate_input,
+    proj_output,
+    gain_mlp,
+    mlp_gate,
+    mlp_up,
+    mlp_down,
+    cotangent,
+):
+    width = tokens.shape[2]
+    rows = width // 32
+    units = mlp_down.shape[0]
+    core = lax.axis_index("wide") % 2
+    part = lax.axis_index("wide") // 2 * 2 + lax.axis_index("narrow") % 2
+    keep = (1 - fresh_rows).astype(full_type)[0]
+
+    columns = jnp.concatenate(
+        [
+            to_lanes(proj).reshape(rows, PARTS, WIDTH).transpose(1, 0, 2)
+            for proj in (proj_input, proj_gate)
+        ],
+        axis=2,
+    )
+    zeros = jnp.zeros((CHUNK, 2 * LANES), low_type)
+    first = lax.axis_index("narrow") < 2
+    gates = jnp.concatenate(
+        [
+            jnp.where(chosen, to_lanes(gate), zeros)
+            for gate in (gate_recur, gate_input)
+            for chosen in (first, jnp.logical_not(first))
+        ],
+        axis=1,
+    )
+    z = lax.axis_index("narrow")
+    taps = pad_rows(jnp.concatenate([conv_kernel, decay_param[None]], axis=0), 16)
+    taps = lax.dynamic_update_slice(jnp.zeros((16, WIDTH), low_type), taps, (0, z * LANES))
+    gain_rows = jnp.stack([gain_mixer, gain_mlp])
+    small = lax.dynamic_update_slice(taps, gain_rows, (5, z % 2 * rows))
+    state_rows = jnp.concatenate(
+        [recur_state, jnp.zeros((4, recur_state.shape[1]), full_type), conv_state[0]], axis=0
+    )
+    states = to_lanes(state_rows * keep).reshape(8, PARTS, WIDTH).transpose(1, 0, 2)
+    (
+        normed_all,
+        states_all,
+        columns,
+        gates,
+        out_rows,
+        mlp_gate,
+        mlp_up,
+        down,
+        cot_all,
+        pre,
+        conv_out,
+        logits,
+        hidden,
+        mixed,
+        after_mixer,
+        normed_two_all,
+        aux,
+        gain_rows,
+    ) = forward_mixer(
+        (
+            tokens[0],
+            small,
+            states,
+            columns,
+            pad_rows(gates, LANES),
+            pad_rows(proj_output, LANES),
+            mlp_gate,
+            mlp_up,
+            mlp_down,
+            cotangent[0],
+        ),
+        rows,
+        width,
+        units,
+    )
+    gain_one, gain_two = gain_rows[0], gain_rows[1]
+    values = tokens[0].astype(full_type)
+    cot_all = cot_all.reshape(SPAN, width)
+    columns = columns.reshape(width, 2 * WIDTH)
+    blocks = gates.reshape(WIDTH, 2 * WIDTH)
+    out_rows = out_rows.reshape(WIDTH, width)
+    mlp_gate = mlp_gate.reshape(width, units * 4)
+    mlp_up = mlp_up.reshape(width, units * 4)
+    down = down.reshape(units * 4, width)
+
+    normed_two_all = normed_two_all.reshape(SPAN, width)
+    gate_part = plain_product(normed_two_all, mlp_gate)
+    up_part = plain_product(normed_two_all, mlp_up)
+    activated = mlp_apply(gate_part, up_part).astype(low_type)
+    out_partial = plain_product(activated, down).astype(low_type).reshape(PARTS, TOK, width)
+    grad_activated = cols_product(cot_all, down)
+    grad_down = rows_product(activated, cot_all).astype(low_type)
+    unused, mlp_pull = jax.vjp(mlp_apply, gate_part, up_part)
+    grad_gate_part, grad_up_part = mlp_pull(grad_activated)
+    grad_gate_part = grad_gate_part.astype(low_type)
+    grad_up_part = grad_up_part.astype(low_type)
+    grad_two = cols_product(grad_gate_part, mlp_gate) + cols_product(grad_up_part, mlp_up)
+    grad_two = grad_two.astype(low_type).reshape(PARTS, TOK, width)
+    grad_mlp_gate = rows_product(normed_two_all, grad_gate_part).astype(low_type)
+    grad_mlp_up = rows_product(normed_two_all, grad_up_part).astype(low_type)
+    grad_two, out_arrived = exchange(
+        "sum_two",
+        4,
+        [
+            (Peers(by_part), grad_two, (PARTS, TOK, width)),
+            (Peers(by_part), out_partial, (PARTS, TOK, width)),
+        ],
+    )
+    output = (after_mixer + jnp.sum(out_arrived.astype(full_type), axis=0)).astype(low_type)
+    grad_two = jnp.sum(grad_two.astype(full_type), axis=0)
+    unused, norm_pull = jax.vjp(norm_scale, after_mixer, gain_two)
+    grad_values, grad_gain_two = norm_pull(grad_two)
+    grad_after = cotangent[0].astype(full_type) + grad_values
+
+    grad_mixed = grad_after.astype(low_type)
+    (mixed_all,) = exchange("gather_mixed", 5, [(Peers(whole), grad_mixed, (PARTS, TOK, width))])
+    mixed_all = mixed_all.reshape(SPAN, width)
+    grad_branch = cols_product(mixed_all, out_rows)
+    grad_out = rows_product(mixed, mixed_all).astype(low_type)
+    grad_pre, grad_blocks, grad_states, grad_aux = in_vmem(
+        mixer_backward_kernel,
+        "mixer_backward",
+        (pre, states_all, aux, blocks, conv_out, logits, hidden, grad_branch),
+        [
+            ((SPAN, 2 * WIDTH), low_type),
+            ((WIDTH, 2 * WIDTH), full_type),
+            ((PARTS, 8, WIDTH), full_type),
+            ((8, WIDTH), full_type),
+        ],
+        [
+            ((WIDTH // 128, SPAN, 128), full_type),
+            ((WIDTH // 128, SPAN, 128), full_type),
+            ((TOK + 16, WIDTH), full_type),
+        ],
+    )
+    grad_one = cols_product(grad_pre, columns).astype(low_type).reshape(PARTS, TOK, width)
+    grad_columns = rows_product(normed_all, grad_pre).astype(low_type)
+    grad_one, grad_states = exchange(
+        "sum_one",
+        6,
+        [
+            (Peers(by_part), grad_one, (PARTS, TOK, width)),
+            (Peers(by_part), grad_states, (PARTS, 8, WIDTH)),
+        ],
+    )
+    grad_one = jnp.sum(grad_one.astype(full_type), axis=0)
+    unused, norm_pull = jax.vjp(norm_scale, values, gain_one)
+    grad_values, grad_gain_one = norm_pull(grad_one)
+    grad_tokens = (grad_after + grad_values).astype(low_type)
+    grad_states = grad_states.transpose(1, 0, 2).reshape(8, PARTS * WIDTH)
+    grad_states = from_lanes(grad_states) * keep
+
+    gains = jnp.stack([grad_gain_one.reshape(32, rows), grad_gain_two.reshape(32, rows)], axis=1)
+    gains = jnp.pad(gains, ((0, 0), (0, 6), (0, 128 - rows)))
+    own_aux = grad_aux.reshape(8, 4, LANES).transpose(1, 0, 2)[:, 0:5]
+    own_aux = jnp.pad(own_aux, ((0, 0), (2, 1), (0, 128 - LANES)))
+    own_aux = lax.dynamic_update_slice(jnp.zeros_like(gains), own_aux, (4 * part, 0, 0))
+    small_terms = (gains + own_aux).reshape(COLUMNS, 2, 4, 8, 128)
+    wide_terms = [
+        array.reshape(COLUMNS, 2, 4, rows, -1) for array in (grad_columns, grad_mlp_gate, grad_mlp_up)
+    ]
+    row_terms = [
+        from_dense(grad_blocks).astype(low_type).reshape(2, 2, LANES, WIDTH),
+        grad_out.reshape(2, 2, LANES, width),
+        grad_down.reshape(2, 2, units, width),
+    ]
+    terms = [small_terms] + wide_terms + row_terms
+    swapped = exchange(
+        "swap_cores",
+        7,
+        [(Swap(), term, term.shape[:1] + term.shape[2:]) for term in terms],
+    )
+    terms = [
+        (
+            lax.dynamic_index_in_dim(term, core, 1, keepdims=False).astype(full_type)
+            + other.astype(full_type)
+        ).astype(term.dtype)
+        for term, other in zip(terms, swapped)
+    ]
+    arrived = exchange(
+        "return_weights",
+        8,
+        [(Owners(), term, (2, PARTS) + term.shape[2:]) for term in terms[:4]]
+        + [(RowOwners(), term, term.shape) for term in terms[4:]],
+    )
+    small_sum = jnp.sum(arrived[0], axis=(0, 1))
+    column_sum, gate_sum, up_sum, block_sum, out_sum, down_sum = (
+        jnp.sum(term.astype(full_type), axis=0) for term in arrived[1:]
+    )
+    column_sum = column_sum.transpose(1, 0, 2)
+    block_sum = block_sum[:CHUNK]
+    return (
+        output[None],
+        grad_tokens[None],
+        grad_states[None, 5:8],
+        grad_states[0:1],
+        small_sum[0, :rows],
+        from_lanes(column_sum[:, :, :WIDTH]).reshape(rows, -1),
+        from_lanes(column_sum[:, :, WIDTH:]).reshape(rows, -1),
+        small_sum[2:6, :CHUNK],
+        small_sum[6, :CHUNK],
+        from_lanes(block_sum[:, : 2 * LANES]),
+        from_lanes(block_sum[:, 2 * LANES :]),
+        out_sum[:CHUNK],
+        small_sum[1, :rows],
+        gate_sum.transpose(1, 0, 2).reshape(rows, -1),
+        up_sum.transpose(1, 0, 2).reshape(rows, -1),
+        down_sum,
+    )
+
+
 def solution(mesh):
+    sizes = (mesh.shape["wide"], mesh.shape["narrow"])
     return jax.shard_map(
-        shards,
+        halves if sizes == (2 * COLUMNS, 2 * LOWS) else shards,
         mesh=mesh,
         in_specs=(
             P(("wide", "narrow"), None, None),

time: 4170 us -> 825 us (0.20)
  waiting for transfers between devices: 3440 us -> 0 us
  Pallas kernels: 0 us -> 681 us
  blocking collectives: 308 us -> 0 us
  matrix products: 240 us -> 67.7 us
  local copies, waits for them, and re-layouts: 93.8 us -> 26.1 us
    reduce_scatter x8 -> x0, waiting for transfers between devices: 3080 us -> none  [the longest x1 496 us: shards(): lax.psum_scatter(mixer_total[1], ('wide', 'narrow'), scatter_dimension=0,...]
    pallas_call x0 -> x7, Pallas kernels: none -> 681 us  [the longest x5 419 us: exchange(): pl.pallas_call(functools.partial(exchange_kernel, plan), out_shape=[jax.S...]
    all_gather x6 -> x0, waiting for transfers between devices: 358 us -> none  [the longest x1 142 us: shards(): lax.all_gather(mlp_down, ('wide', 'narrow'), axis=0, tiled=True)]
    all_gather x3 -> x0, blocking collectives: 265 us -> none  [the longest x1 100 us: shards(): lax.all_gather(gate_input, ('wide', 'narrow'), axis=0, tiled=True)]
    dot_general x6 -> x5, matrix products: 91.9 us -> 25.7 us  [rows_product(): lax.dot_general(left_side, right_side, contract_rows, preferred_element_t...]
    dot_general x6 -> x5, matrix products: 71.9 us -> 27.9 us  [cols_product(): lax.dot_general(left_side, right_side, contract_cols, preferred_element_t...]
    dot_general x6 -> x3, matrix products: 57.7 us -> 14 us  [plain_product(): return jnp.dot(left_side, right_side, preferred_element_type=jnp.float32)]
    unnamed x1 -> x0, blocking collectives: 43.1 us -> none
  transfers between devices with their start and end apart: 15 -> 0, of which waited for: 11 -> 0; matrix products, arithmetic and copies ran while one was open for 6% -> 0% of each run, Pallas kernels for 0% -> 0%
where the time goes in v1:
time: 825 us; the launch traced here: 817 us
  Pallas kernels  681 us (83%)
  matrix products  67.7 us (8%)
  other arithmetic  40.4 us (5%)
  local copies, waits for them, and re-layouts  26.1 us (3%)
    pallas_call x5, Pallas kernels, exchange(): pl.pallas_call(functools.partial(exchange_kernel, plan), out_shape=[jax.S...  419 us
    pallas_call x1, Pallas kernels, forward_mixer(): pl.pallas_call(forward_kernel, out_shape=[jax.ShapeDtypeStruct(shape, kin...  242 us
    dot_general x5, matrix products, cols_product(): lax.dot_general(left_side, right_side, contract_cols, preferred_element_t...  27.9 us
    dot_general x5, matrix products, rows_product(): lax.dot_general(left_side, right_side, contract_rows, preferred_element_t...  25.7 us
    pallas_call x1, Pallas kernels, in_vmem(): pl.pallas_call(kernel, out_shape=[jax.ShapeDtypeStruct(shape, kind) for s...  20 us

profile of v1, /device:TPU:0, one launch (start us, length us, event | category | flops | bytes accessed | tf_op | source)
XLA Modules:
  0.0 817.4 jit_solution(7528839268087204400)
XLA Ops:
  1.4 1.3 fusion.15
  6.5 0.9 reshape.211
  7.4 0.9 reshape.212
  11.3 1.3 reshape.209
  13.0 1.3 reshape.210
  14.9 0.9 pad_maximum_fusion.columns
  15.9 242.3 %forward_mixer.1 = (bf16[1024,2048]{1,0:T(8,128)(2,1)}, f32[8,8,384]{2,1,0:T(8,128)}, bf16[4,2,4,64,768]{4,3,2,1,0:T(8,128)(2,1)}, bf16[2,2,96,768]{3,2,1,0:T(8,...) custom-call(bf16[128,2048]{1,0:T(8,128)(2,1)} %bitcast.131, ...), custom_call_target="tpu_custom_call" | custom-call | tf_op jit(solution)/shard_map/forward_mixer/pallas_call | solution.py:1158
  258.2 1.4 multiply_reduce_fusion.2
  260.4 6.8 fusion.39
  267.3 3.4 fusion.40
  270.7 5.6 multiply_convert_fusion
  276.3 4.9 convolution_convert_fusion.2
  281.2 5.0 convolution_convert_fusion.1
  286.2 5.0 convolution_convert_fusion.4
  291.2 5.2 convolution_convert_fusion.3
  296.4 3.4 fusion.41
  299.9 5.0 add_convert_fusion
  304.9 117.5 %sum_two.1 = (bf16[8,128,2048]{2,1,0:T(8,128)(2,1)}, bf16[8,128,2048]{2,1,0:T(8,128)(2,1)}) custom-call(bf16[8,128,2048]{2,1,0:T(8,128)(2,1)} %bitcast.149, bf16[8,128,2048]{2,1,0:T(8,128)(2,1)} %bitcast.148), custom_call_target="tpu_custom_call" | custom-call | tf_op jit(solution)/shard_map/sum_two/pallas_call | solution.py:817
  422.5 4.2 convert_reduce_fusion.2
  428.2 1.2 fusion.34.refs_0_
  429.4 60.8 %gather_mixed.1 = bf16[8,128,2048]{2,1,0:T(8,128)(2,1)} custom-call(bf16[128,2048]{1,0:T(8,128)(2,1)} %fusion.34.refs_0_), custom_call_target="tpu_custom_call" | custom-call | tf_op jit(solution)/shard_map/gather_mixed/pallas_call | solution.py:817
  490.2 6.2 fusion.42.grad_branch
  496.4 20.0 %mixer_backward.1 = (bf16[1024,768]{1,0:T(8,128)(2,1)}, f32[384,768]{1,0:T(8,128)}, f32[8,8,384]{2,1,0:T(8,128)}, f32[8,384]{1,0:T(8,128)}) custom-call(f32[1024,768]{1,0:T(8,128)} %get-tuple-element.65.pre, f32[8,8,384]{2,1,0:T(8,128)} %get-tuple-element.66.states, f32[8,384]{1,0:T(8,128)} %get-tuple-element.67.aux, bf16[384,768]{1,0:T(8,128)(2,1)} %bitcast.159, ...), custom_call_target="tpu_custom_call" | custom-call | tf_op jit(solution)/shard_map/mixer_backward/pallas_call | solution.py:1264
  516.4 5.5 convolution_convert_fusion.6
  522.0 5.1 convolution_convert_fusion.5
  527.2 1.5 convert.18
  529.7 6.4 convolution_convert_fusion
  536.1 62.6 %sum_one.1 = (bf16[8,128,2048]{2,1,0:T(8,128)(2,1)}, f32[8,8,384]{2,1,0:T(8,128)}) custom-call(bf16[8,128,2048]{2,1,0:T(8,128)(2,1)} %bitcast.150, f32[8,8,384]{2,1,0:T(8,128)} %get-tuple-element.75.refs_1_), custom_call_target="tpu_custom_call" | custom-call | tf_op jit(solution)/shard_map/sum_one/pallas_call | solution.py:817
  598.8 3.1 convert_reduce_fusion
  602.4 1.5 fusion.20
  606.2 14.3 %swap_cores.1 = (f32[4,4,8,128]{3,2,1,0:T(8,128)}, bf16[4,4,64,768]{3,2,1,0:T(8,128)(2,1)}, bf16[4,4,64,768]{3,2,1,0:T(8,128)(2,1)}, bf16[4,4,64,768]{3,2,1,0:T(...) custom-call(f32[4,2,4,8,128]{4,3,2,1,0:T(8,128)} %bitcast.157, ...), custom_call_target="tpu_custom_call" | custom-call | tf_op jit(solution)/shard_map/swap_cores/pallas_call | solution.py:817
  620.6 3.3 fusion.7.refs_6_
  623.9 1.2 fusion.11.refs_5_
  625.1 1.8 fusion.25.refs_4_
  626.9 1.6 fusion.8.refs_3_
  628.5 1.6 fusion.9.refs_2_
  631.4 1.6 fusion.10.refs_1_
  633.7 163.3 %return_weights.1 = (f32[2,8,8,128]{3,2,1,0:T(8,128)}, bf16[2,8,64,768]{3,2,1,0:T(8,128)(2,1)}, bf16[2,8,64,768]{3,2,1,0:T(8,128)(2,1)}, bf16[2,8,64,768]{3,2,1,...) custom-call(f32[4,4,8,128]{3,2,1,0:T(8,128)} %bitcast_add_fusion.refs_0_, ...), custom_call_target="tpu_custom_call" | custom-call | tf_op jit(solution)/shard_map/return_weights/pallas_call | solution.py:817
  797.1 1.0 reduce_sum.169
  799.7 0.9 convert_reduce_fusion.8
  802.5 1.3 convert_reduce_fusion.7
  803.8 0.9 slice.120
  806.0 2.0 reshape_reshape.23
  808.9 2.0 reshape_reshape.22
  810.9 2.0 convert_reduce_fusion.5
  812.9 1.3 copy.100
  814.4 1.3 copy.101
  815.7 1.4 convert_reduce_fusion.3
  (136 shorter events, 21.9 us)
Async XLA Ops:
  0.6 9.8 %copy-start.22 = (bf16[88,2048]{1,0:T(8,128)(2,1)S(1)}, bf16[88,2048]{1,0:T(8,128)(2,1)}, u32[]{:S(2)}) copy-start(bf16[88,2048]{1,0:T(8,128)(2,1)} %param.28) | copy-start | bytes 1081348
  0.7 10.6 %copy-start.20 = (bf16[64,2816]{1,0:T(8,128)(2,1)S(1)}, bf16[64,2816]{1,0:T(8,128)(2,1)}, u32[]{:S(2)}) copy-start(bf16[64,2816]{1,0:T(8,128)(2,1)} %param.22) | copy-start | bytes 1081348
  1.4 11.6 %copy-start.21 = (bf16[64,2816]{1,0:T(8,128)(2,1)S(1)}, bf16[64,2816]{1,0:T(8,128)(2,1)}, u32[]{:S(2)}) copy-start(bf16[64,2816]{1,0:T(8,128)(2,1)} %param.23) | copy-start | bytes 1081348
  5.5 8.8 %copy-start.25 = (bf16[16,384]{1,0:T(8,128)(2,1)}, bf16[16,384]{1,0:T(8,128)(2,1)S(1)}, u32[]{:S(2)}) copy-start(bf16[16,384]{1,0:T(8,128)(2,1)S(1)} %dynamic_update_slice.10.small) | copy-start | bytes 36868
  260.4 6.9 copy-start.28
  260.4 6.9 copy-start.32
  267.2 3.4 copy-start.31
  270.7 5.6 copy-start.29
  276.3 4.9 copy-start.33
  422.5 4.2 copy-start.7
  426.6 1.2 copy-start
  426.6 1.6 copy-start.6
  516.4 5.6 copy-start.27
  516.4 5.6 copy-start.34
  522.0 5.1 copy-start.26
  527.2 2.5 copy-start.30
  598.7 3.2 copy-start.23
  598.7 3.2 copy-start.1
  598.8 3.6 copy-start.8
  605.6 0.7 copy-start.17
  606.2 14.3 %copy-start.4 = (bf16[768,2048]{1,0:T(8,128)(2,1)S(1)}, bf16[768,2048]{1,0:T(8,128)(2,1)}, u32[]{:S(2)}) copy-start(bf16[768,2048]{1,0:T(8,128)(2,1)} %convolution_convert_fusion.2) | copy-start | bytes 9437188
  620.5 3.4 copy-start.9
  620.5 3.4 copy-start.19
  620.6 4.5 copy-start.10
  620.6 6.3 copy-start.3
  620.6 6.3 copy-start.13
  625.1 3.4 copy-start.2
  625.1 3.4 copy-start.12
  628.5 2.5 copy-start.5
  628.5 2.9 copy-start.11
  630.2 2.9 copy-start.18
  630.2 2.9 copy-start.24
  797.1 7.6 copy-start.16
  810.9 3.2 copy-start.15
  814.1 1.6 copy-start.14

commit v2 on v1

--- a/solution.py
+++ b/solution.py
@@ -418,7 +418,7 @@
 WIDTH = 4 * LANES
 SPAN = PARTS * TOK
 MESH = pl.DeviceIdType.MESH
-VMEM_BYTES = 60 * 1024 * 1024
+VMEM_BYTES = 63 * 1024 * 1024
 low_type = jnp.bfloat16
 full_type = jnp.float32
 
@@ -599,7 +599,7 @@
         for shift in itertools.product(range(2), repeat=4):
             column, low, half = place.shifted(*shift)
             z = half * 2 + low
-            block = source.at[column, z]
+            block = source.at[column, place.core, z]
             if any(shift):
                 copy = remote(
                     block, slot, sems.at[0], sems.at[1], (column * 2 + place.core, z)
@@ -623,7 +623,7 @@
         self.copies = []
         slot = target.at[place.half]
         for half in range(2):
-            block = source.at[half]
+            block = source.at[half, place.core]
             copy = remote(
                 block,
                 slot,
@@ -801,30 +801,6 @@
     return source.at[:, pl.ds(pl.multiple_of(part * width, 128), width)]
 
 
-def exchange_kernel(plan, *refs):
-    count = len(plan)
-    sources, targets, sems = refs[:count], refs[count : 2 * count], refs[2 * count]
-    place = Place()
-    greet_all(place)
-    for step in ("start", "relay", "finish"):
-        for index, move in enumerate(plan):
-            getattr(move, step)(place, sources[index], targets[index], sems.at[index])
-
-
-def exchange(name, identity, moves):
-    plan = [move for move, array, shape in moves]
-    hbm = pl.BlockSpec(memory_space=pl.ANY)
-    return pl.pallas_call(
-        functools.partial(exchange_kernel, plan),
-        out_shape=[jax.ShapeDtypeStruct(shape, array.dtype) for move, array, shape in moves],
-        in_specs=[hbm] * len(moves),
-        out_specs=[hbm] * len(moves),
-        scratch_shapes=[pltpu.SemaphoreType.DMA((len(moves), 4))],
-        compiler_params=pltpu.CompilerParams(collective_id=identity, has_side_effects=True),
-        name=name,
-    )(*[array for move, array, shape in moves])
-
-
 def row_block(row):
     return pl.ds(pl.multiple_of(row * TOK, TOK), TOK)
 
@@ -884,7 +860,36 @@
     return values * scale * gain
 
 
-def forward_kernel(
+def whole_block(place, row):
+    return (row // 4, row // 2 % 2, row % 2)
+
+
+def add_swapped(array, landing, core):
+    rows, columns = array.shape[-2:]
+    inner = array.shape[2] if len(array.shape) == 5 else 1
+    outer = array.shape[0]
+    chunk = 32 if columns > 1024 and rows % 32 == 0 else 16 if rows % 16 == 0 else 8
+
+    @pl.loop(0, outer * inner * (rows // chunk))
+    def _(step):
+        part = pl.ds(pl.multiple_of(step % (rows // chunk) * chunk, chunk), chunk)
+        first = step // (rows // chunk)
+        if len(array.shape) == 5:
+            here, there = (first // inner, core, first % inner, part), (first // inner, first % inner, part)
+        else:
+            here, there = (first, core, part), (first, part)
+        total = array[here].astype(full_type) + landing[there].astype(full_type)
+        array[here] = total.astype(array.dtype)
+
+
+def norm_back(values, gain, grad):
+    scale = lax.rsqrt(jnp.mean(values * values, axis=1, keepdims=True) + epsilon)
+    inner = grad * gain
+    along = jnp.mean(inner * values, axis=1, keepdims=True)
+    return (scale * inner - values * (scale * scale * scale * along), grad * values * scale)
+
+
+def block_kernel(
     tokens,
     small,
     states,
@@ -895,55 +900,74 @@
     mlp_up,
     mlp_down,
     cotangent,
-    normed_out,
-    states_out,
-    columns_out,
-    gates_out,
-    rows_out,
-    gate_out,
-    up_out,
-    down_out,
-    cot_out,
-    pre_out,
-    conv_out,
-    logits_out,
-    hidden_out,
-    mixed_out,
-    after_out,
-    two_out,
-    aux_out,
-    gains_out,
-    tokens_all,
+    output,
+    grad_tokens,
+    states_back,
+    small_back,
+    columns_back,
+    gate_back,
+    up_back,
+    blocks_back,
+    rows_back,
+    down_back,
+    normed_kept,
+    cube_one,
+    cube_two,
+    cube_three,
+    blocks,
+    landing_one,
+    landing_two,
+    landing_three,
     small_all,
     states_all,
     columns_all,
     gates_all,
     rows_all,
-    normed,
+    gate_all,
+    up_all,
+    down_all,
     pre,
     conv,
-    logits,
     hidden,
     mixed,
     decays,
-    inputs,
+    carries,
     padded,
-    blocks,
-    landing_one,
-    landing_two,
-    landing_three,
     after,
-    two_all,
+    grad,
+    summed,
     aux,
     gains,
+    grad_gains,
+    grad_aux,
+    active,
+    grad_gate,
+    grad_up,
+    down_landing,
+    grad_pre,
+    grad_blocks,
+    blocks_low,
+    blocks_landing,
+    grad_states,
+    small_terms,
+    small_landing,
     sems,
+    free,
 ):
     place = Place()
     semaphores = Semaphores(sems)
     local = Local(semaphores)
+    width = tokens.shape[1]
+    hidden_units = gate_all.shape[-1]
+    tokens_all = cube_one
+    normed = cube_two
+    two_all = cube_three
 
     def move(plan, source, target):
         return Move(place, plan, source, target, semaphores)
+
+    def whole_matrix(array):
+        return array[...].reshape(-1, array.shape[-1])
 
     own_tokens = tokens_all.at[place.own]
     load = pltpu.make_async_copy(tokens, own_tokens, semaphores.take(1).at[0])
@@ -962,23 +986,22 @@
     gates_move.start()
     rows_move = move(RowSpread(), out_rows, rows_all)
     rows_move.start()
-    local.start(cotangent, cot_out.at[place.own])
     tokens_gather.step(1)
     small_move.relay()
     tokens_gather.step(2)
     late = [
-        move(Spread(by_columns), mlp_gate, gate_out),
-        move(Spread(by_columns), mlp_up, up_out),
-        move(RowSpread(), mlp_down, down_out),
+        move(Spread(by_columns), mlp_gate, gate_all),
+        move(Spread(by_columns), mlp_up, up_all),
+        move(RowSpread(), mlp_down, down_all),
     ]
     for item in late:
         item.start()
     small_move.finish()
     for tap in range(5):
         aux[tap : tap + 1, :] = placed_sum(small_all, place, tap)
-    decay = aux[4:5, :]
-    aux[4:5, :] = jnp.maximum(-decay, 0.0) + jnp.log1p(jnp.exp(-jnp.abs(decay)))
-    aux[5:6, :] = jax.nn.sigmoid(-decay)
+    decay_row = aux[4:5, :]
+    aux[4:5, :] = jnp.maximum(-decay_row, 0.0) + jnp.log1p(jnp.exp(-jnp.abs(decay_row)))
+    aux[5:6, :] = jax.nn.sigmoid(-decay_row)
     aux[6:8, :] = jnp.zeros((2, WIDTH), full_type)
     gains[0:1, :] = placed_gain(small_all, 5)
     gains[1:2, :] = placed_gain(small_all, 6)
@@ -986,38 +1009,35 @@
 
     @pl.loop(0, SPAN // 32)
     def _(step):
-        part, piece = step // 4, step % 4
-        rows = pl.ds(pl.multiple_of(piece * 32, 32), 32)
-        values = tokens_all[part // 4, part // 2 % 2, part % 2, rows, :].astype(full_type)
-        normed[pl.ds(pl.multiple_of(step * 32, 32), 32), :] = scaled_norm(
-            values, gains[0:1, :]
-        ).astype(low_type)
-
-    local.start(normed, normed_out)
-    local.start(aux, aux_out)
-    local.start(gains, gains_out)
+        rows = pl.ds(pl.multiple_of(step % 4 * 32, 32), 32)
+        index = whole_block(place, step // 4) + (rows,)
+        normed[index] = scaled_norm(tokens_all[index].astype(full_type), gains[0:1, :]).astype(
+            low_type
+        )
+
+    keep_normed = local.start(normed, normed_kept)
     columns_move.relay()
     gates_move.relay()
     rows_move.relay()
     columns_move.finish()
-    local.start(columns_all, columns_out)
-
-    @pl.loop(0, SPAN // 256)
+
+    @pl.loop(0, 4)
     def _(step):
         rows = pl.ds(pl.multiple_of(step * 256, 256), 256)
         pre[rows, :] = jnp.dot(
-            normed[rows, :],
-            columns_all[...].reshape(-1, 2 * WIDTH),
+            normed[step // 2, step % 2].reshape(256, width),
+            whole_matrix(columns_all),
             preferred_element_type=full_type,
         )
 
-    local.start(pre, pre_out)
     gates_move.finish()
     states_move.finish()
-    local.start(gates_all, gates_out)
-    local.start(states_all, states_out)
     taps = taps_of(aux)
-    soft = aux[4:5, :]
+    soft, slope = aux[4:5, :], aux[5:6, :]
+
+    def gate_logits(low):
+        both = jnp.dot(low, whole_matrix(gates_all), preferred_element_type=full_type)
+        return (jax.nn.sigmoid(both[:, 0:WIDTH]), jax.nn.sigmoid(both[:, WIDTH:]))
 
     @pl.loop(0, PARTS)
     def _(row):
@@ -1029,22 +1049,16 @@
             total = total + taps[tap] * padded[8 - tap : 8 - tap + TOK, :]
         low = total.astype(low_type)
         conv[rows, :] = low
-        both = jnp.dot(
-            low, gates_all[...].reshape(WIDTH, 2 * WIDTH), preferred_element_type=full_type
-        )
-        logits[rows, :] = both
-        log_decay = -8.0 * jax.nn.sigmoid(both[:, 0:WIDTH]) * soft
+        recur, gate = gate_logits(low)
+        log_decay = -8.0 * recur * soft
         scale = jnp.sqrt(-small_expm1(2.0 * log_decay))
-        put(inputs, rows, scale * jax.nn.sigmoid(both[:, WIDTH:]) * low.astype(full_type))
+        put(carries, rows, scale * gate * low.astype(full_type))
         put(decays, rows, jnp.exp(log_decay))
-
-    local.start(conv, conv_out)
-    local.start(logits, logits_out)
 
     def advance(time, carried):
         across = pl.ds(time, PARTS, stride=TOK)
         carried = [
-            decays[piece, across, :] * before + inputs[piece, across, :]
+            decays[piece, across, :] * before + carries[piece, across, :]
             for piece, before in enumerate(carried)
         ]
         for piece, now in enumerate(carried):
@@ -1054,9 +1068,7 @@
     initial = states_all[:, 0, :]
     initial = [initial[:, piece * 128 : (piece + 1) * 128] for piece in range(WIDTH // 128)]
     lax.fori_loop(0, TOK, advance, initial, unroll=8)
-    local.start(hidden, hidden_out)
     rows_move.finish()
-    local.start(rows_all, rows_out)
 
     @pl.loop(0, PARTS)
     def _(row):
@@ -1064,12 +1076,12 @@
         gated, _ = gelu_parts(pre[rows, WIDTH:])
         low = (take(hidden, rows) * gated).astype(low_type)
         mixed[rows, :] = low
-        blocks[row // 4, row // 2 % 2, row % 2] = jnp.dot(
-            low, rows_all[...].reshape(WIDTH, -1), preferred_element_type=full_type
+        blocks[whole_block(place, row)] = jnp.dot(
+            low, whole_matrix(rows_all), preferred_element_type=full_type
         ).astype(low_type)
 
-    local.start(mixed, mixed_out)
-    mixer_sum = CubeSum(place, blocks, (landing_one, landing_two, landing_three), semaphores)
+    landings = (landing_one, landing_two, landing_three)
+    mixer_sum = CubeSum(place, blocks, landings, semaphores)
     mixer_sum.start()
     mixer_sum.step(0)
     mixer_sum.step(1)
@@ -1082,123 +1094,164 @@
         after[rows, :] = total
         two_all[place.own + (rows,)] = scaled_norm(total, gains[1:2, :]).astype(low_type)
 
-    local.start(after, after_out)
     two_gather = CubeGather(place, two_all, semaphores)
     two_gather.step(0)
-    cot_gather = CubeGather(place, cot_out, semaphores)
-    local.copies[0].wait()
+    cot_all = cube_one
+    load_cot = pltpu.make_async_copy(
+        cotangent, cot_all.at[place.own], semaphores.take(1).at[0]
+    )
+    load_cot.start()
+    cot_gather = CubeGather(place, cot_all, semaphores)
+    load_cot.wait()
     cot_gather.step(0)
     two_gather.step(1)
     cot_gather.step(1)
     two_gather.step(2)
     cot_gather.step(2)
     two_gather.finish()
-    local.start(two_all, two_out)
     mixer_sum.finish()
     for item in late:
         item.relay()
     cot_gather.finish()
+    keep_normed.wait()
     for item in late:
         item.finish()
-    states_move_done = local.copies[1:]
-    for copy in states_move_done:
-        copy.wait()
-
-
-def forward_mixer(arrays, rows, width, units):
-    hbm = pl.BlockSpec(memory_space=pl.ANY)
-    lanes = (WIDTH // 128, SPAN, 128)
-    cube = (2, 2, 2, TOK, width)
-    spread = (COLUMNS, 2, 4, rows)
-    outputs = [
-        ((SPAN, width), low_type),
-        ((PARTS, 8, WIDTH), full_type),
-        (spread + (2 * WIDTH,), low_type),
-        ((2, 2, LANES, 2 * WIDTH), low_type),
-        ((2, 2, LANES, width), low_type),
-        (spread + (4 * units,), low_type),
-        (spread + (4 * units,), low_type),
-        ((2, 2, units, width), low_type),
-        (cube, low_type),
-        ((SPAN, 2 * WIDTH), full_type),
-        ((SPAN, WIDTH), low_type),
-        ((SPAN, 2 * WIDTH), full_type),
-        (lanes, full_type),
-        ((SPAN, WIDTH), low_type),
-        ((TOK, width), full_type),
-        (cube, low_type),
-        ((8, WIDTH), full_type),
-        ((2, width), full_type),
+
+    out_blocks = cube_two
+
+    @pl.loop(0, 4)
+    def _(step):
+        at = (step // 2, step % 2)
+        normed_two = two_all[at].reshape(256, width)
+        cot = cot_all[at].reshape(256, width)
+        gate_part = jnp.dot(normed_two, whole_matrix(gate_all), preferred_element_type=full_type)
+        up_part = jnp.dot(normed_two, whole_matrix(up_all), preferred_element_type=full_type)
+        gated, bend = gelu_parts(gate_part)
+        low = (gated * up_part).astype(low_type)
+        active[step] = low.reshape(4, 64, hidden_units)
+        grad_active = cols_product(cot, whole_matrix(down_all))
+        to_gate = (grad_active * up_part * bend).astype(low_type)
+        to_up = (grad_active * gated).astype(low_type)
+        grad_gate[step] = to_gate.reshape(4, 64, hidden_units)
+        grad_up[step] = to_up.reshape(4, 64, hidden_units)
+        for piece in range(4):
+            cut = pl.ds(piece * (width // 4), width // 4)
+            part = down_all[:, :, :, cut].reshape(hidden_units, width // 4)
+            out_blocks[at + (slice(None), slice(None), cut)] = (
+                jnp.dot(low, part, preferred_element_type=full_type)
+                .astype(low_type)
+                .reshape(2, TOK, width // 4)
+            )
+            back = cols_product(to_gate, whole_matrix(gate_all.at[piece])) + cols_product(
+                to_up, whole_matrix(up_all.at[piece])
+            )
+            blocks[at + (slice(None), slice(None), cut)] = back.astype(low_type).reshape(
+                2, TOK, width // 4
+            )
+
+    two_sum = CubeSum(place, blocks, landings, semaphores)
+    two_sum.start()
+
+    @pl.loop(0, 8)
+    def _(step):
+        cut = pl.ds(pl.multiple_of(step * 256, 256), 256)
+        side = two_all[:, :, :, :, cut].reshape(SPAN, 256)
+        for terms, sums in ((grad_gate, gate_all), (grad_up, up_all)):
+            sums[step // 2, step % 2] = (
+                rows_product(side, whole_matrix(terms))
+                .astype(low_type)
+                .reshape(4, 64, hidden_units)
+            )
+
+    two_sum.step(0)
+
+    @pl.loop(0, 4)
+    def _(step):
+        cut = pl.ds(pl.multiple_of(step * 512, 512), 512)
+        down_all[:, :, :, cut] = (
+            rows_product(whole_matrix(active), cot_all[:, :, :, :, cut].reshape(SPAN, 512))
+            .astype(low_type)
+            .reshape(2, 2, hidden_units // 4, 512)
+        )
+
+    pl.semaphore_signal(
+        free.at[0], inc=1, device_id=place.sibling(), device_id_type=MESH
+    )
+    two_sum.step(1)
+    pl.semaphore_wait(free.at[0], 1)
+    mlp_swaps = [
+        move(Swap(), gate_all, active),
+        move(Swap(), up_all, grad_gate),
+        move(Swap(), down_all, down_landing),
     ]
-    scratch = [
-        (cube, low_type),
-        ((COLUMNS, 2, 4, 16, WIDTH), low_type),
-        ((PARTS, 8, WIDTH), full_type),
-        (spread + (2 * WIDTH,), low_type),
-        ((2, 2, LANES, 2 * WIDTH), low_type),
-        ((2, 2, LANES, width), low_type),
-        ((SPAN, width), low_type),
-        ((SPAN, 2 * WIDTH), full_type),
-        ((SPAN, WIDTH), low_type),
-        ((SPAN, 2 * WIDTH), full_type),
-        (lanes, full_type),
-        ((SPAN, WIDTH), low_type),
-        (lanes, full_type),
-        (lanes, full_type),
-        ((TOK + 8, WIDTH), full_type),
-        (cube, low_type),
-        ((2, 2, TOK, width), low_type),
-        ((2, TOK, width), low_type),
-        ((TOK, width), low_type),
-        ((TOK, width), full_type),
-        (cube, low_type),
-        ((8, WIDTH), full_type),
-        ((2, width), full_type),
+    for item in mlp_swaps:
+        item.start()
+    two_sum.step(2, grad)
+    grad_gains[...] = jnp.zeros_like(grad_gains)
+
+    @pl.loop(0, TOK // 32)
+    def _(step):
+        rows = pl.ds(pl.multiple_of(step * 32, 32), 32)
+        back, by_gain = norm_back(after[rows, :], gains[1:2, :], grad[rows, :])
+        total = cot_all[place.own + (rows,)].astype(full_type) + back
+        grad[rows, :] = total
+        cot_all[place.own + (rows,)] = total.astype(low_type)
+        grad_gains[1:2, :] += jnp.sum(by_gain, axis=0, keepdims=True)
+
+    mixed_all = cube_one
+    mixed_gather = CubeGather(place, mixed_all, semaphores)
+    mixed_gather.step(0)
+    mlp_swaps[0].finish()
+    add_swapped(gate_all, active, place.core)
+    mixed_gather.step(1)
+    mlp_swaps[1].finish()
+    add_swapped(up_all, grad_gate, place.core)
+    mixed_gather.step(2)
+    mlp_swaps[2].finish()
+    add_swapped(down_all, down_landing, place.core)
+    pl.semaphore_signal(
+        free.at[1], inc=1, device_id=place.sibling(), device_id_type=MESH
+    )
+    returns = [
+        move(Owners(), gate_all, gate_back),
+        move(Owners(), up_all, up_back),
+        move(RowOwners(), down_all, down_back),
     ]
-    return pl.pallas_call(
-        forward_kernel,
-        out_shape=[jax.ShapeDtypeStruct(shape, kind) for shape, kind in outputs],
-        in_specs=[hbm] * len(arrays),
-        out_specs=[hbm] * len(outputs),
-        scratch_shapes=[pltpu.VMEM(shape, kind) for shape, kind in scratch]
-        + [pltpu.SemaphoreType.DMA((192,))],
-        compiler_params=pltpu.CompilerParams(
-            collective_id=0, has_side_effects=True, vmem_limit_bytes=VMEM_BYTES
-        ),
-        name="forward_mixer",
-    )(*arrays)
-
-
-def mixer_backward_kernel(
-    pre,
-    states,
-    aux,
-    blocks,
-    conv_out,
-    logits,
-    hidden,
-    grad_branch,
-    grad_pre,
-    grad_blocks,
-    grad_states,
-    grad_aux,
-    decays,
-    carries,
-    padded,
-):
-    taps = taps_of(aux)
-    soft, slope = aux[4:5, :], aux[5:6, :]
+    for item in returns:
+        item.start()
+    two_sum.finish()
+    mixed_gather.finish()
+
+    out_sum = CubeSum(
+        place,
+        out_blocks,
+        (cube_three.at[0], cube_three.at[1, 0], cube_three.at[1, 1, 0]),
+        semaphores,
+    )
+    out_sum.start()
 
     @pl.loop(0, PARTS)
     def _(row):
         rows = row_block(row)
+        branch = cols_product(mixed_all[whole_block(place, row)], whole_matrix(rows_all))
         gated, bend = gelu_parts(pre[rows, WIDTH:])
-        branch = grad_branch[rows, :]
         grad_pre[rows, WIDTH:] = (branch * take(hidden, rows) * bend).astype(low_type)
         put(carries, rows, branch * gated)
-        put(decays, rows, jnp.exp(-8.0 * jax.nn.sigmoid(logits[rows, 0:WIDTH]) * soft))
-
-    def advance(step, state):
+
+    @pl.loop(0, 4)
+    def _(step):
+        cut = pl.ds(pl.multiple_of(step * 512, 512), 512)
+        rows_all[:, :, :, cut] = (
+            rows_product(mixed[...], mixed_all[:, :, :, :, cut].reshape(SPAN, 512))
+            .astype(low_type)
+            .reshape(2, 2, LANES, 512)
+        )
+
+    normed_again = cube_one
+    load_normed = pltpu.make_async_copy(normed_kept, normed_again, semaphores.take(1).at[0])
+    load_normed.start()
+
+    def advance_back(step, state):
         factors, carried = state
         across = pl.ds(TOK - 1 - step, PARTS, stride=TOK)
         carried = [
@@ -1210,37 +1263,33 @@
         return ([decays[piece, across, :] for piece in range(WIDTH // 128)], carried)
 
     zeros = [jnp.zeros((PARTS, 128), full_type)] * (WIDTH // 128)
-    lax.fori_loop(0, TOK, advance, (zeros, zeros), unroll=8)
+    lax.fori_loop(0, TOK, advance_back, (zeros, zeros), unroll=8)
+    out_sum.step(0)
     grad_aux[...] = jnp.zeros_like(grad_aux)
     grad_blocks[...] = jnp.zeros_like(grad_blocks)
 
     @pl.loop(0, PARTS)
     def _(row):
         rows = row_block(row)
-        padded[0:8, :] = jnp.broadcast_to(states[row, 0:1, :], (8, WIDTH))
+        padded[0:8, :] = jnp.broadcast_to(states_all[row, 0:1, :], (8, WIDTH))
         padded[8 : 8 + TOK, :] = take(hidden, rows)
-        recur = jax.nn.sigmoid(logits[rows, 0:WIDTH])
-        gate = jax.nn.sigmoid(logits[rows, WIDTH:])
+        low = conv[rows, :]
+        recur, gate = gate_logits(low)
         log_decay = -8.0 * recur * soft
         decay = take(decays, rows)
         scale = jnp.sqrt(-small_expm1(2.0 * log_decay))
-        low = conv_out[rows, :]
-        conv = low.astype(full_type)
+        conv_full = low.astype(full_type)
         carried = take(carries, rows)
         total = (
             carried * decay * padded[7 : 7 + TOK, :]
-            - carried * gate * conv * (decay * decay) / scale
+            - carried * gate * conv_full * (decay * decay) / scale
         )
         grad_aux[4:5, :] += jnp.sum(total * 8.0 * recur * slope, axis=0, keepdims=True)
         to_recur = (total * (-8.0 * soft) * recur * (1.0 - recur)).astype(low_type)
-        to_input = (carried * scale * conv * gate * (1.0 - gate)).astype(low_type)
+        to_input = (carried * scale * conv_full * gate * (1.0 - gate)).astype(low_type)
         both = jnp.concatenate([to_recur, to_input], axis=1)
-        grad_blocks[...] += lax.dot_general(
-            low, both, contract_rows, preferred_element_type=full_type
-        )
-        back = carried * scale * gate + lax.dot_general(
-            both, blocks[...], contract_cols, preferred_element_type=full_type
-        )
+        grad_blocks[...] += rows_product(low, both)
+        back = carried * scale * gate + cols_product(both, whole_matrix(gates_all))
         first = decay[0:1, :] * carried[0:1, :]
         padded[0:8, :] = jnp.zeros((8, WIDTH), full_type)
         padded[8 : 8 + TOK, :] = back
@@ -1251,24 +1300,178 @@
         grad_pre[rows, 0:WIDTH] = spread[8:, :].astype(low_type)
         grad_states[row] = spread[0:8, :]
         grad_states[row, 0:1, :] = first
-        padded[0:8, :] = states[row]
+        padded[0:8, :] = states_all[row]
         padded[8 : 8 + TOK, :] = pre[rows, 0:WIDTH]
         for tap in range(4):
             grad_aux[tap : tap + 1, :] += jnp.sum(
                 back * padded[8 - tap : 8 - tap + TOK, :], axis=0, keepdims=True
             )
 
-
-def in_vmem(kernel, name, arrays, shapes, scratch):
-    vmem = pl.BlockSpec(memory_space=pltpu.VMEM)
+    states_return = move(Peers(by_part), grad_states, states_back)
+    states_return.start()
+    blocks_low[...] = grad_blocks[...].astype(low_type).reshape(2, 2, LANES, 2 * WIDTH)
+    out_sum.step(1)
+
+    @pl.loop(0, PARTS)
+    def _(row):
+        terms = grad_pre[row_block(row), :]
+        for piece in range(COLUMNS):
+            cut = pl.ds(piece * (width // 4), width // 4)
+            blocks[whole_block(place, row) + (slice(None), cut)] = cols_product(
+                terms, whole_matrix(columns_all.at[piece])
+            ).astype(low_type)
+
+    one_sum = CubeSum(place, blocks, landings, semaphores)
+    one_sum.start()
+    out_sum.step(2, summed)
+
+    @pl.loop(0, TOK // 32)
+    def _(step):
+        rows = pl.ds(pl.multiple_of(step * 32, 32), 32)
+        cube_three[1, 1, 1, rows, :] = (after[rows, :] + summed[rows, :]).astype(low_type)
+
+    local.start(cube_three.at[1, 1, 1], output)
+    one_sum.step(0)
+    load_normed.wait()
+
+    @pl.loop(0, 8)
+    def _(step):
+        cut = pl.ds(pl.multiple_of(step * 256, 256), 256)
+        columns_all[step // 2, step % 2] = (
+            rows_product(normed_again[:, :, :, :, cut].reshape(SPAN, 256), grad_pre[...])
+            .astype(low_type)
+            .reshape(4, 64, 2 * WIDTH)
+        )
+
+    pl.semaphore_wait(free.at[1], 1)
+    mixer_swaps = [
+        move(Swap(), columns_all, active),
+        move(Swap(), rows_all, down_landing.at[:, pl.ds(0, LANES)]),
+        move(Swap(), blocks_low, blocks_landing),
+    ]
+    for item in mixer_swaps:
+        item.start()
+    one_sum.step(1)
+    mixer_swaps[0].finish()
+    add_swapped(columns_all, active, place.core)
+    columns_return = move(Owners(), columns_all, columns_back)
+    columns_return.start()
+    mixer_swaps[1].finish()
+    add_swapped(rows_all, down_landing, place.core)
+    rows_return = move(RowOwners(), rows_all, rows_back)
+    rows_return.start()
+    mixer_swaps[2].finish()
+    add_swapped(blocks_low, blocks_landing, place.core)
+    blocks_return = move(RowOwners(), blocks_low, blocks_back)
+    blocks_return.start()
+    one_sum.step(2, summed)
+    load_tokens = pltpu.make_async_copy(
+        tokens, cube_three.at[1, 0, 0], semaphores.take(1).at[0]
+    )
+    out_sum.finish()
+    load_tokens.start()
+    load_tokens.wait()
+
+    @pl.loop(0, TOK // 32)
+    def _(step):
+        rows = pl.ds(pl.multiple_of(step * 32, 32), 32)
+        values = cube_three[1, 0, 0, rows, :].astype(full_type)
+        back, by_gain = norm_back(values, gains[0:1, :], summed[rows, :])
+        cube_three[1, 0, 1, rows, :] = (grad[rows, :] + back).astype(low_type)
+        grad_gains[0:1, :] += jnp.sum(by_gain, axis=0, keepdims=True)
+
+    local.start(cube_three.at[1, 0, 1], grad_tokens)
+    small_terms[...] = jnp.zeros_like(small_terms)
+    for column, core, z in itertools.product(range(COLUMNS), range(2), range(4)):
+        tile = (column * 8 + core * 4 + z) // 2
+        small_terms[column, core, z, 0:2, 0:128] = grad_gains[:, tile * 128 : (tile + 1) * 128]
+    for z in range(4):
+        small_terms[place.part // 2, place.part % 2, z, 2:7, :] = grad_aux[0:5, :]
+    small_swap = move(Swap(), small_terms, small_landing)
+    small_swap.start()
+    small_swap.finish()
+    add_swapped(small_terms, small_landing, place.core)
+    small_return = move(Owners(), small_terms, small_back)
+    small_return.start()
+    one_sum.finish()
+    for item in [states_return, small_return, columns_return, rows_return, blocks_return] + returns:
+        item.finish()
+    for copy in local.copies[1:]:
+        copy.wait()
+
+
+def block_call(arrays, rows, width, units):
+    hbm = pl.BlockSpec(memory_space=pl.ANY)
+    lanes = (WIDTH // 128, SPAN, 128)
+    cube = (2, 2, 2, TOK, width)
+    spread = (COLUMNS, 2, 4, rows)
+    hidden_units = 4 * units
+    outputs = [
+        ((TOK, width), low_type),
+        ((TOK, width), low_type),
+        ((PARTS, 8, WIDTH), full_type),
+        ((2, PARTS, 8, WIDTH), full_type),
+        ((2, PARTS, rows, 2 * WIDTH), low_type),
+        ((2, PARTS, rows, hidden_units), low_type),
+        ((2, PARTS, rows, hidden_units), low_type),
+        ((2, LANES, 2 * WIDTH), low_type),
+        ((2, LANES, width), low_type),
+        ((2, units, width), low_type),
+        (cube, low_type),
+    ]
+    scratch = [
+        (cube, low_type),
+        (cube, low_type),
+        (cube, low_type),
+        (cube, low_type),
+        ((2, 2, TOK, width), low_type),
+        ((2, TOK, width), low_type),
+        ((TOK, width), low_type),
+        ((COLUMNS, 2, 4, 16, WIDTH), low_type),
+        ((PARTS, 8, WIDTH), full_type),
+        (spread + (2 * WIDTH,), low_type),
+        ((2, 2, LANES, 2 * WIDTH), low_type),
+        ((2, 2, LANES, width), low_type),
+        (spread + (hidden_units,), low_type),
+        (spread + (hidden_units,), low_type),
+        ((2, 2, units, width), low_type),
+        ((SPAN, 2 * WIDTH), full_type),
+        ((SPAN, WIDTH), low_type),
+        (lanes, full_type),
+        ((SPAN, WIDTH), low_type),
+        (lanes, full_type),
+        (lanes, full_type),
+        ((TOK + 16, WIDTH), full_type),
+        ((TOK, width), full_type),
+        ((TOK, width), full_type),
+        ((TOK, width), full_type),
+        ((8, WIDTH), full_type),
+        ((2, width), full_type),
+        ((2, width), full_type),
+        ((8, WIDTH), full_type),
+        ((4, 4, 64, hidden_units), low_type),
+        ((4, 4, 64, hidden_units), low_type),
+        ((4, 4, 64, hidden_units), low_type),
+        ((2, units, width), low_type),
+        ((SPAN, 2 * WIDTH), low_type),
+        ((WIDTH, 2 * WIDTH), full_type),
+        ((2, 2, LANES, 2 * WIDTH), low_type),
+        ((2, LANES, 2 * WIDTH), low_type),
+        ((PARTS, 8, WIDTH), full_type),
+        ((COLUMNS, 2, 4, 8, WIDTH), full_type),
+        ((COLUMNS, 4, 8, WIDTH), full_type),
+    ]
     return pl.pallas_call(
-        kernel,
-        out_shape=[jax.ShapeDtypeStruct(shape, kind) for shape, kind in shapes],
-        in_specs=[vmem] * len(arrays),
-        out_specs=[vmem] * len(shapes),
-        scratch_shapes=[pltpu.VMEM(shape, kind) for shape, kind in scratch],
-        compiler_params=pltpu.CompilerParams(vmem_limit_bytes=VMEM_BYTES),
-        name=name,
+        block_kernel,
+        out_shape=[jax.ShapeDtypeStruct(shape, kind) for shape, kind in outputs],
+        in_specs=[hbm] * len(arrays),
+        out_specs=[hbm] * len(outputs),
+        scratch_shapes=[pltpu.VMEM(shape, kind) for shape, kind in scratch]
+        + [pltpu.SemaphoreType.DMA((320,)), pltpu.SemaphoreType.REGULAR((2,))],
+        compiler_params=pltpu.CompilerParams(
+            collective_id=0, has_side_effects=True, vmem_limit_bytes=VMEM_BYTES
+        ),
+        name="hawk_block",
     )(*arrays)
 
 
@@ -1285,26 +1488,6 @@
 
 def pad_rows(array, rows):
     return jnp.pad(array, ((0, rows - array.shape[0]), (0, 0)))
-
-
-def from_dense(dense):
-    pair = 2 * LANES
-    return jnp.concatenate(
-        [
-            jnp.concatenate(
-                [
-                    dense[
-                        block * pair : (block + 1) * pair,
-                        kind * WIDTH + block * pair : kind * WIDTH + (block + 1) * pair,
-                    ]
-                    for kind in range(2)
-                ],
-                axis=1,
-            )
-            for block in range(2)
-        ],
-        axis=0,
-    )
 
 
 def halves(
@@ -1329,8 +1512,6 @@
     width = tokens.shape[2]
     rows = width // 32
     units = mlp_down.shape[0]
-    core = lax.axis_index("wide") % 2
-    part = lax.axis_index("wide") // 2 * 2 + lax.axis_index("narrow") % 2
     keep = (1 - fresh_rows).astype(full_type)[0]
 
     columns = jnp.concatenate(
@@ -1360,25 +1541,18 @@
     )
     states = to_lanes(state_rows * keep).reshape(8, PARTS, WIDTH).transpose(1, 0, 2)
     (
-        normed_all,
-        states_all,
-        columns,
-        gates,
-        out_rows,
-        mlp_gate,
-        mlp_up,
-        down,
-        cot_all,
-        pre,
-        conv_out,
-        logits,
-        hidden,
-        mixed,
-        after_mixer,
-        normed_two_all,
-        aux,
-        gain_rows,
-    ) = forward_mixer(
+        output,
+        grad_tokens,
+        grad_states,
+        small_back,
+        columns_back,
+        gate_back,
+        up_back,
+        blocks_back,
+        rows_back,
+        down_back,
+        _,
+    ) = block_call(
         (
             tokens[0],
             small,
@@ -1395,136 +1569,41 @@
         width,
         units,
     )
-    gain_one, gain_two = gain_rows[0], gain_rows[1]
-    values = tokens[0].astype(full_type)
-    cot_all = cot_all.reshape(SPAN, width)
-    columns = columns.reshape(width, 2 * WIDTH)
-    blocks = gates.reshape(WIDTH, 2 * WIDTH)
-    out_rows = out_rows.reshape(WIDTH, width)
-    mlp_gate = mlp_gate.reshape(width, units * 4)
-    mlp_up = mlp_up.reshape(width, units * 4)
-    down = down.reshape(units * 4, width)
-
-    normed_two_all = normed_two_all.reshape(SPAN, width)
-    gate_part = plain_product(normed_two_all, mlp_gate)
-    up_part = plain_product(normed_two_all, mlp_up)
-    activated = mlp_apply(gate_part, up_part).astype(low_type)
-    out_partial = plain_product(activated, down).astype(low_type).reshape(PARTS, TOK, width)
-    grad_activated = cols_product(cot_all, down)
-    grad_down = rows_product(activated, cot_all).astype(low_type)
-    unused, mlp_pull = jax.vjp(mlp_apply, gate_part, up_part)
-    grad_gate_part, grad_up_part = mlp_pull(grad_activated)
-    grad_gate_part = grad_gate_part.astype(low_type)
-    grad_up_part = grad_up_part.astype(low_type)
-    grad_two = cols_product(grad_gate_part, mlp_gate) + cols_product(grad_up_part, mlp_up)
-    grad_two = grad_two.astype(low_type).reshape(PARTS, TOK, width)
-    grad_mlp_gate = rows_product(normed_two_all, grad_gate_part).astype(low_type)
-    grad_mlp_up = rows_product(normed_two_all, grad_up_part).astype(low_type)
-    grad_two, out_arrived = exchange(
-        "sum_two",
-        4,
-        [
-            (Peers(by_part), grad_two, (PARTS, TOK, width)),
-            (Peers(by_part), out_partial, (PARTS, TOK, width)),
-        ],
-    )
-    output = (after_mixer + jnp.sum(out_arrived.astype(full_type), axis=0)).astype(low_type)
-    grad_two = jnp.sum(grad_two.astype(full_type), axis=0)
-    unused, norm_pull = jax.vjp(norm_scale, after_mixer, gain_two)
-    grad_values, grad_gain_two = norm_pull(grad_two)
-    grad_after = cotangent[0].astype(full_type) + grad_values
-
-    grad_mixed = grad_after.astype(low_type)
-    (mixed_all,) = exchange("gather_mixed", 5, [(Peers(whole), grad_mixed, (PARTS, TOK, width))])
-    mixed_all = mixed_all.reshape(SPAN, width)
-    grad_branch = cols_product(mixed_all, out_rows)
-    grad_out = rows_product(mixed, mixed_all).astype(low_type)
-    grad_pre, grad_blocks, grad_states, grad_aux = in_vmem(
-        mixer_backward_kernel,
-        "mixer_backward",
-        (pre, states_all, aux, blocks, conv_out, logits, hidden, grad_branch),
-        [
-            ((SPAN, 2 * WIDTH), low_type),
-            ((WIDTH, 2 * WIDTH), full_type),
-            ((PARTS, 8, WIDTH), full_type),
-            ((8, WIDTH), full_type),
-        ],
-        [
-            ((WIDTH // 128, SPAN, 128), full_type),
-            ((WIDTH // 128, SPAN, 128), full_type),
-            ((TOK + 16, WIDTH), full_type),
-        ],
-    )
-    grad_one = cols_product(grad_pre, columns).astype(low_type).reshape(PARTS, TOK, width)
-    grad_columns = rows_product(normed_all, grad_pre).astype(low_type)
-    grad_one, grad_states = exchange(
-        "sum_one",
-        6,
-        [
-            (Peers(by_part), grad_one, (PARTS, TOK, width)),
-            (Peers(by_part), grad_states, (PARTS, 8, WIDTH)),
-        ],
-    )
-    grad_one = jnp.sum(grad_one.astype(full_type), axis=0)
-    unused, norm_pull = jax.vjp(norm_scale, values, gain_one)
-    grad_values, grad_gain_one = norm_pull(grad_one)
-    grad_tokens = (grad_after + grad_values).astype(low_type)
     grad_states = grad_states.transpose(1, 0, 2).reshape(8, PARTS * WIDTH)
     grad_states = from_lanes(grad_states) * keep
-
-    gains = jnp.stack([grad_gain_one.reshape(32, rows), grad_gain_two.reshape(32, rows)], axis=1)
-    gains = jnp.pad(gains, ((0, 0), (0, 6), (0, 128 - rows)))
-    own_aux = grad_aux.reshape(8, 4, LANES).transpose(1, 0, 2)[:, 0:5]
-    own_aux = jnp.pad(own_aux, ((0, 0), (2, 1), (0, 128 - LANES)))
-    own_aux = lax.dynamic_update_slice(jnp.zeros_like(gains), own_aux, (4 * part, 0, 0))
-    small_terms = (gains + own_aux).reshape(COLUMNS, 2, 4, 8, 128)
-    wide_terms = [
-        array.reshape(COLUMNS, 2, 4, rows, -1) for array in (grad_columns, grad_mlp_gate, grad_mlp_up)
+    small_sum = jnp.sum(small_back, axis=(0, 1))
+    gain_sums = lax.dynamic_slice(small_sum, (0, z % 2 * rows), (2, rows))
+    tap_sums = lax.dynamic_slice(small_sum, (2, z * LANES), (5, CHUNK))
+    column_sum, gate_sum, up_sum, block_sum, out_sum, down_sum = (
+        jnp.sum(term.astype(full_type), axis=0)
+        for term in (columns_back, gate_back, up_back, blocks_back, rows_back, down_back)
+    )
+    column_sum = column_sum.transpose(1, 0, 2)
+    pair = 2 * LANES
+    gate_sums = [
+        from_lanes(
+            jnp.where(
+                first,
+                block_sum[:CHUNK, start : start + pair],
+                block_sum[:CHUNK, start + pair : start + 2 * pair],
+            )
+        )
+        for start in (0, WIDTH)
     ]
-    row_terms = [
-        from_dense(grad_blocks).astype(low_type).reshape(2, 2, LANES, WIDTH),
-        grad_out.reshape(2, 2, LANES, width),
-        grad_down.reshape(2, 2, units, width),
-    ]
-    terms = [small_terms] + wide_terms + row_terms
-    swapped = exchange(
-        "swap_cores",
-        7,
-        [(Swap(), term, term.shape[:1] + term.shape[2:]) for term in terms],
-    )
-    terms = [
-        (
-            lax.dynamic_index_in_dim(term, core, 1, keepdims=False).astype(full_type)
-            + other.astype(full_type)
-        ).astype(term.dtype)
-        for term, other in zip(terms, swapped)
-    ]
-    arrived = exchange(
-        "return_weights",
-        8,
-        [(Owners(), term, (2, PARTS) + term.shape[2:]) for term in terms[:4]]
-        + [(RowOwners(), term, term.shape) for term in terms[4:]],
-    )
-    small_sum = jnp.sum(arrived[0], axis=(0, 1))
-    column_sum, gate_sum, up_sum, block_sum, out_sum, down_sum = (
-        jnp.sum(term.astype(full_type), axis=0) for term in arrived[1:]
-    )
-    column_sum = column_sum.transpose(1, 0, 2)
-    block_sum = block_sum[:CHUNK]
     return (
         output[None],
         grad_tokens[None],
         grad_states[None, 5:8],
         grad_states[0:1],
-        small_sum[0, :rows],
+        gain_sums[0],
         from_lanes(column_sum[:, :, :WIDTH]).reshape(rows, -1),
         from_lanes(column_sum[:, :, WIDTH:]).reshape(rows, -1),
-        small_sum[2:6, :CHUNK],
-        small_sum[6, :CHUNK],
-        from_lanes(block_sum[:, : 2 * LANES]),
-        from_lanes(block_sum[:, 2 * LANES :]),
+        tap_sums[0:4],
+        tap_sums[4],
+        gate_sums[0],
+        gate_sums[1],
         out_sum[:CHUNK],
-        small_sum[1, :rows],
+        gain_sums[1],
         gate_sum.transpose(1, 0, 2).reshape(rows, -1),
         up_sum.transpose(1, 0, 2).reshape(rows, -1),
         down_sum,

time: 825 us -> 562 us (0.68)
  Pallas kernels: 681 us -> 520 us
  matrix products: 67.7 us -> 0 us
  other arithmetic: 40.4 us -> 11.1 us
    pallas_call x7 -> x1, Pallas kernels: 681 us -> 520 us  [block_call(): pl.pallas_call(block_kernel, out_shape=[jax.ShapeDtypeStruct(shape, kind)...]
    dot_general x13 -> x0, matrix products: 67.7 us -> none  [the longest x5 27.9 us: cols_product(): lax.dot_general(left_side, right_side, contract_cols, preferred_element_t...]
    convert_element_type x7 -> x0, other arithmetic: 12.3 us -> none  [the longest x6 11.2 us: halves(): terms = [(lax.dynamic_index_in_dim(term, core, 1, keepdims=False).astype(...]
    reduce_sum x8 -> x1, other arithmetic: 12.3 us -> 1.02 us  [halves(): small_sum = jnp.sum(small_back, axis=(0, 1))]
where the time goes in v2:
time: 562 us; the launch traced here: 559 us
  Pallas kernels  520 us (93%)
  local copies, waits for them, and re-layouts  26.3 us (5%)
  other arithmetic  11.1 us (2%)
    pallas_call x1, Pallas kernels, block_call(): pl.pallas_call(block_kernel, out_shape=[jax.ShapeDtypeStruct(shape, kind)...  520 us

profile of v2, /device:TPU:0, one launch (start us, length us, event | category | flops | bytes accessed | tf_op | source)
XLA Modules:
  0.0 558.7 jit_solution(9927625627235429917)
XLA Ops:
  1.4 0.7 pad_maximum_fusion.1
  2.2 0.7 fusion.9
  2.9 0.7 reduce
  3.7 0.2 dynamic_update_slice.6
  3.9 0.3 dynamic_update_slice.7.small
  4.2 0.9 reduce.1
  5.2 0.9 reshape.99
  6.1 0.9 reshape.100
  7.2 0.7 copy.64
  7.8 0.2 broadcast_select_fusion.2
  8.4 0.8 fusion.6.gates
  9.1 0.8 pad.39.out_rows
  9.9 1.3 reshape.97
  11.3 0.4 reshape_reshape.19
  11.7 1.3 reshape.98
  13.1 0.4 reshape_reshape.20
  13.5 0.1 copy_bitcast_fusion
  13.6 0.9 pad_maximum_fusion.columns
  14.5 519.6 %hawk_block.1 = (bf16[128,2048]{1,0:T(8,128)(2,1)}, bf16[128,2048]{1,0:T(8,128)(2,1)}, f32[8,8,384]{2,1,0:T(8,128)}, f32[2,8,8,384]{3,2,1,0:T(8,128)}, bf16[2,8,...) custom-call(bf16[128,2048]{1,0:T(8,128)(2,1)} %bitcast.46, ...), custom_call_target="tpu_custom_call" | custom-call | tf_op jit(solution)/shard_map/hawk_block/pallas_call | solution.py:1464
  534.1 1.0 reduce_sum.63
  535.3 0.5 slice_bitcast_fusion
  535.8 0.5 slice_bitcast_fusion.1
  536.4 0.6 slice.67
  536.9 0.9 copy.53
  538.0 0.7 broadcast_in_dim.28
  538.7 0.7 slice.61
  539.4 1.0 convert_reduce_fusion.5
  540.7 0.8 reshape.106
  541.6 0.8 reshape.104
  542.3 0.1 convert_reduce_fusion.4
  542.5 0.9 slice.90
  543.4 0.3 convert_reduce_fusion.3
  543.6 0.2 fusion.10
  543.8 0.6 reshape.102
  544.4 0.3 copy.55
  544.7 2.0 reshape_reshape.23
  546.7 0.6 reshape.101
  547.3 0.3 copy.54
  547.6 2.0 reshape_reshape.22
  549.6 1.9 convert_reduce_fusion.2
  551.4 1.3 copy.59
  552.7 0.7 copy-done.1
  553.4 0.3 convert_reduce_fusion.1
  553.7 1.3 copy.60
  555.0 0.7 copy-done
  555.7 1.4 convert_reduce_fusion
  557.1 0.8 copy.70
  557.9 0.8 copy.71
  (41 shorter events, 1.7 us)
Async XLA Ops:
  0.6 8.5 %copy-start.8 = (bf16[88,2048]{1,0:T(8,128)(2,1)S(1)}, bf16[88,2048]{1,0:T(8,128)(2,1)}, u32[]{:S(2)}) copy-start(bf16[88,2048]{1,0:T(8,128)(2,1)} %param.28) | copy-start | bytes 1081348
  0.7 9.3 %copy-start.6 = (bf16[64,2816]{1,0:T(8,128)(2,1)S(1)}, bf16[64,2816]{1,0:T(8,128)(2,1)}, u32[]{:S(2)}) copy-start(bf16[64,2816]{1,0:T(8,128)(2,1)} %param.22) | copy-start | bytes 1081348
  4.2 7.0 %copy-start.9 = (bf16[16,384]{1,0:T(8,128)(2,1)}, bf16[16,384]{1,0:T(8,128)(2,1)S(1)}, u32[]{:S(2)}) copy-start(bf16[16,384]{1,0:T(8,128)(2,1)S(1)} %dynamic_update_slice.7.small) | copy-start | bytes 36868
  9.9 1.8 copy-start.7
  534.1 8.2 %copy-start.3 = (bf16[2,96,2048]{2,1,0:T(8,128)(2,1)S(1)}, bf16[2,96,2048]{2,1,0:T(8,128)(2,1)}, u32[]{:S(2)}) copy-start(bf16[2,96,2048]{2,1,0:T(8,128)(2,1)} %get-tuple-element.32) | copy-start | bytes 2359300
  541.6 1.8 copy-start.2
  551.4 2.0 copy-start.1
  553.7 2.0 copy-start
  555.7 1.5 copy-start.5
  555.7 2.2 copy-start.4

commit v3 on v2

--- a/solution.py
+++ b/solution.py
@@ -418,7 +418,7 @@
 WIDTH = 4 * LANES
 SPAN = PARTS * TOK
 MESH = pl.DeviceIdType.MESH
-VMEM_BYTES = 63 * 1024 * 1024
+VMEM_BYTES = 63 * 1024 * 1024 + 896 * 1024
 low_type = jnp.bfloat16
 full_type = jnp.float32
 
@@ -480,14 +480,55 @@
     pltpu.make_async_copy(view, view, semaphore).wait()
 
 
+SHIFTS = tuple(
+    near + (half,) for near in itertools.product(range(2), repeat=3) for half in (1, 0)
+)
+
+
+def row_pieces(place, source, slot_of, sems, copies, block_of=None):
+    rows_all = source.shape[-2]
+    step = rows_all // 3
+    device = lambda half: (place.column * 2 + place.low, half * 2 + place.core)
+
+    def piece(rows, half):
+        block = source.at[rows] if block_of is None else block_of(half, rows)
+        copy = remote(block, slot_of(half, rows), sems.at[0], sems.at[1], device(half))
+        own = (place.low == place.core) & (place.half == half)
+
+        @pl.when(own)
+        def _():
+            pltpu.make_async_copy(block, slot_of(half, rows), sems.at[1]).start()
+
+        @pl.when(jnp.logical_not(own))
+        def _():
+            copy.start()
+
+        copies.append((own, copy))
+
+    return [
+        functools.partial(piece, pl.ds(third * step, step), half)
+        for third in range(3)
+        for half in range(2)
+    ]
+
+
+def wait_pieces(copies):
+    for own, copy in copies:
+
+        @pl.when(jnp.logical_not(own))
+        def _():
+            copy.wait_send()
+
+
 class Spread:
     def __init__(self, pick):
         self.pick = pick
 
-    def start(self, place, source, target, sems):
+    def pieces(self, place, source, target, sems):
         self.copies = []
         slot = target.at[place.column, place.core, place.z]
-        for shift in itertools.product(range(2), repeat=4):
+
+        def piece(shift):
             column, low, half = place.shifted(*shift)
             block = self.pick(source, column * 2 + low)
             if any(shift):
@@ -499,6 +540,8 @@
             else:
                 pltpu.make_async_copy(block, slot, sems.at[1]).start()
 
+        return [functools.partial(piece, shift) for shift in SHIFTS]
+
     def relay(self, place, source, target, sems):
         mine = target.at[:, place.core]
         await_bytes(mine, sems.at[1])
@@ -512,28 +555,10 @@
 
 
 class RowSpread:
-    def start(self, place, source, target, sems):
+    def pieces(self, place, source, target, sems):
         self.copies = []
         slot = target.at[place.half, place.low]
-        for half in range(2):
-            copy = remote(
-                source,
-                slot,
-                sems.at[0],
-                sems.at[1],
-                (place.column * 2 + place.low, half * 2 + place.core),
-            )
-            own = (place.low == place.core) & (place.half == half)
-
-            @pl.when(own)
-            def _():
-                pltpu.make_async_copy(source, slot, sems.at[1]).start()
-
-            @pl.when(jnp.logical_not(own))
-            def _():
-                copy.start()
-
-            self.copies.append((own, copy))
+        return row_pieces(place, source, lambda half, rows: slot.at[rows], sems, self.copies)
 
     def relay(self, place, source, target, sems):
         mine = target.at[:, place.core]
@@ -543,11 +568,7 @@
 
     def finish(self, place, source, target, sems):
         self.passed.wait()
-        for own, copy in self.copies:
-
-            @pl.when(jnp.logical_not(own))
-            def _():
-                copy.wait_send()
+        wait_pieces(self.copies)
 
 
 class Peers:
@@ -593,10 +614,16 @@
 
 
 class Owners:
-    def start(self, place, source, target, sems):
+    def pieces(self, place, source, target, sems):
         self.copies = []
-        slot = target.at[place.half, place.part]
-        for shift in itertools.product(range(2), repeat=4):
+        if len(target.shape) == 3:
+            width = source.shape[-1]
+            cut = pl.ds(pl.multiple_of(place.part * width, 128), width)
+            slot = target.at[place.half, :, cut]
+        else:
+            slot = target.at[place.half, place.part]
+
+        def piece(shift):
             column, low, half = place.shifted(*shift)
             z = half * 2 + low
             block = source.at[column, place.core, z]
@@ -609,8 +636,7 @@
             else:
                 pltpu.make_async_copy(block, slot, sems.at[1]).start()
 
-    def relay(self, place, source, target, sems):
-        pass
+        return [functools.partial(piece, shift) for shift in SHIFTS]
 
     def finish(self, place, source, target, sems):
         await_bytes(target, sems.at[1])
@@ -619,40 +645,25 @@
 
 
 class RowOwners:
-    def start(self, place, source, target, sems):
+    def pieces(self, place, source, target, sems):
         self.copies = []
         slot = target.at[place.half]
-        for half in range(2):
-            block = source.at[half, place.core]
-            copy = remote(
-                block,
-                slot,
-                sems.at[0],
-                sems.at[1],
-                (place.column * 2 + place.low, half * 2 + place.core),
-            )
-            own = (place.low == place.core) & (place.half == half)
-
-            @pl.when(own)
-            def _():
-                pltpu.make_async_copy(block, slot, sems.at[1]).start()
-
-            @pl.when(jnp.logical_not(own))
-            def _():
-                copy.start()
-
-            self.copies.append((own, copy))
-
-    def relay(self, place, source, target, sems):
-        pass
+        return row_pieces(
+            place,
+            source,
+            lambda half, rows: slot.at[rows],
+            sems,
+            self.copies,
+            lambda half, rows: source.at[half, place.core, rows],
+        )
 
     def finish(self, place, source, target, sems):
         await_bytes(target, sems.at[1])
-        for own, copy in self.copies:
-
-            @pl.when(jnp.logical_not(own))
-            def _():
-                copy.wait_send()
+        wait_pieces(self.copies)
+
+
+PACE = (6, 0, 0, 3, 1, 1)
+PART = TOK // 2
 
 
 class Semaphores:
@@ -665,73 +676,76 @@
         return taken
 
 
-ORDERS = ((2, 0, 1), (2, 1, 0), (0, 2, 1), (1, 2, 0))
-ROUTES = len(ORDERS)
-
-
-def cuts(width):
-    part = width // ROUTES
-    return [pl.ds(route * part, part) for route in range(ROUTES)]
+LIGHT = ((2, 0, 1), (2, 1, 0), (0, 2, 1), (1, 2, 0))
+EVEN = ((0, 1, 2), (1, 2, 0), (2, 0, 1))
+
+
+def cuts(width, count):
+    ends = [-(-(width // 128) * step // count) * 128 for step in range(count + 1)]
+    return [pl.ds(start, end - start) for start, end in zip(ends, ends[1:])]
 
 
 class CubeGather:
-    def __init__(self, place, buffer, semaphores):
+    def __init__(self, place, buffer, semaphores, rows, orders=LIGHT):
         self.place, self.buffer, self.copies = place, buffer, []
-        self.sems = semaphores.take(6 * ROUTES)
+        self.rows, self.orders = rows, orders
+        self.cuts = cuts(buffer.shape[4], len(orders))
+        self.sems = semaphores.take(6 * len(orders))
 
     def step(self, number):
-        rows = pl.ds(0, self.buffer.shape[3])
-        for order, cut in enumerate(cuts(self.buffer.shape[4])):
-            axes = ORDERS[order]
+        routes = len(self.orders)
+        for route, (axes, cut) in enumerate(zip(self.orders, self.cuts)):
             if number > 0:
-                self.copies[ROUTES * (number - 1) + order].wait_recv()
-            region = self.buffer.at[self.place.cube(axes[number:]) + (rows, cut)]
-            index = ROUTES * number + order
+                self.copies[routes * (number - 1) + route].wait_recv()
+            region = self.buffer.at[self.place.cube(axes[number:]) + (self.rows, cut)]
+            index = routes * number + route
             copy = remote(
                 region,
                 region,
                 self.sems.at[index],
-                self.sems.at[3 * ROUTES + index],
+                self.sems.at[3 * routes + index],
                 self.place.neighbour(axes[number]),
             )
             copy.start()
             self.copies.append(copy)
 
     def finish(self):
-        for copy in self.copies[2 * ROUTES :]:
+        for copy in self.copies[2 * len(self.orders) :]:
             copy.wait_recv()
         for copy in self.copies:
             copy.wait_send()
 
 
 class CubeSum:
-    def __init__(self, place, blocks, landings, semaphores):
+    def __init__(self, place, blocks, landings, semaphores, start, count, orders=LIGHT):
         self.place, self.blocks, self.landings, self.copies = place, blocks, landings, []
-        self.sems = semaphores.take(6 * ROUTES)
-
-    def send(self, number, order, cut):
-        axes = ORDERS[order][::-1]
-        index = ROUTES * number + order
-        rows = pl.ds(0, TOK)
+        self.first, self.count = start, count
+        self.orders = [axes[::-1] for axes in orders]
+        self.cuts = cuts(blocks.shape[4], len(orders))
+        self.sems = semaphores.take(6 * len(orders))
+
+    def send(self, number, route):
+        axes, cut, routes = self.orders[route], self.cuts[route], len(self.orders)
+        index = routes * number + route
+        rows = pl.ds(self.first, self.count)
         landing = self.landings[number]
         copy = remote(
             self.blocks.at[self.place.cube(axes[:number], axes[number]) + (rows, cut)],
             landing.at[(slice(None),) * (2 - number) + (rows, cut)],
             self.sems.at[index],
-            self.sems.at[3 * ROUTES + index],
+            self.sems.at[3 * routes + index],
             self.place.neighbour(axes[number]),
         )
         copy.start()
         self.copies.append(copy)
 
     def start(self):
-        for order, cut in enumerate(cuts(self.blocks.shape[4])):
-            self.send(0, order, cut)
+        for route in range(len(self.orders)):
+            self.send(0, route)
 
     def step(self, number, result=None):
-        for order, cut in enumerate(cuts(self.blocks.shape[4])):
-            axes = ORDERS[order][::-1]
-            self.copies[ROUTES * number + order].wait_recv()
+        for route, (axes, cut) in enumerate(zip(self.orders, self.cuts)):
+            self.copies[len(self.orders) * number + route].wait_recv()
             landing = self.landings[number]
             for picks in itertools.product(range(2), repeat=2 - number):
                 chosen = iter(picks)
@@ -740,9 +754,9 @@
                     for axis in range(3)
                 )
 
-                @pl.loop(0, TOK // 32)
+                @pl.loop(0, self.count // 32)
                 def _(block):
-                    rows = pl.ds(pl.multiple_of(block * 32, 32), 32)
+                    rows = pl.ds(pl.multiple_of(self.first + block * 32, 32), 32)
                     total = self.blocks[index + (rows, cut)].astype(full_type) + landing[
                         picks + (rows, cut)
                     ].astype(full_type)
@@ -752,7 +766,7 @@
                         result[rows, cut] = total
 
             if number < 2:
-                self.send(number + 1, order, cut)
+                self.send(number + 1, route)
 
     def finish(self):
         for copy in self.copies:
@@ -763,14 +777,40 @@
     def __init__(self, place, plan, source, target, semaphores):
         self.plan, self.arguments = plan, (place, source, target, semaphores.take(4))
 
+    def pieces(self):
+        return self.plan.pieces(*self.arguments)
+
     def start(self):
-        self.plan.start(*self.arguments)
+        if hasattr(self.plan, "start"):
+            self.plan.start(*self.arguments)
+        else:
+            for piece in self.pieces():
+                piece()
 
     def relay(self):
         self.plan.relay(*self.arguments)
 
     def finish(self):
         self.plan.finish(*self.arguments)
+
+
+class Pump:
+    def __init__(self, wide, tall):
+        wide = [item.pieces() for item in wide]
+        tall = [item.pieces() for item in tall]
+        self.units = []
+        for step in range(8):
+            self.units.append([piece for each in wide for piece in each[2 * step : 2 * step + 2]])
+            if step % 3 == 1:
+                third = step // 3
+                self.units.append(
+                    [piece for each in tall for piece in each[2 * third : 2 * third + 2]]
+                )
+
+    def start(self, count):
+        for _ in range(min(count, len(self.units))):
+            for piece in self.units.pop(0):
+                piece()
 
 
 class Local:
@@ -911,6 +951,7 @@
     rows_back,
     down_back,
     normed_kept,
+    cot_kept,
     cube_one,
     cube_two,
     cube_three,
@@ -974,8 +1015,14 @@
     load.start()
     greet_all(place)
     load.wait()
-    tokens_gather = CubeGather(place, tokens_all, semaphores)
+    every = pl.ds(0, TOK)
+    parts = (pl.ds(0, PART), pl.ds(PART, PART))
+    tokens_gather = CubeGather(place, tokens_all, semaphores, every, EVEN)
     tokens_gather.step(0)
+    load_own_cot = pltpu.make_async_copy(
+        cotangent, cot_kept.at[place.own], semaphores.take(1).at[0]
+    )
+    load_own_cot.start()
     small_move = move(Spread(whole), small, small_all)
     small_move.start()
     states_move = move(Peers(by_part), states, states_all)
@@ -994,8 +1041,8 @@
         move(Spread(by_columns), mlp_up, up_all),
         move(RowSpread(), mlp_down, down_all),
     ]
-    for item in late:
-        item.start()
+    late_pump = Pump(late[:2], late[2:])
+    late_pump.start(PACE[0])
     small_move.finish()
     for tap in range(5):
         aux[tap : tap + 1, :] = placed_sum(small_all, place, tap)
@@ -1006,6 +1053,8 @@
     gains[0:1, :] = placed_gain(small_all, 5)
     gains[1:2, :] = placed_gain(small_all, 6)
     tokens_gather.finish()
+    cot_gather = CubeGather(place, cot_kept, semaphores, every)
+    load_own_cot.wait()
 
     @pl.loop(0, SPAN // 32)
     def _(step):
@@ -1020,6 +1069,7 @@
     gates_move.relay()
     rows_move.relay()
     columns_move.finish()
+    late_pump.start(PACE[1])
 
     @pl.loop(0, 4)
     def _(step):
@@ -1030,6 +1080,7 @@
             preferred_element_type=full_type,
         )
 
+    late_pump.start(PACE[2])
     gates_move.finish()
     states_move.finish()
     taps = taps_of(aux)
@@ -1065,168 +1116,227 @@
             hidden[piece, across, :] = now
         return carried
 
+    late_pump.start(PACE[3])
     initial = states_all[:, 0, :]
     initial = [initial[:, piece * 128 : (piece + 1) * 128] for piece in range(WIDTH // 128)]
     lax.fori_loop(0, TOK, advance, initial, unroll=8)
     rows_move.finish()
 
-    @pl.loop(0, PARTS)
-    def _(row):
-        rows = row_block(row)
-        gated, _ = gelu_parts(pre[rows, WIDTH:])
-        low = (take(hidden, rows) * gated).astype(low_type)
-        mixed[rows, :] = low
-        blocks[whole_block(place, row)] = jnp.dot(
-            low, whole_matrix(rows_all), preferred_element_type=full_type
-        ).astype(low_type)
+    def project_out(part):
+        @pl.loop(0, PARTS)
+        def _(row):
+            rows = pl.ds(pl.multiple_of(row * TOK + part * PART, PART), PART)
+            gated, _ = gelu_parts(pre[rows, WIDTH:])
+            low = (take(hidden, rows) * gated).astype(low_type)
+            mixed[rows, :] = low
+            blocks[whole_block(place, row) + (parts[part],)] = jnp.dot(
+                low, whole_matrix(rows_all), preferred_element_type=full_type
+            ).astype(low_type)
+
+    def norm_two(part):
+        @pl.loop(0, PART // 32)
+        def _(step):
+            rows = pl.ds(pl.multiple_of(part * PART + step * 32, 32), 32)
+            total = after[rows, :] + tokens_all[place.own + (rows,)].astype(full_type)
+            after[rows, :] = total
+            two_all[place.own + (rows,)] = scaled_norm(total, gains[1:2, :]).astype(low_type)
 
     landings = (landing_one, landing_two, landing_three)
-    mixer_sum = CubeSum(place, blocks, landings, semaphores)
-    mixer_sum.start()
-    mixer_sum.step(0)
-    mixer_sum.step(1)
-    mixer_sum.step(2, after)
-
-    @pl.loop(0, TOK // 32)
-    def _(step):
-        rows = pl.ds(pl.multiple_of(step * 32, 32), 32)
-        total = after[rows, :] + tokens_all[place.own + (rows,)].astype(full_type)
-        after[rows, :] = total
-        two_all[place.own + (rows,)] = scaled_norm(total, gains[1:2, :]).astype(low_type)
-
-    two_gather = CubeGather(place, two_all, semaphores)
-    two_gather.step(0)
+
+    def cube_sum(array, part):
+        return CubeSum(place, array, landings, semaphores, part * PART, PART)
+
+    mixer_sums = [cube_sum(blocks, part) for part in range(2)]
+    two_gathers = [CubeGather(place, two_all, semaphores, rows) for rows in parts]
+    for part in range(2):
+        project_out(part)
+        mixer_sums[part].start()
+        late_pump.start(PACE[4 + part])
+    cot_gather.step(0)
+    for part in range(2):
+        mixer_sums[part].step(0)
+    cot_gather.step(1)
+    for part in range(2):
+        mixer_sums[part].step(1)
+    for part in range(2):
+        mixer_sums[part].step(2, after)
+        norm_two(part)
+        two_gathers[part].step(0)
+    late_pump.start(20)
+    cot_gather.step(2)
+    for part in range(2):
+        two_gathers[part].step(1)
+    for part in range(2):
+        two_gathers[part].step(2)
+    cot_gather.finish()
     cot_all = cube_one
-    load_cot = pltpu.make_async_copy(
-        cotangent, cot_all.at[place.own], semaphores.take(1).at[0]
-    )
+    load_cot = pltpu.make_async_copy(cot_kept, cot_all, semaphores.take(1).at[0])
     load_cot.start()
-    cot_gather = CubeGather(place, cot_all, semaphores)
-    load_cot.wait()
-    cot_gather.step(0)
-    two_gather.step(1)
-    cot_gather.step(1)
-    two_gather.step(2)
-    cot_gather.step(2)
-    two_gather.finish()
-    mixer_sum.finish()
     for item in late:
         item.relay()
-    cot_gather.finish()
+    for part in range(2):
+        mixer_sums[part].finish()
     keep_normed.wait()
+    load_cot.wait()
     for item in late:
         item.finish()
 
     out_blocks = cube_two
 
-    @pl.loop(0, 4)
-    def _(step):
-        at = (step // 2, step % 2)
-        normed_two = two_all[at].reshape(256, width)
-        cot = cot_all[at].reshape(256, width)
-        gate_part = jnp.dot(normed_two, whole_matrix(gate_all), preferred_element_type=full_type)
-        up_part = jnp.dot(normed_two, whole_matrix(up_all), preferred_element_type=full_type)
-        gated, bend = gelu_parts(gate_part)
-        low = (gated * up_part).astype(low_type)
-        active[step] = low.reshape(4, 64, hidden_units)
-        grad_active = cols_product(cot, whole_matrix(down_all))
-        to_gate = (grad_active * up_part * bend).astype(low_type)
-        to_up = (grad_active * gated).astype(low_type)
-        grad_gate[step] = to_gate.reshape(4, 64, hidden_units)
-        grad_up[step] = to_up.reshape(4, 64, hidden_units)
+    def mlp(part, y):
+        rows = parts[part]
+        at = (y, slice(None), slice(None), rows)
+        index = y * 2 + part
+        normed_two = two_all[at].reshape(4 * PART, width)
+        cot = cot_all[at].reshape(4 * PART, width)
+        for piece in range(2):
+            cut = pl.ds(piece * (hidden_units // 2), hidden_units // 2)
+            gate_part, up_part = (
+                jnp.dot(
+                    normed_two,
+                    array[:, :, :, :, cut].reshape(width, hidden_units // 2),
+                    preferred_element_type=full_type,
+                )
+                for array in (gate_all, up_all)
+            )
+            gated, bend = gelu_parts(gate_part)
+            matrix = down_all[piece].reshape(hidden_units // 2, width)
+            grad_active = cols_product(cot, matrix)
+            for array, values in (
+                (active, gated * up_part),
+                (grad_gate, grad_active * up_part * bend),
+                (grad_up, grad_active * gated),
+            ):
+                array[index, :, :, cut] = values.astype(low_type).reshape(
+                    4, PART, hidden_units // 2
+                )
+        low, to_gate, to_up = (whole_matrix(array.at[index]) for array in (active, grad_gate, grad_up))
         for piece in range(4):
             cut = pl.ds(piece * (width // 4), width // 4)
-            part = down_all[:, :, :, cut].reshape(hidden_units, width // 4)
-            out_blocks[at + (slice(None), slice(None), cut)] = (
-                jnp.dot(low, part, preferred_element_type=full_type)
+            matrix = down_all[:, :, :, cut].reshape(hidden_units, width // 4)
+            out_blocks[at + (cut,)] = (
+                jnp.dot(low, matrix, preferred_element_type=full_type)
                 .astype(low_type)
-                .reshape(2, TOK, width // 4)
+                .reshape(2, 2, PART, width // 4)
             )
             back = cols_product(to_gate, whole_matrix(gate_all.at[piece])) + cols_product(
                 to_up, whole_matrix(up_all.at[piece])
             )
-            blocks[at + (slice(None), slice(None), cut)] = back.astype(low_type).reshape(
-                2, TOK, width // 4
-            )
-
-    two_sum = CubeSum(place, blocks, landings, semaphores)
-    two_sum.start()
-
-    @pl.loop(0, 8)
-    def _(step):
-        cut = pl.ds(pl.multiple_of(step * 256, 256), 256)
-        side = two_all[:, :, :, :, cut].reshape(SPAN, 256)
-        for terms, sums in ((grad_gate, gate_all), (grad_up, up_all)):
+            blocks[at + (cut,)] = back.astype(low_type).reshape(2, 2, PART, width // 4)
+
+    def by_tokens(array, cut):
+        return jnp.concatenate(
+            [
+                array[y, :, :, rows, cut].reshape(4 * PART, cut.size)
+                for y in range(2)
+                for rows in parts
+            ],
+            axis=0,
+        )
+
+    def grad_rows(terms, sums):
+        @pl.loop(0, 8)
+        def _(step):
+            side = by_tokens(two_all, pl.ds(pl.multiple_of(step * 256, 256), 256))
             sums[step // 2, step % 2] = (
                 rows_product(side, whole_matrix(terms))
                 .astype(low_type)
                 .reshape(4, 64, hidden_units)
             )
 
-    two_sum.step(0)
+    def norm_two_back(part):
+        @pl.loop(0, PART // 32)
+        def _(step):
+            rows = pl.ds(pl.multiple_of(part * PART + step * 32, 32), 32)
+            back, by_gain = norm_back(after[rows, :], gains[1:2, :], grad[rows, :])
+            total = cot_all[place.own + (rows,)].astype(full_type) + back
+            grad[rows, :] = total
+            cot_all[place.own + (rows,)] = total.astype(low_type)
+            grad_gains[1:2, :] += jnp.sum(by_gain, axis=0, keepdims=True)
+
+    mixed_all = cube_one
+    two_sums = [cube_sum(blocks, part) for part in range(2)]
+    mixed_gathers = [CubeGather(place, cube_one, semaphores, rows) for rows in parts]
+    two_gathers[0].finish()
+
+    @pl.loop(0, 2)
+    def _(y):
+        mlp(0, y)
+
+    two_sums[0].start()
+    two_gathers[1].finish()
+    mlp(1, 0)
+    two_sums[0].step(0)
+    mlp(1, 1)
+    two_sums[1].start()
 
     @pl.loop(0, 4)
     def _(step):
         cut = pl.ds(pl.multiple_of(step * 512, 512), 512)
-        down_all[:, :, :, cut] = (
-            rows_product(whole_matrix(active), cot_all[:, :, :, :, cut].reshape(SPAN, 512))
-            .astype(low_type)
-            .reshape(2, 2, hidden_units // 4, 512)
+        side = by_tokens(cot_all, cut)
+        for piece in range(2):
+            half = pl.ds(piece * (hidden_units // 2), hidden_units // 2)
+            down_all[piece, :, :, cut] = (
+                rows_product(active[:, :, :, half].reshape(SPAN, hidden_units // 2), side)
+                .astype(low_type)
+                .reshape(2, hidden_units // 4, 512)
+            )
+
+    def tell_sibling(number):
+        pl.semaphore_signal(
+            free.at[number], inc=1, device_id=place.sibling(), device_id_type=MESH
         )
 
-    pl.semaphore_signal(
-        free.at[0], inc=1, device_id=place.sibling(), device_id_type=MESH
-    )
-    two_sum.step(1)
+    gate_swap = move(Swap(), gate_all, active)
+    up_swap = move(Swap(), up_all, grad_gate)
+    down_swap = move(Swap(), down_all, down_landing)
+    gate_return = move(Owners(), gate_all, gate_back)
+    up_return = move(Owners(), up_all, up_back)
+    down_return = move(RowOwners(), down_all, down_back)
+    returns = [gate_return, up_return, down_return]
+    tell_sibling(0)
+    down_swap.start()
+    two_sums[0].step(1)
+    two_sums[1].step(0)
+    grad_rows(grad_gate, gate_all)
+    tell_sibling(1)
     pl.semaphore_wait(free.at[0], 1)
-    mlp_swaps = [
-        move(Swap(), gate_all, active),
-        move(Swap(), up_all, grad_gate),
-        move(Swap(), down_all, down_landing),
-    ]
-    for item in mlp_swaps:
-        item.start()
-    two_sum.step(2, grad)
+    gate_swap.start()
     grad_gains[...] = jnp.zeros_like(grad_gains)
-
-    @pl.loop(0, TOK // 32)
-    def _(step):
-        rows = pl.ds(pl.multiple_of(step * 32, 32), 32)
-        back, by_gain = norm_back(after[rows, :], gains[1:2, :], grad[rows, :])
-        total = cot_all[place.own + (rows,)].astype(full_type) + back
-        grad[rows, :] = total
-        cot_all[place.own + (rows,)] = total.astype(low_type)
-        grad_gains[1:2, :] += jnp.sum(by_gain, axis=0, keepdims=True)
-
-    mixed_all = cube_one
-    mixed_gather = CubeGather(place, mixed_all, semaphores)
-    mixed_gather.step(0)
-    mlp_swaps[0].finish()
+    two_sums[0].step(2, grad)
+    norm_two_back(0)
+    mixed_gathers[0].step(0)
+    two_sums[1].step(1)
+    down_swap.finish()
+    add_swapped(down_all, down_landing, place.core)
+    grad_rows(grad_up, up_all)
+    pl.semaphore_wait(free.at[1], 1)
+    up_swap.start()
+    two_sums[1].step(2, grad)
+    norm_two_back(1)
+    mixed_gathers[1].step(0)
+    gate_swap.finish()
     add_swapped(gate_all, active, place.core)
-    mixed_gather.step(1)
-    mlp_swaps[1].finish()
+    mixed_gathers[0].step(1)
+    mixed_gathers[1].step(1)
+    up_swap.finish()
     add_swapped(up_all, grad_gate, place.core)
-    mixed_gather.step(2)
-    mlp_swaps[2].finish()
-    add_swapped(down_all, down_landing, place.core)
-    pl.semaphore_signal(
-        free.at[1], inc=1, device_id=place.sibling(), device_id_type=MESH
-    )
-    returns = [
-        move(Owners(), gate_all, gate_back),
-        move(Owners(), up_all, up_back),
-        move(RowOwners(), down_all, down_back),
-    ]
+    tell_sibling(2)
+    mixed_gathers[0].step(2)
+    mixed_gathers[1].step(2)
     for item in returns:
         item.start()
-    two_sum.finish()
-    mixed_gather.finish()
+    for part in range(2):
+        two_sums[part].finish()
+        mixed_gathers[part].finish()
 
     out_sum = CubeSum(
         place,
         out_blocks,
         (cube_three.at[0], cube_three.at[1, 0], cube_three.at[1, 1, 0]),
         semaphores,
+        0,
+        TOK,
     )
     out_sum.start()
 
@@ -1247,6 +1357,9 @@
             .reshape(2, 2, LANES, 512)
         )
 
+    pl.semaphore_wait(free.at[2], 1)
+    rows_swap = move(Swap(), rows_all, down_landing.at[:, pl.ds(0, LANES)])
+    rows_swap.start()
     normed_again = cube_one
     load_normed = pltpu.make_async_copy(normed_kept, normed_again, semaphores.take(1).at[0])
     load_normed.start()
@@ -1264,7 +1377,10 @@
 
     zeros = [jnp.zeros((PARTS, 128), full_type)] * (WIDTH // 128)
     lax.fori_loop(0, TOK, advance_back, (zeros, zeros), unroll=8)
-    out_sum.step(0)
+    rows_swap.finish()
+    add_swapped(rows_all, down_landing, place.core)
+    rows_return = move(RowOwners(), rows_all, rows_back)
+    rows_return.start()
     grad_aux[...] = jnp.zeros_like(grad_aux)
     grad_blocks[...] = jnp.zeros_like(grad_blocks)
 
@@ -1310,19 +1426,25 @@
     states_return = move(Peers(by_part), grad_states, states_back)
     states_return.start()
     blocks_low[...] = grad_blocks[...].astype(low_type).reshape(2, 2, LANES, 2 * WIDTH)
+    out_sum.step(0)
+
+    one_sums = [cube_sum(blocks, part) for part in range(2)]
+    for part in range(2):
+
+        @pl.loop(0, PARTS)
+        def _(row):
+            terms = grad_pre[pl.ds(pl.multiple_of(row * TOK + part * PART, PART), PART), :]
+            for piece in range(COLUMNS):
+                cut = pl.ds(piece * (width // 4), width // 4)
+                blocks[whole_block(place, row) + (parts[part], cut)] = cols_product(
+                    terms, whole_matrix(columns_all.at[piece])
+                ).astype(low_type)
+
+        one_sums[part].start()
+
     out_sum.step(1)
-
-    @pl.loop(0, PARTS)
-    def _(row):
-        terms = grad_pre[row_block(row), :]
-        for piece in range(COLUMNS):
-            cut = pl.ds(piece * (width // 4), width // 4)
-            blocks[whole_block(place, row) + (slice(None), cut)] = cols_product(
-                terms, whole_matrix(columns_all.at[piece])
-            ).astype(low_type)
-
-    one_sum = CubeSum(place, blocks, landings, semaphores)
-    one_sum.start()
+    one_sums[0].step(0)
+    one_sums[1].step(0)
     out_sum.step(2, summed)
 
     @pl.loop(0, TOK // 32)
@@ -1331,7 +1453,6 @@
         cube_three[1, 1, 1, rows, :] = (after[rows, :] + summed[rows, :]).astype(low_type)
 
     local.start(cube_three.at[1, 1, 1], output)
-    one_sum.step(0)
     load_normed.wait()
 
     @pl.loop(0, 8)
@@ -1343,28 +1464,24 @@
             .reshape(4, 64, 2 * WIDTH)
         )
 
-    pl.semaphore_wait(free.at[1], 1)
     mixer_swaps = [
         move(Swap(), columns_all, active),
-        move(Swap(), rows_all, down_landing.at[:, pl.ds(0, LANES)]),
         move(Swap(), blocks_low, blocks_landing),
     ]
     for item in mixer_swaps:
         item.start()
-    one_sum.step(1)
+    one_sums[0].step(1)
+    one_sums[1].step(1)
     mixer_swaps[0].finish()
     add_swapped(columns_all, active, place.core)
     columns_return = move(Owners(), columns_all, columns_back)
     columns_return.start()
     mixer_swaps[1].finish()
-    add_swapped(rows_all, down_landing, place.core)
-    rows_return = move(RowOwners(), rows_all, rows_back)
-    rows_return.start()
-    mixer_swaps[2].finish()
     add_swapped(blocks_low, blocks_landing, place.core)
     blocks_return = move(RowOwners(), blocks_low, blocks_back)
     blocks_return.start()
-    one_sum.step(2, summed)
+    one_sums[0].step(2, summed)
+    one_sums[1].step(2, summed)
     load_tokens = pltpu.make_async_copy(
         tokens, cube_three.at[1, 0, 0], semaphores.take(1).at[0]
     )
@@ -1393,7 +1510,8 @@
     add_swapped(small_terms, small_landing, place.core)
     small_return = move(Owners(), small_terms, small_back)
     small_return.start()
-    one_sum.finish()
+    for part in range(2):
+        one_sums[part].finish()
     for item in [states_return, small_return, columns_return, rows_return, blocks_return] + returns:
         item.finish()
     for copy in local.copies[1:]:
@@ -1412,11 +1530,12 @@
         ((PARTS, 8, WIDTH), full_type),
         ((2, PARTS, 8, WIDTH), full_type),
         ((2, PARTS, rows, 2 * WIDTH), low_type),
-        ((2, PARTS, rows, hidden_units), low_type),
-        ((2, PARTS, rows, hidden_units), low_type),
+        ((2, rows, PARTS * hidden_units), low_type),
+        ((2, rows, PARTS * hidden_units), low_type),
         ((2, LANES, 2 * WIDTH), low_type),
         ((2, LANES, width), low_type),
         ((2, units, width), low_type),
+        (cube, low_type),
         (cube, low_type),
     ]
     scratch = [
@@ -1467,7 +1586,7 @@
         in_specs=[hbm] * len(arrays),
         out_specs=[hbm] * len(outputs),
         scratch_shapes=[pltpu.VMEM(shape, kind) for shape, kind in scratch]
-        + [pltpu.SemaphoreType.DMA((320,)), pltpu.SemaphoreType.REGULAR((2,))],
+        + [pltpu.SemaphoreType.DMA((480,)), pltpu.SemaphoreType.REGULAR((3,))],
         compiler_params=pltpu.CompilerParams(
             collective_id=0, has_side_effects=True, vmem_limit_bytes=VMEM_BYTES
         ),
@@ -1551,6 +1670,7 @@
         blocks_back,
         rows_back,
         down_back,
+        _,
         _,
     ) = block_call(
         (
@@ -1604,8 +1724,8 @@
         gate_sums[1],
         out_sum[:CHUNK],
         gain_sums[1],
-        gate_sum.transpose(1, 0, 2).reshape(rows, -1),
-        up_sum.transpose(1, 0, 2).reshape(rows, -1),
+        gate_sum,
+        up_sum,
         down_sum,
     )
 

time: 562 us -> 526 us (0.936)
  Pallas kernels: 520 us -> 481 us
    pallas_call x1, Pallas kernels: 520 us -> 481 us  [block_call(): pl.pallas_call(block_kernel, out_shape=[jax.ShapeDtypeStruct(shape, kind)...]
where the time goes in v3:
time: 526 us; the launch traced here: 519 us
  Pallas kernels  481 us (91%)
  local copies, waits for them, and re-layouts  22.8 us (4%)
  other arithmetic  13.4 us (3%)
    pallas_call x1, Pallas kernels, block_call(): pl.pallas_call(block_kernel, out_shape=[jax.ShapeDtypeStruct(shape, kind)...  481 us

profile of v3, /device:TPU:0, one launch (start us, length us, event | category | flops | bytes accessed | tf_op | source)
XLA Modules:
  0.0 519.5 jit_solution(11017852051275778053)
XLA Ops:
  1.4 0.7 pad_maximum_fusion.1
  2.2 0.7 fusion.9
  2.9 0.7 reduce
  3.7 0.2 dynamic_update_slice.6
  3.9 0.3 dynamic_update_slice.7.small
  4.2 0.9 reduce.1
  5.2 0.9 reshape.93
  6.1 0.9 reshape.94
  7.2 0.7 copy.53
  7.8 0.2 broadcast_select_fusion.2
  8.4 0.8 fusion.6.gates
  9.1 0.8 pad.39.out_rows
  9.9 1.3 reshape.91
  11.3 0.4 reshape_reshape.19
  11.7 1.3 reshape.92
  13.1 0.4 reshape_reshape.20
  13.5 0.1 copy_bitcast_fusion
  13.6 0.9 pad_maximum_fusion.columns
  14.5 481.1 %hawk_block.1 = (bf16[128,2048]{1,0:T(8,128)(2,1)}, bf16[128,2048]{1,0:T(8,128)(2,1)}, f32[8,8,384]{2,1,0:T(8,128)}, f32[2,8,8,384]{3,2,1,0:T(8,128)}, bf16[2,8,...) custom-call(bf16[128,2048]{1,0:T(8,128)(2,1)} %bitcast.36, ...), custom_call_target="tpu_custom_call" | custom-call | tf_op jit(solution)/shard_map/hawk_block/pallas_call | solution.py:1583
  495.6 1.0 reduce_sum.63
  496.8 0.5 slice_bitcast_fusion
  497.3 0.5 slice_bitcast_fusion.1
  497.9 0.6 slice.67
  498.4 0.9 copy.46
  499.5 0.7 broadcast_in_dim.28
  500.2 0.7 slice.61
  500.9 1.0 convert_reduce_fusion.5
  502.0 0.1 slice_select_fusion
  502.1 0.1 reshape.99
  502.2 0.8 reshape.100
  502.9 0.1 reshape.97
  503.1 0.8 reshape.98
  503.8 0.1 convert_reduce_fusion.4
  504.0 0.9 slice.90
  504.9 0.3 convert_reduce_fusion.3
  505.1 0.2 fusion.10
  505.3 0.6 reshape.96
  505.9 0.3 copy.48
  506.2 2.0 reshape_reshape.23
  508.2 0.6 reshape.95
  508.8 0.3 copy.47
  509.1 2.0 reshape_reshape.22
  511.1 3.1 convert_reduce_fusion.2
  514.1 1.4 convert_reduce_fusion.1
  515.6 0.4 copy-done
  516.0 1.4 convert_reduce_fusion
  517.4 0.8 copy.59
  518.2 0.8 copy.60
  (39 shorter events, 1.3 us)
Async XLA Ops:
  0.6 8.5 %copy-start.8 = (bf16[88,2048]{1,0:T(8,128)(2,1)S(1)}, bf16[88,2048]{1,0:T(8,128)(2,1)}, u32[]{:S(2)}) copy-start(bf16[88,2048]{1,0:T(8,128)(2,1)} %param.28) | copy-start | bytes 1081348
  0.7 9.3 %copy-start.6 = (bf16[64,2816]{1,0:T(8,128)(2,1)S(1)}, bf16[64,2816]{1,0:T(8,128)(2,1)}, u32[]{:S(2)}) copy-start(bf16[64,2816]{1,0:T(8,128)(2,1)} %param.22) | copy-start | bytes 1081348
  4.2 7.0 %copy-start.9 = (bf16[16,384]{1,0:T(8,128)(2,1)}, bf16[16,384]{1,0:T(8,128)(2,1)S(1)}, u32[]{:S(2)}) copy-start(bf16[16,384]{1,0:T(8,128)(2,1)S(1)} %dynamic_update_slice.7.small) | copy-start | bytes 36868
  9.9 1.8 copy-start.7
  495.6 8.2 %copy-start.3 = (bf16[2,96,2048]{2,1,0:T(8,128)(2,1)S(1)}, bf16[2,96,2048]{2,1,0:T(8,128)(2,1)}, u32[]{:S(2)}) copy-start(bf16[2,96,2048]{2,1,0:T(8,128)(2,1)} %get-tuple-element.32) | copy-start | bytes 2359300
  503.1 1.8 copy-start.2
  511.1 3.1 copy-start.1
  514.1 1.8 copy-start
  516.0 1.5 copy-start.5
  516.0 2.2 copy-start.4

commit v4 on v3

--- a/solution.py
+++ b/solution.py
@@ -1594,19 +1594,158 @@
     )(*arrays)
 
 
-def to_lanes(array):
-    chunks = array.reshape(array.shape[:-1] + (-1, CHUNK))
-    pads = [(0, 0)] * (chunks.ndim - 1) + [(0, LANES - CHUNK)]
-    return jnp.pad(chunks, pads).reshape(array.shape[:-1] + (-1,))
-
-
-def from_lanes(array):
-    chunks = array.reshape(array.shape[:-1] + (-1, LANES))
-    return chunks[..., :CHUNK].reshape(array.shape[:-1] + (-1,))
-
-
-def pad_rows(array, rows):
-    return jnp.pad(array, ((0, rows - array.shape[0]), (0, 0)))
+def spread_lanes(values):
+    gap = jnp.zeros((values.shape[0], LANES - CHUNK), values.dtype)
+    pieces = []
+    for start in range(0, values.shape[1], CHUNK):
+        pieces += [values[:, start : start + CHUNK], gap]
+    return jnp.concatenate(pieces, axis=1)
+
+
+def joined_lanes(values):
+    return [values[:, start : start + CHUNK] for start in range(0, values.shape[1], LANES)]
+
+
+def prepare_kernel(
+    fresh,
+    gain_mixer,
+    gain_mlp,
+    conv_kernel,
+    decay_param,
+    proj_input,
+    proj_gate,
+    gate_recur,
+    gate_input,
+    proj_output,
+    conv_state,
+    recur_state,
+    small,
+    states,
+    columns,
+    gates,
+    out_rows,
+):
+    z = lax.axis_index("narrow")
+    keep = (1 - fresh[0]).astype(full_type)
+    for kind, proj in enumerate((proj_input, proj_gate)):
+        for part in range(PARTS):
+            piece = proj[:, part * 4 * CHUNK : (part + 1) * 4 * CHUNK].astype(full_type)
+            columns[part, :, kind * WIDTH : (kind + 1) * WIDTH] = spread_lanes(piece).astype(
+                low_type
+            )
+    pair = 2 * LANES
+    gates[CHUNK:, :] = jnp.zeros((LANES - CHUNK, 2 * WIDTH), low_type)
+    for kind, gate in enumerate((gate_recur, gate_input)):
+        values = spread_lanes(gate[...].astype(full_type))
+        for block in range(2):
+            start = kind * WIDTH + block * pair
+            gates[0:CHUNK, start : start + pair] = jnp.where(
+                z // 2 == block, values, jnp.zeros_like(values)
+            ).astype(low_type)
+    out_rows[0:CHUNK, :] = proj_output[...]
+    out_rows[CHUNK:, :] = jnp.zeros((LANES - CHUNK, out_rows.shape[1]), low_type)
+    taps = jnp.concatenate([conv_kernel[...], decay_param[...]], axis=0).astype(full_type)
+    taps = spread_lanes(taps)
+    taps = jnp.concatenate(
+        [jnp.where(z == place, taps, jnp.zeros_like(taps)) for place in range(4)], axis=1
+    )
+    gains = jnp.concatenate([gain_mixer[...], gain_mlp[...]], axis=0).astype(full_type)
+    gains = [jnp.where(z % 2 == odd, gains, jnp.zeros_like(gains)) for odd in range(2)]
+    gains = jnp.concatenate(gains + [jnp.zeros((2, WIDTH - 128), full_type)], axis=1)
+    rest = jnp.zeros((9, WIDTH), full_type)
+    small[...] = jnp.concatenate([taps, gains, rest], axis=0).astype(low_type)
+    states[...] = jnp.zeros_like(states)
+    for part in range(PARTS):
+        cut = slice(part * 4 * CHUNK, (part + 1) * 4 * CHUNK)
+        states[part, 0:1, :] = spread_lanes(recur_state[:, cut]) * keep
+        states[part, 5:8, :] = spread_lanes(conv_state[0, :, cut]) * keep
+
+
+def finish_kernel(
+    fresh,
+    output,
+    grad_tokens,
+    states_back,
+    small_back,
+    columns_back,
+    gate_back,
+    up_back,
+    blocks_back,
+    rows_back,
+    down_back,
+    output_out,
+    tokens_out,
+    conv_out,
+    recur_out,
+    gain_one_out,
+    input_out,
+    gate_out,
+    taps_out,
+    decay_out,
+    gate_recur_out,
+    gate_input_out,
+    rows_out,
+    gain_two_out,
+    mlp_gate_out,
+    mlp_up_out,
+    down_out,
+):
+    z = lax.axis_index("narrow")
+    keep = (1 - fresh[0]).astype(full_type)
+    output_out[0] = output[...]
+    tokens_out[0] = grad_tokens[...]
+    states = jnp.concatenate(
+        [piece for part in range(PARTS) for piece in joined_lanes(states_back[part])], axis=1
+    )
+    recur_out[...] = states[0:1, :] * keep
+    conv_out[0] = states[5:8, :] * keep
+
+    def both(array, *index):
+        return array[(0,) + index].astype(full_type) + array[(1,) + index].astype(full_type)
+
+    for kind, target in enumerate((input_out, gate_out)):
+        pieces = []
+        for part in range(PARTS):
+            cut = slice(kind * WIDTH, (kind + 1) * WIDTH)
+            pieces += joined_lanes(both(columns_back, part, slice(None), cut))
+        target[...] = jnp.concatenate(pieces, axis=1)
+    pair = 2 * LANES
+    for kind, target in enumerate((gate_recur_out, gate_input_out)):
+        start = kind * WIDTH
+        first = both(blocks_back, slice(0, CHUNK), slice(start, start + pair))
+        second = both(blocks_back, slice(0, CHUNK), slice(start + pair, start + 2 * pair))
+        target[...] = jnp.concatenate(joined_lanes(jnp.where(z < 2, first, second)), axis=1)
+    total = jnp.zeros((8, WIDTH), full_type)
+    for half, part in itertools.product(range(2), range(PARTS)):
+        total = total + small_back[half, part]
+    rows = gain_one_out.shape[1]
+    gains = jnp.where(z % 2 == 0, total[0:2, 0:rows], total[0:2, rows : 2 * rows])
+    gain_one_out[...] = gains[0:1, :]
+    gain_two_out[...] = gains[1:2, :]
+    taps = total[2:7, 0:CHUNK]
+    for place in range(1, 4):
+        taps = jnp.where(z == place, total[2:7, place * LANES : place * LANES + CHUNK], taps)
+    taps_out[...] = taps[0:4, :]
+    decay_out[...] = taps[4:5, :]
+    rows_out[...] = both(rows_back, slice(0, CHUNK))
+    for source, target in ((gate_back, mlp_gate_out), (up_back, mlp_up_out), (down_back, down_out)):
+
+        @pl.loop(0, target.shape[0] // 8)
+        def _(step):
+            part = pl.ds(pl.multiple_of(step * 8, 8), 8)
+            target[part, :] = both(source, part)
+
+
+def plain_call(kernel, name, flags, arrays, outputs):
+    vmem = pl.BlockSpec(memory_space=pltpu.VMEM)
+    return pl.pallas_call(
+        kernel,
+        out_shape=[jax.ShapeDtypeStruct(shape, kind) for shape, kind in outputs],
+        in_specs=[pl.BlockSpec(memory_space=pltpu.SMEM)] + [vmem] * len(arrays),
+        out_specs=[vmem] * len(outputs),
+        compiler_params=pltpu.CompilerParams(vmem_limit_bytes=VMEM_BYTES),
+        name=name,
+    )(flags, *arrays)
 
 
 def halves(
@@ -1631,55 +1770,39 @@
     width = tokens.shape[2]
     rows = width // 32
     units = mlp_down.shape[0]
-    keep = (1 - fresh_rows).astype(full_type)[0]
-
-    columns = jnp.concatenate(
+    small, states, columns, gates, out_rows = plain_call(
+        prepare_kernel,
+        "prepare",
+        fresh_rows,
+        (
+            gain_mixer[None],
+            gain_mlp[None],
+            conv_kernel,
+            decay_param[None],
+            proj_input,
+            proj_gate,
+            gate_recur,
+            gate_input,
+            proj_output,
+            conv_state,
+            recur_state,
+        ),
         [
-            to_lanes(proj).reshape(rows, PARTS, WIDTH).transpose(1, 0, 2)
-            for proj in (proj_input, proj_gate)
+            ((16, WIDTH), low_type),
+            ((PARTS, 8, WIDTH), full_type),
+            ((PARTS, rows, 2 * WIDTH), low_type),
+            ((LANES, 2 * WIDTH), low_type),
+            ((LANES, width), low_type),
         ],
-        axis=2,
-    )
-    zeros = jnp.zeros((CHUNK, 2 * LANES), low_type)
-    first = lax.axis_index("narrow") < 2
-    gates = jnp.concatenate(
-        [
-            jnp.where(chosen, to_lanes(gate), zeros)
-            for gate in (gate_recur, gate_input)
-            for chosen in (first, jnp.logical_not(first))
-        ],
-        axis=1,
-    )
-    z = lax.axis_index("narrow")
-    taps = pad_rows(jnp.concatenate([conv_kernel, decay_param[None]], axis=0), 16)
-    taps = lax.dynamic_update_slice(jnp.zeros((16, WIDTH), low_type), taps, (0, z * LANES))
-    gain_rows = jnp.stack([gain_mixer, gain_mlp])
-    small = lax.dynamic_update_slice(taps, gain_rows, (5, z % 2 * rows))
-    state_rows = jnp.concatenate(
-        [recur_state, jnp.zeros((4, recur_state.shape[1]), full_type), conv_state[0]], axis=0
-    )
-    states = to_lanes(state_rows * keep).reshape(8, PARTS, WIDTH).transpose(1, 0, 2)
-    (
-        output,
-        grad_tokens,
-        grad_states,
-        small_back,
-        columns_back,
-        gate_back,
-        up_back,
-        blocks_back,
-        rows_back,
-        down_back,
-        _,
-        _,
-    ) = block_call(
+    )
+    results = block_call(
         (
             tokens[0],
             small,
             states,
             columns,
-            pad_rows(gates, LANES),
-            pad_rows(proj_output, LANES),
+            gates,
+            out_rows,
             mlp_gate,
             mlp_up,
             mlp_down,
@@ -1689,44 +1812,32 @@
         width,
         units,
     )
-    grad_states = grad_states.transpose(1, 0, 2).reshape(8, PARTS * WIDTH)
-    grad_states = from_lanes(grad_states) * keep
-    small_sum = jnp.sum(small_back, axis=(0, 1))
-    gain_sums = lax.dynamic_slice(small_sum, (0, z % 2 * rows), (2, rows))
-    tap_sums = lax.dynamic_slice(small_sum, (2, z * LANES), (5, CHUNK))
-    column_sum, gate_sum, up_sum, block_sum, out_sum, down_sum = (
-        jnp.sum(term.astype(full_type), axis=0)
-        for term in (columns_back, gate_back, up_back, blocks_back, rows_back, down_back)
-    )
-    column_sum = column_sum.transpose(1, 0, 2)
-    pair = 2 * LANES
-    gate_sums = [
-        from_lanes(
-            jnp.where(
-                first,
-                block_sum[:CHUNK, start : start + pair],
-                block_sum[:CHUNK, start + pair : start + 2 * pair],
-            )
-        )
-        for start in (0, WIDTH)
-    ]
-    return (
-        output[None],
-        grad_tokens[None],
-        grad_states[None, 5:8],
-        grad_states[0:1],
-        gain_sums[0],
-        from_lanes(column_sum[:, :, :WIDTH]).reshape(rows, -1),
-        from_lanes(column_sum[:, :, WIDTH:]).reshape(rows, -1),
-        tap_sums[0:4],
-        tap_sums[4],
-        gate_sums[0],
-        gate_sums[1],
-        out_sum[:CHUNK],
-        gain_sums[1],
-        gate_sum,
-        up_sum,
-        down_sum,
+    results = plain_call(
+        finish_kernel,
+        "finish",
+        fresh_rows,
+        results[:10],
+        [
+            (tokens.shape, low_type),
+            (tokens.shape, low_type),
+            (conv_state.shape, full_type),
+            (recur_state.shape, full_type),
+            ((1, rows), full_type),
+            (proj_input.shape, full_type),
+            (proj_gate.shape, full_type),
+            (conv_kernel.shape, full_type),
+            ((1, CHUNK), full_type),
+            (gate_recur.shape, full_type),
+            (gate_input.shape, full_type),
+            (proj_output.shape, full_type),
+            ((1, rows), full_type),
+            (mlp_gate.shape, full_type),
+            (mlp_up.shape, full_type),
+            (mlp_down.shape, full_type),
+        ],
+    )
+    return tuple(
+        result[0] if place in (4, 8, 12) else result for place, result in enumerate(results)
     )
 
 

time: 526 us -> 497 us (0.945); the launches traced: 519 us -> 496 us
  local copies, waits for them, and re-layouts: 22.8 us -> 2.83 us
  other arithmetic: 13.4 us -> 0 us
  Pallas kernels: 481 us -> 492 us
    pallas_call x0 -> x2, Pallas kernels: none -> 11.8 us  [plain_call(): pl.pallas_call(kernel, out_shape=[jax.ShapeDtypeStruct(shape, kind) for s...]
    reduce_sum x7 -> x0, other arithmetic: 8.38 us -> none  [the longest x6 7.36 us: halves(): jnp.sum(term.astype(full_type), axis=0)]
    reshape x10 -> x0, local copies, waits for them, and re-layouts: 7.22 us -> none  [the longest x4 4.3 us: to_lanes(): chunks = array.reshape(array.shape[:-1] + (-1, CHUNK))]
    another operation x7 -> x0, local copies, waits for them, and re-layouts: 5.5 us -> none  [the longest x1 1.97 us: halves(): from_lanes(column_sum[:, :, :WIDTH]).reshape(rows, -1)]
where the time goes in v4:
time: 497 us; the launch traced here: 496 us
  Pallas kernels  492 us (99%)
    pallas_call x1, Pallas kernels, block_call(): pl.pallas_call(block_kernel, out_shape=[jax.ShapeDtypeStruct(shape, kind)...  480 us
    pallas_call x2, Pallas kernels, plain_call(): pl.pallas_call(kernel, out_shape=[jax.ShapeDtypeStruct(shape, kind) for s...  11.8 us

profile of v4, /device:TPU:0, one launch (start us, length us, event | category | flops | bytes accessed | tf_op | source)
XLA Modules:
  0.0 496.4 jit_solution(14754275491600419211)
XLA Ops:
  1.3 1.4 copy.33.conv_state
  2.7 3.1 prepare.1
  5.8 480.4 %hawk_block.1 = (bf16[128,2048]{1,0:T(8,128)(2,1)}, bf16[128,2048]{1,0:T(8,128)(2,1)}, f32[8,8,384]{2,1,0:T(8,128)}, f32[2,8,8,384]{3,2,1,0:T(8,128)}, bf16[2,8,...) custom-call(bf16[128,2048]{1,0:T(8,128)(2,1)} %bitcast.8, ...), custom_call_target="tpu_custom_call" | custom-call | tf_op jit(solution)/shard_map/hawk_block/pallas_call | solution.py:1583
  486.2 8.7 %finish.1 = (bf16[1,128,2048]{2,1,0:T(8,128)(2,1)}, bf16[1,128,2048]{2,1,0:T(8,128)(2,1)}, f32[1,3,2816]{2,1,0:T(4,128)}, f32[1,2816]{1,0:T(1,128)}, f32[1,64]{1...) custom-call(s32[1]{0:T(128)S(6)} %copy.35.fresh, ...), custom_call_target="tpu_custom_call" | custom-call | tf_op jit(solution)/shard_map/finish/pallas_call | solution.py:1741
  494.9 1.4 copy.34

commit v5 on v4

--- a/solution.py
+++ b/solution.py
@@ -962,6 +962,7 @@
     small_all,
     states_all,
     columns_all,
+    gates_sent,
     gates_all,
     rows_all,
     gate_all,
@@ -1029,7 +1030,7 @@
     states_move.start()
     columns_move = move(Spread(by_part), columns, columns_all)
     columns_move.start()
-    gates_move = move(RowSpread(), gates, gates_all)
+    gates_move = move(RowSpread(), gates, gates_sent)
     gates_move.start()
     rows_move = move(RowSpread(), out_rows, rows_all)
     rows_move.start()
@@ -1083,6 +1084,16 @@
     late_pump.start(PACE[2])
     gates_move.finish()
     states_move.finish()
+    pair = 2 * LANES
+    for block, odd in itertools.product(range(2), range(2)):
+        sent = gates_sent[block, odd].astype(full_type)
+        empty = jnp.zeros((LANES, pair), full_type)
+        pieces = []
+        for kind in range(2):
+            piece = sent[:, kind * pair : (kind + 1) * pair]
+            pieces += [piece, empty] if block == 0 else [empty, piece]
+        gates_all[block, odd] = jnp.concatenate(pieces, axis=1).astype(low_type)
+
     taps = taps_of(aux)
     soft, slope = aux[4:5, :], aux[5:6, :]
 
@@ -1152,12 +1163,12 @@
         project_out(part)
         mixer_sums[part].start()
         late_pump.start(PACE[4 + part])
+    for part in range(2):
+        mixer_sums[part].step(0)
     cot_gather.step(0)
     for part in range(2):
-        mixer_sums[part].step(0)
+        mixer_sums[part].step(1)
     cot_gather.step(1)
-    for part in range(2):
-        mixer_sums[part].step(1)
     for part in range(2):
         mixer_sums[part].step(2, after)
         norm_two(part)
@@ -1425,7 +1436,15 @@
 
     states_return = move(Peers(by_part), grad_states, states_back)
     states_return.start()
-    blocks_low[...] = grad_blocks[...].astype(low_type).reshape(2, 2, LANES, 2 * WIDTH)
+    for block in range(2):
+        rows = slice(block * pair, (block + 1) * pair)
+        kinds = [
+            grad_blocks[rows, kind * WIDTH : (kind + 1) * WIDTH][:, rows] for kind in range(2)
+        ]
+        blocks_low[block] = (
+            jnp.concatenate(kinds, axis=1).astype(low_type).reshape(2, LANES, WIDTH)
+        )
+
     out_sum.step(0)
 
     one_sums = [cube_sum(blocks, part) for part in range(2)]
@@ -1532,7 +1551,7 @@
         ((2, PARTS, rows, 2 * WIDTH), low_type),
         ((2, rows, PARTS * hidden_units), low_type),
         ((2, rows, PARTS * hidden_units), low_type),
-        ((2, LANES, 2 * WIDTH), low_type),
+        ((2, LANES, WIDTH), low_type),
         ((2, LANES, width), low_type),
         ((2, units, width), low_type),
         (cube, low_type),
@@ -1549,6 +1568,7 @@
         ((COLUMNS, 2, 4, 16, WIDTH), low_type),
         ((PARTS, 8, WIDTH), full_type),
         (spread + (2 * WIDTH,), low_type),
+        ((2, 2, LANES, WIDTH), low_type),
         ((2, 2, LANES, 2 * WIDTH), low_type),
         ((2, 2, LANES, width), low_type),
         (spread + (hidden_units,), low_type),
@@ -1574,8 +1594,8 @@
         ((2, units, width), low_type),
         ((SPAN, 2 * WIDTH), low_type),
         ((WIDTH, 2 * WIDTH), full_type),
-        ((2, 2, LANES, 2 * WIDTH), low_type),
-        ((2, LANES, 2 * WIDTH), low_type),
+        ((2, 2, LANES, WIDTH), low_type),
+        ((2, LANES, WIDTH), low_type),
         ((PARTS, 8, WIDTH), full_type),
         ((COLUMNS, 2, 4, 8, WIDTH), full_type),
         ((COLUMNS, 4, 8, WIDTH), full_type),
@@ -1633,15 +1653,10 @@
             columns[part, :, kind * WIDTH : (kind + 1) * WIDTH] = spread_lanes(piece).astype(
                 low_type
             )
-    pair = 2 * LANES
-    gates[CHUNK:, :] = jnp.zeros((LANES - CHUNK, 2 * WIDTH), low_type)
-    for kind, gate in enumerate((gate_recur, gate_input)):
-        values = spread_lanes(gate[...].astype(full_type))
-        for block in range(2):
-            start = kind * WIDTH + block * pair
-            gates[0:CHUNK, start : start + pair] = jnp.where(
-                z // 2 == block, values, jnp.zeros_like(values)
-            ).astype(low_type)
+    gates[CHUNK:, :] = jnp.zeros((LANES - CHUNK, WIDTH), low_type)
+    gates[0:CHUNK, :] = jnp.concatenate(
+        [spread_lanes(gate[...].astype(full_type)) for gate in (gate_recur, gate_input)], axis=1
+    ).astype(low_type)
     out_rows[0:CHUNK, :] = proj_output[...]
     out_rows[CHUNK:, :] = jnp.zeros((LANES - CHUNK, out_rows.shape[1]), low_type)
     taps = jnp.concatenate([conv_kernel[...], decay_param[...]], axis=0).astype(full_type)
@@ -1658,7 +1673,7 @@
     for part in range(PARTS):
         cut = slice(part * 4 * CHUNK, (part + 1) * 4 * CHUNK)
         states[part, 0:1, :] = spread_lanes(recur_state[:, cut]) * keep
-        states[part, 5:8, :] = spread_lanes(conv_state[0, :, cut]) * keep
+        states[part, 5:8, :] = spread_lanes(conv_state[:, 0, cut]) * keep
 
 
 def finish_kernel(
@@ -1692,57 +1707,63 @@
 ):
     z = lax.axis_index("narrow")
     keep = (1 - fresh[0]).astype(full_type)
+    def both(array, *index):
+        return array[(0,) + index].astype(full_type) + array[(1,) + index].astype(full_type)
+
     output_out[0] = output[...]
     tokens_out[0] = grad_tokens[...]
-    states = jnp.concatenate(
-        [piece for part in range(PARTS) for piece in joined_lanes(states_back[part])], axis=1
-    )
-    recur_out[...] = states[0:1, :] * keep
-    conv_out[0] = states[5:8, :] * keep
-
-    def both(array, *index):
-        return array[(0,) + index].astype(full_type) + array[(1,) + index].astype(full_type)
-
-    for kind, target in enumerate((input_out, gate_out)):
-        pieces = []
-        for part in range(PARTS):
-            cut = slice(kind * WIDTH, (kind + 1) * WIDTH)
-            pieces += joined_lanes(both(columns_back, part, slice(None), cut))
-        target[...] = jnp.concatenate(pieces, axis=1)
-    pair = 2 * LANES
-    for kind, target in enumerate((gate_recur_out, gate_input_out)):
-        start = kind * WIDTH
-        first = both(blocks_back, slice(0, CHUNK), slice(start, start + pair))
-        second = both(blocks_back, slice(0, CHUNK), slice(start + pair, start + 2 * pair))
-        target[...] = jnp.concatenate(joined_lanes(jnp.where(z < 2, first, second)), axis=1)
-    total = jnp.zeros((8, WIDTH), full_type)
-    for half, part in itertools.product(range(2), range(PARTS)):
-        total = total + small_back[half, part]
-    rows = gain_one_out.shape[1]
-    gains = jnp.where(z % 2 == 0, total[0:2, 0:rows], total[0:2, rows : 2 * rows])
-    gain_one_out[...] = gains[0:1, :]
-    gain_two_out[...] = gains[1:2, :]
-    taps = total[2:7, 0:CHUNK]
-    for place in range(1, 4):
-        taps = jnp.where(z == place, total[2:7, place * LANES : place * LANES + CHUNK], taps)
-    taps_out[...] = taps[0:4, :]
-    decay_out[...] = taps[4:5, :]
-    rows_out[...] = both(rows_back, slice(0, CHUNK))
     for source, target in ((gate_back, mlp_gate_out), (up_back, mlp_up_out), (down_back, down_out)):
-
-        @pl.loop(0, target.shape[0] // 8)
-        def _(step):
-            part = pl.ds(pl.multiple_of(step * 8, 8), 8)
+        for start in range(0, target.shape[0], 8):
+            part = slice(start, start + 8)
             target[part, :] = both(source, part)
 
-
-def plain_call(kernel, name, flags, arrays, outputs):
-    vmem = pl.BlockSpec(memory_space=pltpu.VMEM)
+    @pl.when(pl.program_id(0) == 0)
+    def _():
+        states = jnp.concatenate(
+            [piece for part in range(PARTS) for piece in joined_lanes(states_back[part])], axis=1
+        )
+        recur_out[...] = states[0:1, :] * keep
+        conv_out[:, 0, :] = states[5:8, :] * keep
+
+        for kind, target in enumerate((input_out, gate_out)):
+            pieces = []
+            for part in range(PARTS):
+                cut = slice(kind * WIDTH, (kind + 1) * WIDTH)
+                pieces += joined_lanes(both(columns_back, part, slice(None), cut))
+            target[...] = jnp.concatenate(pieces, axis=1)
+        pair = 2 * LANES
+        for kind, target in enumerate((gate_recur_out, gate_input_out)):
+            values = both(blocks_back, slice(0, CHUNK))[:, kind * pair : (kind + 1) * pair]
+            target[...] = jnp.concatenate(joined_lanes(values), axis=1)
+        total = jnp.zeros((8, WIDTH), full_type)
+        for half, part in itertools.product(range(2), range(PARTS)):
+            total = total + small_back[half, part]
+        rows = gain_one_out.shape[1]
+        gains = jnp.where(z % 2 == 0, total[0:2, 0:rows], total[0:2, rows : 2 * rows])
+        gain_one_out[...] = gains[0:1, :]
+        gain_two_out[...] = gains[1:2, :]
+        taps = total[2:7, 0:CHUNK]
+        for place in range(1, 4):
+            taps = jnp.where(z == place, total[2:7, place * LANES : place * LANES + CHUNK], taps)
+        taps_out[...] = taps[0:4, :]
+        decay_out[...] = taps[4:5, :]
+        rows_out[...] = both(rows_back, slice(0, CHUNK))
+
+
+def plain_call(kernel, name, flags, arrays, outputs, steps=1, cuts_in={}, cuts_out={}):
+    def spec(shape, cut):
+        block = tuple(size // steps if axis == cut else size for axis, size in enumerate(shape))
+        return pl.BlockSpec(
+            block, lambda step: tuple(step if axis == cut else 0 for axis in range(len(shape)))
+        )
+
     return pl.pallas_call(
         kernel,
+        grid=(steps,),
         out_shape=[jax.ShapeDtypeStruct(shape, kind) for shape, kind in outputs],
-        in_specs=[pl.BlockSpec(memory_space=pltpu.SMEM)] + [vmem] * len(arrays),
-        out_specs=[vmem] * len(outputs),
+        in_specs=[pl.BlockSpec(memory_space=pltpu.SMEM)]
+        + [spec(array.shape, cuts_in.get(place)) for place, array in enumerate(arrays)],
+        out_specs=[spec(shape, cuts_out.get(place)) for place, (shape, kind) in enumerate(outputs)],
         compiler_params=pltpu.CompilerParams(vmem_limit_bytes=VMEM_BYTES),
         name=name,
     )(flags, *arrays)
@@ -1784,14 +1805,14 @@
             gate_recur,
             gate_input,
             proj_output,
-            conv_state,
+            conv_state.transpose(1, 0, 2),
             recur_state,
         ),
         [
             ((16, WIDTH), low_type),
             ((PARTS, 8, WIDTH), full_type),
             ((PARTS, rows, 2 * WIDTH), low_type),
-            ((LANES, 2 * WIDTH), low_type),
+            ((LANES, WIDTH), low_type),
             ((LANES, width), low_type),
         ],
     )
@@ -1820,7 +1841,7 @@
         [
             (tokens.shape, low_type),
             (tokens.shape, low_type),
-            (conv_state.shape, full_type),
+            ((conv_state.shape[1], 1, conv_state.shape[2]), full_type),
             (recur_state.shape, full_type),
             ((1, rows), full_type),
             (proj_input.shape, full_type),
@@ -1835,9 +1856,17 @@
             (mlp_up.shape, full_type),
             (mlp_down.shape, full_type),
         ],
+        4,
+        {0: 0, 1: 0, 5: 1, 6: 1, 9: 1},
+        {0: 1, 1: 1, 13: 0, 14: 0, 15: 0},
     )
     return tuple(
-        result[0] if place in (4, 8, 12) else result for place, result in enumerate(results)
+        result[0]
+        if place in (4, 8, 12)
+        else result.transpose(1, 0, 2)
+        if place == 2
+        else result
+        for place, result in enumerate(results)
     )
 
 

time: 497 us -> 483 us (0.972)
  Pallas kernels: 492 us -> 481 us
    pallas_call x1, Pallas kernels: 480 us -> 470 us  [block_call(): pl.pallas_call(block_kernel, out_shape=[jax.ShapeDtypeStruct(shape, kind)...]
where the time goes in v5:
time: 483 us
  Pallas kernels  481 us (100%)
    pallas_call x1, Pallas kernels, block_call(): pl.pallas_call(block_kernel, out_shape=[jax.ShapeDtypeStruct(shape, kind)...  470 us
    pallas_call x2, Pallas kernels, plain_call(): pl.pallas_call(kernel, grid=(steps,), out_shape=[jax.ShapeDtypeStruct(sha...  11.4 us

profile of v5, /device:TPU:0, one launch (start us, length us, event | category | flops | bytes accessed | tf_op | source)
XLA Modules:
  0.0 482.9 jit_solution(2302737651852316753)
XLA Ops:
  1.3 3.0 prepare.1
  4.3 469.9 %hawk_block.1 = (bf16[128,2048]{1,0:T(8,128)(2,1)}, bf16[128,2048]{1,0:T(8,128)(2,1)}, f32[8,8,384]{2,1,0:T(8,128)}, f32[2,8,8,384]{3,2,1,0:T(8,128)}, bf16[2,8,...) custom-call(bf16[128,2048]{1,0:T(8,128)(2,1)} %bitcast.10, ...), custom_call_target="tpu_custom_call" | custom-call | tf_op jit(solution)/shard_map/hawk_block/pallas_call | solution.py:1603
  474.3 8.4 %finish.1 = (bf16[1,128,2048]{2,1,0:T(8,128)(2,1)}, bf16[1,128,2048]{2,1,0:T(8,128)(2,1)}, f32[3,1,2816]{2,1,0:T(1,128)}, f32[1,2816]{1,0:T(1,128)}, f32[1,64]{1...) custom-call(s32[1]{0:T(128)S(6)} %copy.33.fresh, ...), custom_call_target="tpu_custom_call" | custom-call | tf_op jit(solution)/shard_map/finish/pallas_call | solution.py:1760
